TPU v7x, 512 devices: a whole 4x8x8 slice. The times are simulated.
512 devices in a mesh: blk: 64 (over y, x, z_lo), group: 8 (over z_hi, core).
Axes of the slice: x: 4, y: 8, z: 8 (z_hi: 4, z_lo: 2; z = z_hi * 2 + z_lo), core: 2. Of those that a mesh axis runs over, the one named last changes fastest.
Arguments:
- tokens: bfloat16 [8, 32768, 1024], P('group', 'blk'), may hold values from -6 to 6
- norm_gain: float32 [1024], replicated, may hold values from 0.5 to 2
- proj_weight: bfloat16 [1024, 1024], replicated, may hold values from -0.1875 to 0.1875
- text_feats: bfloat16 [8, 2048, 1024], P('group', 'blk'), may hold values from -6 to 6
- lengths: int32 [8, 64, 32], P('group', 'blk'), may hold values from 1 to 48, 512 in all within a row
- positives: int32 [8, 2048], P('group', 'blk'), may hold values from 0 to 2047, each once within a row
- sample_weight: float32 [8, 2048], P('group', 'blk'), may hold values from 0.5 to 13.5
- log_temp: float32 [], replicated, may hold values from 3.9 to 4.6
- logit_bias: float32 [], replicated, may hold values from -11 to -7
- loss_scale: float32 [], replicated, may hold values from 4194304 to 16777216
Outputs:
- grad_tokens: bfloat16 [8, 32768, 1024], P('group', 'blk')
- grad_texts: float32 [8, 2048, 1024], P('group', 'blk')
- loss_value: float32 [], replicated
- grad_temp: float32 [], replicated
- grad_bias: float32 [], replicated
Inputs may be any that keep to these rules, and one draw needn't show every extreme that they name: The 32 lengths of one device sum to 512, and that device's tokens hold its sketches one after another in order. In each cycle a permutation: sketch i of the cycle is paired with text positives[i] of the cycle.
All inputs are finite; a program needn't handle non-finite values.
Results may differ from a plain program's by a relative error of at most 0.023.
Values may be sent and summed in bfloat16 or wider, within the bound.
No kernel may reach another device: no remote copies, remote signals or barrier semaphores. Data moves between devices by JAX's collectives and lax.ppermute only.
A program may use at most 64 MiB of HBM per device.

v0:
```python
import jax
import jax.numpy as jnp
from jax import lax
from jax.sharding import PartitionSpec as P

EPSILON = 1e-06
GELU_SCALE = 0.7978845608028654


def from_behind(block, axis, distance):
    devices = range(lax.axis_size(axis))
    route = [((i - distance) % len(devices), i) for i in devices]
    return lax.ppermute(block, axis, route)


def gelu_value(values):
    inner_arg = GELU_SCALE * (values + 0.044715 * values * values * values)
    return 0.5 * values * (1.0 + jnp.tanh(inner_arg))


def gelu_slope(values):
    inner_arg = GELU_SCALE * (values + 0.044715 * values * values * values)
    tanh_part = jnp.tanh(inner_arg)
    return 0.5 * (1.0 + tanh_part) + 0.5 * values * (1.0 - tanh_part * tanh_part) * GELU_SCALE * (
        1.0 + 3.0 * 0.044715 * values * values
    )


def add_sums(first_sums, second_sums):
    return (
        first_sums[0] + second_sums[0],
        first_sums[1] + second_sums[1],
        first_sums[2] + second_sums[2],
    )


def pass_onward(payload):
    return from_behind(payload, "blk", 1)


def on_device(
    tokens,
    norm_gain,
    proj_weight,
    text_feats,
    lengths,
    positives,
    sample_weight,
    log_temp,
    logit_bias,
    loss_scale,
):
    inputs = tokens[0].astype(jnp.float32)
    tok_count = inputs.shape[0]
    sketches = text_feats.shape[1]
    cycle_size = lax.axis_size("blk")
    inv_count = 1.0 / (lax.axis_size("group") * cycle_size * sketches)
    cycle_place = lax.axis_index("blk")
    inv_rms = lax.rsqrt(jnp.mean(inputs * inputs, axis=-1, keepdims=True) + EPSILON)
    normal_x = inputs * inv_rms
    normed = (normal_x * norm_gain).astype(jnp.bfloat16)
    preact = jnp.dot(normed, proj_weight, preferred_element_type=jnp.float32)
    activated = gelu_value(preact).astype(jnp.bfloat16)
    sketch_lens = lengths[0, 0]
    seg_ends = jnp.cumsum(sketch_lens)
    local_pos = jnp.arange(tok_count, dtype=jnp.int32)
    seg_local = jnp.sum((local_pos[:, None] >= seg_ends[None, :]).astype(jnp.int32), axis=1)
    membership = (seg_local[None, :] == jnp.arange(sketches, dtype=jnp.int32)[:, None]).astype(
        jnp.bfloat16
    )
    len_col = sketch_lens.astype(jnp.float32)[:, None]
    pooled = jnp.dot(membership, activated, preferred_element_type=jnp.float32) / len_col
    pool_rnorm = lax.rsqrt(jnp.sum(pooled * pooled, axis=-1, keepdims=True) + EPSILON)
    sketch_unit = pooled * pool_rnorm
    sketch_embed = sketch_unit.astype(jnp.bfloat16)
    text_in = text_feats[0].astype(jnp.float32)
    text_rnorm = lax.rsqrt(jnp.sum(text_in * text_in, axis=-1, keepdims=True) + EPSILON)
    text_unit = text_in * text_rnorm
    text_embed = text_unit.astype(jnp.bfloat16)
    temper = jnp.exp(log_temp)
    factor = temper * loss_scale
    paired = positives[0]
    weights_row = sample_weight[0]
    local_cols = jnp.arange(sketches, dtype=jnp.int32)

    def score_tile(text_block, block_owner):
        dot_scores = lax.dot_general(
            sketch_embed, text_block, (((1,), (1,)), ((), ())), preferred_element_type=jnp.float32
        )
        logits = temper * dot_scores + logit_bias
        global_cols = block_owner * sketches + local_cols
        pair_signs = jnp.where(paired[:, None] == global_cols[None, :], 1.0, -1.0).astype(
            jnp.float32
        )
        pair_loss = jax.nn.softplus(-pair_signs * logits)
        coeffs = (
            -weights_row[:, None] * pair_signs * jax.nn.sigmoid(-pair_signs * logits) * inv_count
        )
        scaled_coef = (coeffs * factor).astype(jnp.bfloat16)
        sketch_part = jnp.dot(scaled_coef, text_block, preferred_element_type=jnp.float32)
        text_part = lax.dot_general(
            scaled_coef, sketch_embed, (((0,), (0,)), ((), ())), preferred_element_type=jnp.float32
        )
        tile_sums = (
            jnp.sum(weights_row[:, None] * pair_loss) * inv_count,
            jnp.sum(coeffs * temper * dot_scores),
            jnp.sum(coeffs),
        )
        return (sketch_part, text_part, tile_sums)

    zero_rows = jnp.zeros((sketches, text_embed.shape[1]), jnp.float32)
    zero_sums = (jnp.zeros((), jnp.float32), jnp.zeros((), jnp.float32), jnp.zeros((), jnp.float32))

    def step_one(step_index, cycle_state):
        text_block, partial_value, sketch_grad, sums_now = cycle_state
        block_owner = (cycle_place - step_index) % cycle_size
        sketch_part, text_part, tile_sums = score_tile(text_block, block_owner)
        text_block = from_behind(text_block, "blk", 1)
        partial_value = pass_onward(partial_value + text_part)
        return (text_block, partial_value, sketch_grad + sketch_part, add_sums(sums_now, tile_sums))

    text_block, partial_value, sketch_grad, sums_now = lax.fori_loop(
        0, cycle_size - 1, step_one, (text_embed, zero_rows, zero_rows, zero_sums)
    )
    last_owner = (cycle_place - (cycle_size - 1)) % cycle_size
    sketch_part, text_part, tile_sums = score_tile(text_block, last_owner)
    sketch_grad = sketch_grad + sketch_part
    sums_now = add_sums(sums_now, tile_sums)
    text_grad = pass_onward(partial_value + text_part)
    loss_value, grad_temp, grad_bias = lax.psum(
        (sums_now[0], sums_now[1], sums_now[2]), ("blk", "group")
    )
    along_unit = jnp.sum(sketch_unit * sketch_grad, axis=-1, keepdims=True)
    pool_grad = pool_rnorm * (sketch_grad - sketch_unit * along_unit)
    per_token = jnp.take(pool_grad / len_col, seg_local, axis=0)
    act_grad = (per_token * gelu_slope(preact)).astype(jnp.bfloat16)
    normed_grad = lax.dot_general(
        act_grad, proj_weight, (((1,), (1,)), ((), ())), preferred_element_type=jnp.float32
    )
    gain_part = normed_grad * norm_gain
    token_grad = inv_rms * (
        gain_part - normal_x * jnp.mean(gain_part * normal_x, axis=-1, keepdims=True)
    )
    text_along = jnp.sum(text_unit * text_grad, axis=-1, keepdims=True)
    text_out = text_rnorm * (text_grad - text_unit * text_along)
    return (token_grad.astype(jnp.bfloat16)[None], text_out[None], loss_value, grad_temp, grad_bias)


def solution(mesh):
    placed = (
        P("group", "blk", None),
        P(),
        P(),
        P("group", "blk", None),
        P("group", "blk", None),
        P("group", "blk"),
        P("group", "blk"),
        P(),
        P(),
        P(),
    )
    return jax.shard_map(
        on_device,
        mesh=mesh,
        in_specs=placed,
        out_specs=(P("group", "blk", None), P("group", "blk", None), P(), P(), P()),
        check_vma=False,
    )
```

profile of v0, /device:TPU:1, one launch (start us, length us, event | category | flops | bytes accessed | tf_op | source)
XLA Modules:
  0.0 1071.8 jit_solution(11958137689973304001)
XLA Ops:
  12.3 876.2 %while.26 = (s32[]{:T(128)}, bf16[32,1024]{1,0:T(8,128)(2,1)S(1)}, f32[32,1024]{1,0:T(8,128)S(1)}, f32[32,1024]{1,0:T(8,128)S(1)}, f32[]{:T(128)}, /*index=5*/f3...) while((s32[]{:T(128)}, bf16[32,1024]{1,0:T(8,128)(2,1)S(1)}, ...), condition=%wide.region_9.10_spmd.clone, body=%wide.region_5.9_spmd.clone.sunk | while | flops 6418481 | bytes 1717368 | solution.py:122
  12.3 4.8 collective-permute-start
  23.9 5.8 collective-permute-done.1
  38.9 5.0 collective-permute-done.1
  53.1 4.3 collective-permute-done.1
  66.7 4.3 collective-permute-done.1
  80.2 4.3 collective-permute-done.1
  93.8 4.3 collective-permute-done.1
  107.4 4.2 collective-permute-done.1
  134.4 4.3 collective-permute-done.1
  148.0 5.0 collective-permute-done.1
  162.8 5.0 collective-permute-done.1
  177.1 4.8 collective-permute-done.1
  191.1 4.3 collective-permute-done.1
  204.6 4.6 collective-permute-done.1
  218.5 5.0 collective-permute-done.1
  232.7 5.1 collective-permute-done.1
  247.1 4.8 collective-permute-done.1
  261.1 4.3 collective-permute-done.1
  274.6 4.3 collective-permute-done.1
  288.2 4.3 collective-permute-done.1
  301.7 4.3 collective-permute-done.1
  315.8 3.8 collective-permute-done.1
  329.2 4.0 collective-permute-done.1
  342.4 4.3 collective-permute-done.1
  356.0 5.0 collective-permute-done.1
  370.7 5.0 collective-permute-done.1
  384.9 4.3 collective-permute-done.1
  398.5 4.3 collective-permute-done.1
  412.0 5.0 collective-permute-done.1
  426.3 5.1 collective-permute-done.1
  440.6 5.1 collective-permute-done.1
  454.9 4.7 collective-permute-done.1
  468.9 4.3 collective-permute-done.1
  482.4 4.3 collective-permute-done.1
  495.9 4.3 collective-permute-done.1
  509.5 4.3 collective-permute-done.1
  536.6 4.3 collective-permute-done.1
  550.1 4.3 collective-permute-done.1
  564.1 5.0 collective-permute-done.1
  578.3 5.2 collective-permute-done.1
  592.7 4.3 collective-permute-done.1
  606.3 4.3 collective-permute-done.1
  619.8 5.0 collective-permute-done.1
  634.1 5.2 collective-permute-done.1
  648.5 5.0 collective-permute-done.1
  662.7 4.3 collective-permute-done.1
  676.3 4.3 collective-permute-done.1
  689.8 4.3 collective-permute-done.1
  703.4 4.3 collective-permute-done.1
  717.0 4.2 collective-permute-done.1
  744.0 4.3 collective-permute-done.1
  757.6 5.0 collective-permute-done.1
  772.4 5.0 collective-permute-done.1
  786.6 4.7 collective-permute-done.1
  800.5 4.3 collective-permute-done.1
  814.1 4.7 collective-permute-done.1
  828.0 5.0 collective-permute-done.1
  842.3 5.1 collective-permute-done.1
  856.6 4.8 collective-permute-done.1
  870.6 4.3 collective-permute-done.1
  884.2 4.3 collective-permute-done.1
  895.7 5.8 fusion.10
  905.8 165.1 %all-reduce = (f32[]{:T(128)}, f32[]{:T(128)}, f32[]{:T(128)}) all-reduce(f32[]{:T(128)S(6)} %add.271, f32[]{:T(128)S(6)} %add.272, f32[]{:T(128)S(6)} %add.273), channel_id=1, replica_groups=mesh['blk'=64,'group'=8] {'blk','group'}, use_global_device_ids=true, to_apply=%region_14.15 | all-reduce | flops 3 | bytes 24 | tf_op jit(solution)/shard_map/psum | solution.py:130
  (552 shorter events, 497.9 us)
Async XLA Ops:
  12.3 11.6 %collective-permute-start = (bf16[32,1024]{1,0:T(8,128)(2,1)S(1)}, bf16[32,1024]{1,0:T(8,128)(2,1)S(1)}, u32[]{:S(2)}, u32[]{:S(2)}) collective-permute-start(bf16[32,1024]{1,0:T(8,128)(2,1)S(1)} %copy.26), channel_id=1, source_target_pairs={{504,0},{0,8},{8,16},{16,24},{24,32},{32,40},{40,48},{48,56},{56,6... | collective-permute-start | bytes 196616 | tf_op jit(solution)/shard_map/while/body/eval_jaxpr/ppermute | solution.py:13
  18.9 10.8 %collective-permute-start.1 = (f32[32,1024]{1,0:T(8,128)S(1)}, f32[32,1024]{1,0:T(8,128)S(1)}, u32[]{:S(2)}, u32[]{:S(2)}) collective-permute-start(f32[32,1024]{1,0:T(8,128)S(1)} %convolution_add_fusion.6), channel_id=1, source_target_pairs={{504,0},{0,8},{8,16},{16,24},{24,32},{32,40},{40,48},{48,56},{56,6... | collective-permute-start | bytes 393224 | tf_op jit(solution)/shard_map/while/body/eval_jaxpr/ppermute | solution.py:13
  33.3 10.6 collective-permute-start.1
  47.5 9.9 collective-permute-start.1
  61.1 9.9 collective-permute-start.1
  74.6 9.9 collective-permute-start.1
  88.2 9.9 collective-permute-start.1
  101.7 9.9 collective-permute-start.1
  111.7 10.2 collective-permute-start
  115.3 9.9 collective-permute-start.1
  128.8 9.9 collective-permute-start.1
  142.4 10.6 collective-permute-start.1
  156.6 11.3 %collective-permute-start.1 = (f32[32,1024]{1,0:T(8,128)S(1)}, f32[32,1024]{1,0:T(8,128)S(1)}, u32[]{:S(2)}, u32[]{:S(2)}) collective-permute-start(f32[32,1024]{1,0:T(8,128)S(1)} %convolution_add_fusion.6), channel_id=1, source_target_pairs={{504,0},{0,8},{8,16},{16,24},{24,32},{32,40},{40,48},{48,56},{56,6... | collective-permute-start | bytes 393224 | tf_op jit(solution)/shard_map/while/body/eval_jaxpr/ppermute | solution.py:13
  171.4 10.4 collective-permute-start.1
  199.0 10.3 collective-permute-start.1
  212.9 10.6 collective-permute-start.1
  227.1 10.8 %collective-permute-start.1 = (f32[32,1024]{1,0:T(8,128)S(1)}, f32[32,1024]{1,0:T(8,128)S(1)}, u32[]{:S(2)}, u32[]{:S(2)}) collective-permute-start(f32[32,1024]{1,0:T(8,128)S(1)} %convolution_add_fusion.6), channel_id=1, source_target_pairs={{504,0},{0,8},{8,16},{16,24},{24,32},{32,40},{40,48},{48,56},{56,6... | collective-permute-start | bytes 393224 | tf_op jit(solution)/shard_map/while/body/eval_jaxpr/ppermute | solution.py:13
  241.5 10.4 collective-permute-start.1
  255.5 9.9 collective-permute-start.1
  269.0 9.9 collective-permute-start.1
  282.6 9.9 collective-permute-start.1
  296.1 9.9 collective-permute-start.1
  309.7 9.9 collective-permute-start.1
  323.2 9.9 collective-permute-start.1
  336.8 9.9 collective-permute-start.1
  350.3 10.7 collective-permute-start.1
  364.6 11.1 %collective-permute-start.1 = (f32[32,1024]{1,0:T(8,128)S(1)}, f32[32,1024]{1,0:T(8,128)S(1)}, u32[]{:S(2)}, u32[]{:S(2)}) collective-permute-start(f32[32,1024]{1,0:T(8,128)S(1)} %convolution_add_fusion.6), channel_id=1, source_target_pairs={{504,0},{0,8},{8,16},{16,24},{24,32},{32,40},{40,48},{48,56},{56,6... | collective-permute-start | bytes 393224 | tf_op jit(solution)/shard_map/while/body/eval_jaxpr/ppermute | solution.py:13
  379.3 9.9 collective-permute-start.1
  392.9 9.9 collective-permute-start.1
  406.4 10.6 collective-permute-start.1
  420.7 10.7 collective-permute-start.1
  435.0 10.7 %collective-permute-start.1 = (f32[32,1024]{1,0:T(8,128)S(1)}, f32[32,1024]{1,0:T(8,128)S(1)}, u32[]{:S(2)}, u32[]{:S(2)}) collective-permute-start(f32[32,1024]{1,0:T(8,128)S(1)} %convolution_add_fusion.6), channel_id=1, source_target_pairs={{504,0},{0,8},{8,16},{16,24},{24,32},{32,40},{40,48},{48,56},{56,6... | collective-permute-start | bytes 393224 | tf_op jit(solution)/shard_map/while/body/eval_jaxpr/ppermute | solution.py:13
  449.3 10.3 collective-permute-start.1
  463.2 9.9 collective-permute-start.1
  476.8 9.9 collective-permute-start.1
  490.3 9.9 collective-permute-start.1
  503.9 9.9 collective-permute-start.1
  513.8 10.0 collective-permute-start
  517.4 9.9 collective-permute-start.1
  531.0 9.9 collective-permute-start.1
  544.5 9.9 collective-permute-start.1
  558.1 11.0 %collective-permute-start.1 = (f32[32,1024]{1,0:T(8,128)S(1)}, f32[32,1024]{1,0:T(8,128)S(1)}, u32[]{:S(2)}, u32[]{:S(2)}) collective-permute-start(f32[32,1024]{1,0:T(8,128)S(1)} %convolution_add_fusion.6), channel_id=1, source_target_pairs={{504,0},{0,8},{8,16},{16,24},{24,32},{32,40},{40,48},{48,56},{56,6... | collective-permute-start | bytes 393224 | tf_op jit(solution)/shard_map/while/body/eval_jaxpr/ppermute | solution.py:13
  572.7 10.8 %collective-permute-start.1 = (f32[32,1024]{1,0:T(8,128)S(1)}, f32[32,1024]{1,0:T(8,128)S(1)}, u32[]{:S(2)}, u32[]{:S(2)}) collective-permute-start(f32[32,1024]{1,0:T(8,128)S(1)} %convolution_add_fusion.6), channel_id=1, source_target_pairs={{504,0},{0,8},{8,16},{16,24},{24,32},{32,40},{40,48},{48,56},{56,6... | collective-permute-start | bytes 393224 | tf_op jit(solution)/shard_map/while/body/eval_jaxpr/ppermute | solution.py:13
  587.1 9.9 collective-permute-start.1
  600.7 9.9 collective-permute-start.1
  614.2 10.6 collective-permute-start.1
  628.5 10.8 %collective-permute-start.1 = (f32[32,1024]{1,0:T(8,128)S(1)}, f32[32,1024]{1,0:T(8,128)S(1)}, u32[]{:S(2)}, u32[]{:S(2)}) collective-permute-start(f32[32,1024]{1,0:T(8,128)S(1)} %convolution_add_fusion.6), channel_id=1, source_target_pairs={{504,0},{0,8},{8,16},{16,24},{24,32},{32,40},{40,48},{48,56},{56,6... | collective-permute-start | bytes 393224 | tf_op jit(solution)/shard_map/while/body/eval_jaxpr/ppermute | solution.py:13
  642.9 10.6 collective-permute-start.1
  657.1 9.9 collective-permute-start.1
  670.7 9.9 collective-permute-start.1
  684.2 9.9 collective-permute-start.1
  697.7 9.9 collective-permute-start.1
  721.2 10.2 collective-permute-start
  738.4 9.9 collective-permute-start.1
  751.9 10.7 collective-permute-start.1
  766.2 11.2 %collective-permute-start.1 = (f32[32,1024]{1,0:T(8,128)S(1)}, f32[32,1024]{1,0:T(8,128)S(1)}, u32[]{:S(2)}, u32[]{:S(2)}) collective-permute-start(f32[32,1024]{1,0:T(8,128)S(1)} %convolution_add_fusion.6), channel_id=1, source_target_pairs={{504,0},{0,8},{8,16},{16,24},{24,32},{32,40},{40,48},{48,56},{56,6... | collective-permute-start | bytes 393224 | tf_op jit(solution)/shard_map/while/body/eval_jaxpr/ppermute | solution.py:13
  781.0 10.3 collective-permute-start.1
  794.9 9.9 collective-permute-start.1
  808.5 10.4 collective-permute-start.1
  822.4 10.6 collective-permute-start.1
  836.7 10.7 %collective-permute-start.1 = (f32[32,1024]{1,0:T(8,128)S(1)}, f32[32,1024]{1,0:T(8,128)S(1)}, u32[]{:S(2)}, u32[]{:S(2)}) collective-permute-start(f32[32,1024]{1,0:T(8,128)S(1)} %convolution_add_fusion.6), channel_id=1, source_target_pairs={{504,0},{0,8},{8,16},{16,24},{24,32},{32,40},{40,48},{48,56},{56,6... | collective-permute-start | bytes 393224 | tf_op jit(solution)/shard_map/while/body/eval_jaxpr/ppermute | solution.py:13
  851.0 10.4 collective-permute-start.1
  865.0 9.9 collective-permute-start.1
  890.1 180.7 %collective-permute-start.2 = (f32[32,1024]{1,0:T(8,128)}, f32[32,1024]{1,0:T(8,128)S(1)}, u32[]{:S(2)}, u32[]{:S(2)}) collective-permute-start(f32[32,1024]{1,0:T(8,128)} %convolution_add_fusion.2), channel_id=1, source_target_pairs={{504,0},{0,8},{8,16},{16,24},{24,32},{32,40},{40,48},{48,56},{56,6... | collective-permute-start | bytes 393224 | tf_op jit(solution)/shard_map/ppermute | solution.py:13
  (70 other events, 605.5 us)
where the time goes:
time: 1080 us; the launch traced here: 1070 us
  waiting for transfers between devices  400 us (37%)
  starting transfers between devices  246 us (23%)
  blocking collectives  165 us (15%)
  matrix products  125 us (12%)
  loops' own time  117 us (11%)
    ppermute x127, waiting for transfers between devices, from_behind(): return lax.ppermute(block, axis, route)  400 us
    ppermute x127, starting transfers between devices, from_behind(): return lax.ppermute(block, axis, route)  246 us
    psum x1, blocking collectives, on_device(): lax.psum((sums_now[0], sums_now[1], sums_now[2]), ('blk', 'group'))  165 us
    another operation x1, loops' own time, on_device(): lax.fori_loop(0, cycle_size - 1, step_one, (text_embed, zero_rows, zero_r...  117 us
    dot_general x64, matrix products, score_tile(): lax.dot_general(sketch_embed, text_block, (((1,), (1,)), ((), ())), prefe...  93.6 us
  transfers between devices with their start and end apart: 127, of which 126 were waited for; matrix products, arithmetic and copies ran while one was open for 12% of the time, Pallas kernels for 0%

commit v1 on v0

v1 whole, which is shorter than its diff:
```python
import functools

import jax
import jax.numpy as jnp
from jax import lax
from jax.experimental import pallas as pl
from jax.experimental.pallas import tpu as pltpu
from jax.sharding import PartitionSpec as P

EPSILON = 1e-06
GELU_SCALE = 0.7978845608028654
GELU_CUBE = 0.044715
LANES = 128
VMEM_LIMIT = 48 * 1024 * 1024
F32 = jnp.float32
BF16 = jnp.bfloat16

VMEM = pl.BlockSpec(memory_space=pltpu.VMEM)
SMEM = pl.BlockSpec(memory_space=pltpu.SMEM)


def params():
    return pltpu.CompilerParams(vmem_limit_bytes=VMEM_LIMIT)


def three_parts(values):
    high = values.astype(BF16).astype(F32)
    rest = values - high
    middle = rest.astype(BF16).astype(F32)
    return high, middle, rest - middle


def rows_to_column(row, count):
    here = lax.broadcasted_iota(jnp.int32, (count, count), 0)
    there = lax.broadcasted_iota(jnp.int32, (count, count), 1)
    return jnp.sum(jnp.where(here == there, row, 0.0), axis=1, keepdims=True)


def text_kernel(text_ref, out_ref):
    text_in = text_ref[0].astype(F32)
    text_rnorm = lax.rsqrt(jnp.sum(text_in * text_in, axis=-1, keepdims=True) + EPSILON)
    text_embed = (text_in * text_rnorm).astype(BF16)
    for member in range(out_ref.shape[0]):
        out_ref[member] = text_embed


def forward_kernel(
    tokens_ref,
    gain_ref,
    weight_ref,
    lengths_ref,
    positives_ref,
    sample_ref,
    send_ref,
    slope_ref,
    pooled_ref,
    normed_ref,
):
    step = pl.program_id(0)
    sketches = lengths_ref.shape[-1]
    tok_count = tokens_ref.shape[1]
    width = weight_ref.shape[1]

    @pl.when(step == 0)
    def _():
        inputs = tokens_ref[0].astype(F32)
        inv_rms = lax.rsqrt(jnp.mean(inputs * inputs, axis=-1, keepdims=True) + EPSILON)
        normed_ref[...] = (inputs * inv_rms * gain_ref[...]).astype(BF16)

    lens_row = lengths_ref[0].astype(F32)
    lens_col = rows_to_column(lens_row, sketches)
    here = lax.broadcasted_iota(jnp.int32, (sketches, sketches), 0)
    there = lax.broadcasted_iota(jnp.int32, (sketches, sketches), 1)
    ends = jnp.sum(jnp.where(there <= here, lens_row, 0.0), axis=1, keepdims=True)
    place = lax.broadcasted_iota(jnp.int32, (sketches, tok_count), 1).astype(F32)
    membership = jnp.where((place < ends) & (place >= ends - lens_col), 1.0, 0.0).astype(BF16)

    values = jnp.dot(normed_ref[...], weight_ref[...], preferred_element_type=F32)
    square = values * values
    tanh_part = jnp.tanh(values * (GELU_SCALE + (GELU_SCALE * GELU_CUBE) * square))
    half = 0.5 + 0.5 * tanh_part
    activated = (values * half).astype(BF16)
    slope = half + values * (1.0 - tanh_part * tanh_part) * (
        0.5 * GELU_SCALE + (1.5 * GELU_SCALE * GELU_CUBE) * square
    )
    slope_ref[...] = slope.astype(BF16)
    pooled = jnp.dot(membership, activated, preferred_element_type=F32) / lens_col
    pooled_ref[:, pl.ds(pl.multiple_of(step * width, width), width)] = pooled

    @pl.when(step == pl.num_programs(0) - 1)
    def _():
        all_pooled = pooled_ref[...]
        rnorm = lax.rsqrt(jnp.sum(all_pooled * all_pooled, axis=-1, keepdims=True) + EPSILON)
        embed = (all_pooled * rnorm).astype(BF16)
        paired = rows_to_column(positives_ref[...].astype(F32), sketches)
        paired_high = jnp.floor(paired * (1.0 / 16.0))
        weight = three_parts(rows_to_column(sample_ref[...], sketches))
        columns = (paired_high, paired - 16.0 * paired_high) + weight
        lane = lax.broadcasted_iota(jnp.int32, (sketches, LANES), 1)
        extra = jnp.zeros((sketches, LANES), F32)
        for i, column in enumerate(columns):
            extra = jnp.where(lane == i, column, extra)
        extra = extra.astype(BF16)
        features = embed.shape[1]
        for member in range(send_ref.shape[0]):
            send_ref[member, :, :features] = embed
            send_ref[member, :, features:] = extra


def score_kernel(inv_count, cols, blk_ref, log_temp_ref, bias_ref, scale_ref, sketch_ref, text_ref, out_s_ref, out_t_ref):
    members, sketches, features = text_ref.shape
    rows = members * sketches
    sketch = sketch_ref[:, :, :features].reshape(rows, features)
    text = text_ref[...].reshape(rows, features)
    extra = sketch_ref[:, :, features:].reshape(rows, LANES).astype(F32)
    paired = extra[:, 0:1] * 16.0 + extra[:, 1:2]
    weight = (extra[:, 2:3] + extra[:, 3:4]) + extra[:, 4:5]
    weight = weight * inv_count
    dots = lax.dot_general(sketch, text, (((1,), (1,)), ((), ())), preferred_element_type=F32)
    temper = jnp.exp(jnp.full((1, 1), log_temp_ref[0], F32))
    logits = temper * dots + bias_ref[0]
    column = lax.broadcasted_iota(jnp.int32, (1, rows), 1)
    column = (column // sketches) * (cols * sketches) + (blk_ref[0] % cols) * sketches + column % sketches
    is_pair = paired == column.astype(F32)
    signs = jnp.where(is_pair, 1.0, -1.0)
    against = jnp.where(is_pair, -logits, logits)
    decay = jnp.exp(-jnp.abs(against))
    chance = jnp.where(against >= 0.0, 1.0, decay) / (1.0 + decay)
    pair_loss = jnp.maximum(against, 0.0) + jnp.log1p(decay)
    coeffs = -weight * signs * chance
    scaled = (coeffs * (temper * scale_ref[0])).astype(BF16)
    sketch_part = jnp.dot(scaled, text, preferred_element_type=F32).astype(BF16)
    text_part = lax.dot_general(scaled, sketch, (((0,), (0,)), ((), ())), preferred_element_type=F32).astype(BF16)
    out_t_ref[...] = text_part.reshape(text_ref.shape)
    out_s_ref[:, :, :features] = sketch_part.reshape(text_ref.shape)

    def total(values):
        return jnp.sum(jnp.sum(values, axis=1, keepdims=True), axis=0, keepdims=True)

    lane = lax.broadcasted_iota(jnp.int32, (sketches, LANES), 1)
    sums = jnp.zeros((sketches, LANES), F32)
    for i, value in enumerate((total(weight * pair_loss), total(coeffs * temper * dots), total(coeffs))):
        for j, piece in enumerate(three_parts(value)):
            sums = jnp.where(lane == 3 * j + i, piece, sums)
    sums = sums.astype(BF16)
    for member in range(members):
        out_s_ref[member, :, features:] = sums


def first_sums_kernel(in_ref, out_ref):
    members = in_ref.shape[0]
    gathered = jnp.zeros((8, LANES), F32)
    for member in range(members):
        gathered = gathered + in_ref[member, :8, :].astype(F32)
    lane = lax.broadcasted_iota(jnp.int32, (8, LANES), 1)
    result = jnp.zeros((8, LANES), F32)
    for i in range(3):
        value = gathered[:, i : i + 1] + (gathered[:, i + 3 : i + 4] + gathered[:, i + 6 : i + 7])
        result = jnp.where(lane == i, value, result)
    for member in range(out_ref.shape[0]):
        out_ref[member] = result


def next_sums_kernel(in_ref, out_ref):
    result = jnp.sum(in_ref[...], axis=0)
    for member in range(out_ref.shape[0]):
        out_ref[member] = result


def last_sums_kernel(in_ref, loss_ref, temp_ref, bias_ref):
    result = jnp.sum(in_ref[...], axis=0)
    loss_ref[...] = result[0:1, 0:1]
    temp_ref[...] = result[0:1, 1:2]
    bias_ref[...] = result[0:1, 2:3]


def backward_kernel(parts_ref, pooled_ref, lengths_ref, slope_ref, tokens_ref, gain_ref, weight_ref, out_ref, grad_ref):
    step = pl.program_id(0)
    sketches = lengths_ref.shape[-1]
    block = slope_ref.shape[0]
    lens_row = lengths_ref[0].astype(F32)
    lens_col = rows_to_column(lens_row, sketches)

    @pl.when(step == 0)
    def _():
        sketch_grad = jnp.sum(parts_ref[...].astype(F32), axis=0)
        pooled = pooled_ref[...]
        rnorm = lax.rsqrt(jnp.sum(pooled * pooled, axis=-1, keepdims=True) + EPSILON)
        unit = pooled * rnorm
        along = jnp.sum(unit * sketch_grad, axis=-1, keepdims=True)
        pool_grad = rnorm * (sketch_grad - unit * along) / lens_col
        high = pool_grad.astype(BF16)
        grad_ref[:sketches] = high
        grad_ref[sketches:] = (pool_grad - high.astype(F32)).astype(BF16)

    here = lax.broadcasted_iota(jnp.int32, (sketches, sketches), 0)
    there = lax.broadcasted_iota(jnp.int32, (sketches, sketches), 1)
    ends = jnp.sum(jnp.where(here <= there, lens_col, 0.0), axis=0, keepdims=True)
    place = lax.broadcasted_iota(jnp.int32, (block, sketches), 0).astype(F32) + (step * block).astype(F32)
    membership = jnp.where((place < ends) & (place >= ends - lens_row), 1.0, 0.0).astype(BF16)
    per_token = jnp.dot(membership, grad_ref[:sketches], preferred_element_type=F32) + jnp.dot(
        membership, grad_ref[sketches:], preferred_element_type=F32
    )
    act_grad = (per_token * slope_ref[...].astype(F32)).astype(BF16)
    normed_grad = lax.dot_general(
        act_grad, weight_ref[...], (((1,), (1,)), ((), ())), preferred_element_type=F32
    )
    inputs = tokens_ref[0].astype(F32)
    inv_rms = lax.rsqrt(jnp.mean(inputs * inputs, axis=-1, keepdims=True) + EPSILON)
    normal_x = inputs * inv_rms
    gain_part = normed_grad * gain_ref[...]
    token_grad = inv_rms * (gain_part - normal_x * jnp.mean(gain_part * normal_x, axis=-1, keepdims=True))
    out_ref[0] = token_grad.astype(BF16)


def text_grad_kernel(parts_ref, text_ref, out_ref):
    text_grad = jnp.sum(parts_ref[...].astype(F32), axis=0)
    text_in = text_ref[0].astype(F32)
    rnorm = lax.rsqrt(jnp.sum(text_in * text_in, axis=-1, keepdims=True) + EPSILON)
    unit = text_in * rnorm
    along = jnp.sum(unit * text_grad, axis=-1, keepdims=True)
    out_ref[0] = rnorm * (text_grad - unit * along)


def on_device(cycle_size, cycles, tokens, norm_gain, proj_weight, text_feats, lengths, positives, sample_weight, log_temp, logit_bias, loss_scale):
    tok_count, depth = tokens.shape[1:]
    features = proj_weight.shape[1]
    sketches = text_feats.shape[1]
    members = 8
    cols = cycle_size // members
    row_groups = [[r * members + c for c in range(members)] for r in range(cols)]
    col_groups = [[r * members + c for r in range(cols)] for c in range(members)]
    inv_count = 1.0 / (cycles * cycle_size * sketches)
    wide = features + LANES
    gain = norm_gain.reshape(1, depth)
    lens = lengths.reshape(1, 1, sketches)

    def exchange(values, groups):
        return lax.all_to_all(values, "blk", 0, 0, axis_index_groups=groups, tiled=True)

    text_send = pl.pallas_call(
        text_kernel,
        out_shape=jax.ShapeDtypeStruct((cols, sketches, features), BF16),
        in_specs=[VMEM],
        out_specs=VMEM,
        name="text_embed",
    )(text_feats)
    text_all = exchange(text_send, col_groups)

    steps = 4
    width = features // steps
    sketch_send, slope, pooled = pl.pallas_call(
        forward_kernel,
        grid=(steps,),
        out_shape=(
            jax.ShapeDtypeStruct((members, sketches, wide), BF16),
            jax.ShapeDtypeStruct((tok_count, features), BF16),
            jax.ShapeDtypeStruct((sketches, features), F32),
        ),
        in_specs=[
            pl.BlockSpec((1, tok_count, depth), lambda i: (0, 0, 0)),
            pl.BlockSpec((1, depth), lambda i: (0, 0)),
            pl.BlockSpec((depth, width), lambda i: (0, i)),
            pl.BlockSpec((1, 1, sketches), lambda i: (0, 0, 0)),
            pl.BlockSpec((1, sketches), lambda i: (0, 0)),
            pl.BlockSpec((1, sketches), lambda i: (0, 0)),
        ],
        out_specs=(
            pl.BlockSpec((members, sketches, wide), lambda i: (0, 0, 0)),
            pl.BlockSpec((tok_count, width), lambda i: (0, i)),
            pl.BlockSpec((sketches, features), lambda i: (0, 0)),
        ),
        scratch_shapes=[pltpu.VMEM((tok_count, depth), BF16)],
        compiler_params=params(),
        cost_estimate=pl.CostEstimate(flops=2 * tok_count * depth * features, bytes_accessed=5 << 20, transcendentals=tok_count * features),
        name="forward",
    )(tokens, gain, proj_weight, lens, positives, sample_weight)
    sketch_all = exchange(sketch_send, row_groups)

    blk = lax.axis_index("blk").astype(jnp.int32).reshape(1)
    sketch_parts, text_parts = pl.pallas_call(
        functools.partial(score_kernel, inv_count, members),
        out_shape=(
            jax.ShapeDtypeStruct((members, sketches, wide), BF16),
            jax.ShapeDtypeStruct((cols, sketches, features), BF16),
        ),
        in_specs=[SMEM, SMEM, SMEM, SMEM, VMEM, VMEM],
        out_specs=(VMEM, VMEM),
        compiler_params=params(),
        name="score",
    )(blk, log_temp.reshape(1), logit_bias.reshape(1), loss_scale.reshape(1), sketch_all, text_all)
    sketch_back = exchange(sketch_parts, row_groups)
    text_back = exchange(text_parts, col_groups)

    row_sums = pl.pallas_call(
        first_sums_kernel,
        grid=(1,),
        out_shape=jax.ShapeDtypeStruct((cols, 8, LANES), F32),
        in_specs=[pl.BlockSpec((members, sketches, LANES), lambda i: (0, 0, features // LANES))],
        out_specs=pl.BlockSpec((cols, 8, LANES), lambda i: (0, 0, 0)),
        name="row_sums",
    )(sketch_back)
    cycle_parts = exchange(row_sums, col_groups)
    cycle_sums = pl.pallas_call(
        next_sums_kernel,
        out_shape=jax.ShapeDtypeStruct((cycles, 8, LANES), F32),
        in_specs=[VMEM],
        out_specs=VMEM,
        name="cycle_sums",
    )(cycle_parts)
    all_parts = lax.all_to_all(cycle_sums, "group", 0, 0, tiled=True)
    scalar = jax.ShapeDtypeStruct((1, 1), F32)
    loss_value, grad_temp, grad_bias = pl.pallas_call(
        last_sums_kernel,
        out_shape=(scalar, scalar, scalar),
        in_specs=[VMEM],
        out_specs=(VMEM, VMEM, VMEM),
        name="all_sums",
    )(all_parts)

    block = 128
    grad_tokens = pl.pallas_call(
        backward_kernel,
        grid=(tok_count // block,),
        out_shape=jax.ShapeDtypeStruct(tokens.shape, BF16),
        in_specs=[
            pl.BlockSpec((members, sketches, features), lambda i: (0, 0, 0)),
            pl.BlockSpec((sketches, features), lambda i: (0, 0)),
            pl.BlockSpec((1, 1, sketches), lambda i: (0, 0, 0)),
            pl.BlockSpec((block, features), lambda i: (i, 0)),
            pl.BlockSpec((1, block, depth), lambda i: (0, i, 0)),
            pl.BlockSpec((1, depth), lambda i: (0, 0)),
            pl.BlockSpec((depth, features), lambda i: (0, 0)),
        ],
        out_specs=pl.BlockSpec((1, block, depth), lambda i: (0, i, 0)),
        scratch_shapes=[pltpu.VMEM((2 * sketches, features), BF16)],
        compiler_params=params(),
        cost_estimate=pl.CostEstimate(flops=2 * tok_count * depth * features, bytes_accessed=5 << 20, transcendentals=0),
        name="backward",
    )(sketch_back, pooled, lens, slope, tokens, gain, proj_weight)

    grad_texts = pl.pallas_call(
        text_grad_kernel,
        out_shape=jax.ShapeDtypeStruct(text_feats.shape, F32),
        in_specs=[VMEM, VMEM],
        out_specs=VMEM,
        name="text_grad",
    )(text_back, text_feats)
    return (grad_tokens, grad_texts, loss_value.reshape(()), grad_temp.reshape(()), grad_bias.reshape(()))


def solution(mesh):
    placed = (
        P("group", "blk", None),
        P(),
        P(),
        P("group", "blk", None),
        P("group", "blk", None),
        P("group", "blk"),
        P("group", "blk"),
        P(),
        P(),
        P(),
    )
    return jax.shard_map(
        functools.partial(on_device, mesh.shape["blk"], mesh.shape["group"]),
        mesh=mesh,
        in_specs=placed,
        out_specs=(P("group", "blk", None), P("group", "blk", None), P(), P(), P()),
        check_vma=False,
    )
```

time: 1080 us -> 114 us (0.11)
  waiting for transfers between devices: 400 us -> 29.2 us
  starting transfers between devices: 246 us -> 37.9 us
  blocking collectives: 165 us -> 12.8 us
  matrix products: 125 us -> 0 us
  loops' own time: 117 us -> 0 us
  Pallas kernels: 0 us -> 20.6 us
    ppermute x127 -> x0, waiting for transfers between devices: 400 us -> none  [from_behind(): return lax.ppermute(block, axis, route)]
    ppermute x127 -> x0, starting transfers between devices: 246 us -> none  [from_behind(): return lax.ppermute(block, axis, route)]
    psum x1 -> x0, blocking collectives: 165 us -> none  [on_device(): lax.psum((sums_now[0], sums_now[1], sums_now[2]), ('blk', 'group'))]
    dot_general x195 -> x0, matrix products: 125 us -> none  [the longest x64 93.6 us: score_tile(): lax.dot_general(sketch_embed, text_block, (((1,), (1,)), ((), ())), prefe...]
    another operation x1 -> x0, loops' own time: 117 us -> none  [on_device(): lax.fori_loop(0, cycle_size - 1, step_one, (text_embed, zero_rows, zero_r...]
    all_to_all x0 -> x5, starting transfers between devices: none -> 37.9 us  [the longest x4 23.6 us: exchange(): lax.all_to_all(values, 'blk', 0, 0, axis_index_groups=groups, tiled=True)]
    all_to_all x0 -> x5, waiting for transfers between devices: none -> 29.2 us  [the longest x4 29.2 us: exchange(): lax.all_to_all(values, 'blk', 0, 0, axis_index_groups=groups, tiled=True)]
    pallas_call x0 -> x8, Pallas kernels: none -> 20.6 us  [the longest x1 5.73 us: on_device(): pl.pallas_call(backward_kernel, grid=(tok_count // block,), out_shape=jax...]
  transfers between devices with their start and end apart: 127 -> 5, of which waited for: 126 -> 4; matrix products, arithmetic and copies ran while one was open for 12% -> 0% of each run, Pallas kernels for 0% -> 13%
where the time goes in v1:
time: 114 us; the launch traced here: 113 us
  starting transfers between devices  37.9 us (33%)
  waiting for transfers between devices  29.2 us (26%)
  Pallas kernels  20.6 us (18%)
  blocking collectives  12.8 us (11%)
  local copies, waits for them, and re-layouts  10.1 us (9%)
  between operations  2.65 us (2%)
    all_to_all x4, waiting for transfers between devices, exchange(): lax.all_to_all(values, 'blk', 0, 0, axis_index_groups=groups, tiled=True)  29.2 us
    all_to_all x4, starting transfers between devices, exchange(): lax.all_to_all(values, 'blk', 0, 0, axis_index_groups=groups, tiled=True)  23.6 us
    all_to_all x1, starting transfers between devices, on_device(): all_parts = lax.all_to_all(cycle_sums, 'group', 0, 0, tiled=True)  14.2 us
    all_to_all x1, blocking collectives, exchange(): lax.all_to_all(values, 'blk', 0, 0, axis_index_groups=groups, tiled=True)  12.8 us
    unnamed x32, local copies, waits for them, and re-layouts  10.1 us
    pallas_call x1, Pallas kernels, on_device(): pl.pallas_call(backward_kernel, grid=(tok_count // block,), out_shape=jax...  5.73 us
    pallas_call x1, Pallas kernels, on_device(): pl.pallas_call(forward_kernel, grid=(steps,), out_shape=(jax.ShapeDtypeSt...  4.89 us
  transfers between devices with their start and end apart: 5, of which 4 were waited for; matrix products, arithmetic and copies ran while one was open for 0% of the time, Pallas kernels for 13%

profile of v1, /device:TPU:1, one launch (start us, length us, event | category | flops | bytes accessed | tf_op | source)
XLA Modules:
  0.0 113.1 jit_solution(17758199847732705666)
XLA Ops:
  0.6 1.8 %text_embed.1 = bf16[8,32,1024]{2,1,0:T(8,128)(2,1)} custom-call(bf16[1,32,1024]{2,1,0:T(8,128)(2,1)} %text_ref.3), custom_call_target="tpu_custom_call" | custom-call | tf_op jit(solution)/shard_map/text_embed/pallas_call | solution.py:241
  2.4 7.7 %all-to-all-start.1 = ((bf16[8,32,1024]{2,1,0:T(8,128)(2,1)}), bf16[8,32,1024]{2,1,0:T(8,128)(2,1)S(1)}, u32[]{:S(2)}, u32[]{:S(2)}) async-start(bf16[8,32,1024]{2,1,0:T(8,128)(2,1)} %text_embed.1), calls=%async_computation.1 | async-start | bytes 1048576 | tf_op jit(solution)/shard_map/all_to_all | solution.py:239
  10.1 0.0 copy-start.1
  10.1 1.6 %copy-done.1 = bf16[1024,1024]{1,0:T(8,128)(2,1)S(1)} copy-done((bf16[1024,1024]{1,0:T(8,128)(2,1)S(1)}, bf16[1024,1024]{1,0:T(8,128)(2,1)}, u32[]{:S(2)}) %copy-start.1) | copy-done | bytes 2097176
  11.7 0.0 copy-start.3
  11.7 1.2 %copy-done.3 = bf16[1,512,1024]{2,1,0:T(8,128)(2,1)S(1)} copy-done((bf16[1,512,1024]{2,1,0:T(8,128)(2,1)S(1)}, bf16[1,512,1024]{2,1,0:T(8,128)(2,1)}, u32[]{:S(2)}) %copy-start.3) | copy-done | bytes 1048600
  12.9 0.0 copy-start.7
  12.9 0.7 copy-done.7
  13.6 0.0 copy-start.9
  13.6 0.7 copy-done.9
  14.2 0.0 copy-start.11
  14.2 0.7 copy-done.11
  14.9 0.0 copy-start.12
  14.9 0.7 copy-done.12
  15.5 4.9 %forward.1 = (bf16[8,32,1152]{2,1,0:T(8,128)(2,1)}, bf16[512,1024]{1,0:T(8,128)(2,1)S(1)}, f32[32,1024]{1,0:T(8,128)S(1)}) custom-call(bf16[1,512,1024]{2,1,0:T(8,128)(2,1)S(1)} %copy-done.3, f32[1,1024]{1,0:T(1,128)S(1)} %bitcast.11, bf16[1024,1024]{1,0:T(8,128)(2,1)S(1)} %copy-done.1, s32[1,1,32]{2,1,0:T(1,128)S(1)} %copy-done.9, s32[1,32]{1,0:T(1,128)S(1)} %copy-done.11, ...), custom_call_target="tpu_custom_call" | custom-call | flops 1073741824 | bytes 5242880 | tf_op jit(solution)/shard_map/forward/pallas_call | solution.py:252
  20.4 0.0 copy-start.5
  20.4 1.0 copy-done.5
  21.4 3.4 %all-to-all-done.1.text_ref = bf16[8,32,1024]{2,1,0:T(8,128)(2,1)S(1)} async-done(((bf16[8,32,1024]{2,1,0:T(8,128)(2,1)}), bf16[8,32,1024]{2,1,0:T(8,128)(2,1)S(1)}, u32[]{:S(2)}, u32[]{:S(2)}) %all-to-all-start.1) | async-done | bytes 524320 | tf_op jit(solution)/shard_map/all_to_all | solution.py:239
  24.8 9.0 %all-to-all-start = ((bf16[8,32,1152]{2,1,0:T(8,128)(2,1)}), bf16[8,32,1152]{2,1,0:T(8,128)(2,1)S(1)}, u32[]{:S(2)}, u32[]{:S(2)}) async-start(bf16[8,32,1152]{2,1,0:T(8,128)(2,1)} %get-tuple-element.13), calls=%async_computation | async-start | bytes 1179648 | tf_op jit(solution)/shard_map/all_to_all | solution.py:239
  35.8 7.8 %all-to-all-done.sketch_ref = bf16[8,32,1152]{2,1,0:T(8,128)(2,1)S(1)} async-done(((bf16[8,32,1152]{2,1,0:T(8,128)(2,1)}), bf16[8,32,1152]{2,1,0:T(8,128)(2,1)S(1)}, u32[]{:S(2)}, u32[]{:S(2)}) %all-to-all-start) | async-done | bytes 589856 | tf_op jit(solution)/shard_map/all_to_all | solution.py:239
  43.6 1.9 %score.1 = (bf16[8,32,1152]{2,1,0:T(8,128)(2,1)S(1)}, bf16[8,32,1024]{2,1,0:T(8,128)(2,1)}) custom-call(s32[1]{0:T(128)} %bitcast.blk_ref, f32[1]{0:T(128)} %bitcast.8.log_temp_ref, f32[1]{0:T(128)} %bitcast.9.bias_ref, f32[1]{0:T(128)} %bitcast.10.scale_ref, bf16[8,32,1152]{2,1,0:T(8,128)(2,1)S(1)} %all-to-all-done.sketch_ref, ...), custom_call_target="tpu_custom_call" | custom-call | tf_op jit(solution)/shard_map/score/pallas_call | solution.py:281
  45.5 0.0 copy-start.2
  45.5 0.0 copy-start.8
  45.5 0.0 copy-start.10
  45.5 12.8 %all_to_all.30.parts_ref.in_ref = bf16[8,32,1152]{2,1,0:T(8,128)(2,1)} all-to-all(bf16[8,32,1152]{2,1,0:T(8,128)(2,1)S(1)} %get-tuple-element.14), channel_id=1, replica_groups={{0,8,16,24,32,40,48,56},{64,72,80,88,96,104,112,120},{128,136,144,152,1..., dimensions={0} | all-to-all | bytes 1179648 | tf_op jit(solution)/shard_map/all_to_all | solution.py:239
  58.3 0.0 copy-start
  58.3 3.6 %all-to-all-start.3 = ((bf16[8,32,1024]{2,1,0:T(8,128)(2,1)}), bf16[8,32,1024]{2,1,0:T(8,128)(2,1)S(1)}, u32[]{:S(2)}, u32[]{:S(2)}) async-start(bf16[8,32,1024]{2,1,0:T(8,128)(2,1)} %get-tuple-element.17), calls=%async_computation.3 | async-start | bytes 1048576 | tf_op jit(solution)/shard_map/all_to_all | solution.py:239
  61.9 1.7 %row_sums.1 = f32[8,8,128]{2,1,0:T(8,128)} custom-call(bf16[8,32,1152]{2,1,0:T(8,128)(2,1)} %all_to_all.30.parts_ref.in_ref), custom_call_target="tpu_custom_call" | custom-call | tf_op jit(solution)/shard_map/row_sums/pallas_call | solution.py:295
  63.6 13.0 %all-to-all-done.3.parts_ref = bf16[8,32,1024]{2,1,0:T(8,128)(2,1)S(1)} async-done(((bf16[8,32,1024]{2,1,0:T(8,128)(2,1)}), bf16[8,32,1024]{2,1,0:T(8,128)(2,1)S(1)}, u32[]{:S(2)}, u32[]{:S(2)}) %all-to-all-start.3) | async-done | bytes 524320 | tf_op jit(solution)/shard_map/all_to_all | solution.py:239
  76.6 0.0 copy-start.13
  76.6 3.3 %all-to-all-start.4 = ((f32[8,8,128]{2,1,0:T(8,128)}), f32[8,8,128]{2,1,0:T(8,128)S(1)}, u32[]{:S(2)}, u32[]{:S(2)}) async-start(f32[8,8,128]{2,1,0:T(8,128)} %row_sums.1), calls=%async_computation.4 | async-start | bytes 65536 | tf_op jit(solution)/shard_map/all_to_all | solution.py:239
  79.9 0.0 copy-done.13
  79.9 1.9 %text_grad.1 = f32[1,32,1024]{2,1,0:T(8,128)} custom-call(bf16[8,32,1024]{2,1,0:T(8,128)(2,1)} %copy-done.13, bf16[1,32,1024]{2,1,0:T(8,128)(2,1)} %text_ref.3), custom_call_target="tpu_custom_call" | custom-call | tf_op jit(solution)/shard_map/text_grad/pallas_call | solution.py:342
  81.8 4.9 %all-to-all-done.4.in_ref = f32[8,8,128]{2,1,0:T(8,128)S(1)} async-done(((f32[8,8,128]{2,1,0:T(8,128)}), f32[8,8,128]{2,1,0:T(8,128)S(1)}, u32[]{:S(2)}, u32[]{:S(2)}) %all-to-all-start.4) | async-done | bytes 32800 | tf_op jit(solution)/shard_map/all_to_all | solution.py:239
  86.7 0.0 copy-start.15
  86.7 0.6 copy-done.15
  87.3 1.4 %cycle_sums.1 = f32[8,8,128]{2,1,0:T(8,128)} custom-call(f32[8,8,128]{2,1,0:T(8,128)} %copy-done.15), custom_call_target="tpu_custom_call" | custom-call | tf_op jit(solution)/shard_map/cycle_sums/pallas_call | solution.py:304
  88.7 14.2 %all-to-all-start.5 = ((f32[8,8,128]{2,1,0:T(8,128)}), f32[8,8,128]{2,1,0:T(8,128)S(1)}, u32[]{:S(2)}, u32[]{:S(2)}) async-start(f32[8,8,128]{2,1,0:T(8,128)} %cycle_sums.1), calls=%async_computation.5 | async-start | bytes 65536 | tf_op jit(solution)/shard_map/all_to_all | solution.py:311
  103.0 0.0 copy-done.2
  103.0 0.0 copy-done.8
  103.0 0.0 copy-done.10
  103.0 0.0 copy-done
  103.0 0.0 copy-start.4
  103.0 1.2 %copy-done.4 = bf16[1,512,1024]{2,1,0:T(8,128)(2,1)S(1)} copy-done((bf16[1,512,1024]{2,1,0:T(8,128)(2,1)S(1)}, bf16[1,512,1024]{2,1,0:T(8,128)(2,1)}, u32[]{:S(2)}) %copy-start.4) | copy-done | bytes 1048600
  104.2 0.0 copy-start.6
  104.2 1.2 %copy-done.6 = bf16[512,1024]{1,0:T(8,128)(2,1)S(1)} copy-done((bf16[512,1024]{1,0:T(8,128)(2,1)S(1)}, bf16[512,1024]{1,0:T(8,128)(2,1)}, u32[]{:S(2)}) %copy-start.6) | copy-done | bytes 1048600
  105.4 5.7 %backward.1 = bf16[1,512,1024]{2,1,0:T(8,128)(2,1)} custom-call(bf16[8,32,1152]{2,1,0:T(8,128)(2,1)S(1)} %copy-done, f32[32,1024]{1,0:T(8,128)S(1)} %get-tuple-element.15.pooled_ref, s32[1,1,32]{2,1,0:T(1,128)S(1)} %copy-done.10, bf16[512,1024]{1,0:T(8,128)(2,1)S(1)} %copy-done.6, bf16[1,512,1024]{2,1,0:T(8,128)(2,1)S(1)} %copy-done.4, ...), custom_call_target="tpu_custom_call" | custom-call | flops 1073741824 | bytes 5242880 | tf_op jit(solution)/shard_map/backward/pallas_call | solution.py:322
  111.2 0.0 all-to-all-done.5.in_ref
  111.2 0.0 copy-start.14
  111.2 0.6 copy-done.14
  111.8 1.3 %all_sums.1 = (f32[1,1]{1,0:T(1,128)}, f32[1,1]{1,0:T(1,128)}, f32[1,1]{1,0:T(1,128)}) custom-call(f32[8,8,128]{2,1,0:T(8,128)} %copy-done.14), custom_call_target="tpu_custom_call" | custom-call | tf_op jit(solution)/shard_map/all_sums/pallas_call | solution.py:313
Async XLA Ops:
  2.4 22.4 %all-to-all-start.1 = ((bf16[8,32,1024]{2,1,0:T(8,128)(2,1)}), bf16[8,32,1024]{2,1,0:T(8,128)(2,1)S(1)}, u32[]{:S(2)}, u32[]{:S(2)}) async-start(bf16[8,32,1024]{2,1,0:T(8,128)(2,1)} %text_embed.1), calls=%async_computation.1 | async-start | bytes 1048576 | tf_op jit(solution)/shard_map/all_to_all | solution.py:239
  10.1 1.6 %copy-start.1 = (bf16[1024,1024]{1,0:T(8,128)(2,1)S(1)}, bf16[1024,1024]{1,0:T(8,128)(2,1)}, u32[]{:S(2)}) copy-start(bf16[1024,1024]{1,0:T(8,128)(2,1)} %weight_ref.3) | copy-start | bytes 6291460
  11.7 1.2 %copy-start.3 = (bf16[1,512,1024]{2,1,0:T(8,128)(2,1)S(1)}, bf16[1,512,1024]{2,1,0:T(8,128)(2,1)}, u32[]{:S(2)}) copy-start(bf16[1,512,1024]{2,1,0:T(8,128)(2,1)} %tokens_ref.3) | copy-start | bytes 3145732
  12.9 0.7 copy-start.7
  13.6 0.7 copy-start.9
  14.2 0.7 copy-start.11
  14.9 0.7 copy-start.12
  20.4 1.0 copy-start.5
  24.8 18.8 %all-to-all-start = ((bf16[8,32,1152]{2,1,0:T(8,128)(2,1)}), bf16[8,32,1152]{2,1,0:T(8,128)(2,1)S(1)}, u32[]{:S(2)}, u32[]{:S(2)}) async-start(bf16[8,32,1152]{2,1,0:T(8,128)(2,1)} %get-tuple-element.13), calls=%async_computation | async-start | bytes 1179648 | tf_op jit(solution)/shard_map/all_to_all | solution.py:239
  45.5 57.5 %copy-start.2 = (bf16[1024,1024]{1,0:T(8,128)(2,1)S(1)}, bf16[1024,1024]{1,0:T(8,128)(2,1)}, u32[]{:S(2)}) copy-start(bf16[1024,1024]{1,0:T(8,128)(2,1)} %weight_ref.3) | copy-start | bytes 6291460
  45.5 57.5 %copy-start.8 = (f32[1024]{0:T(1024)S(1)}, f32[1024]{0:T(1024)}, u32[]{:S(2)}) copy-start(f32[1024]{0:T(1024)} %param.11) | copy-start | bytes 12292
  45.5 57.5 %copy-start.10 = (s32[1,1,32]{2,1,0:T(1,128)S(1)}, s32[1,1,32]{2,1,0:T(1,128)}, u32[]{:S(2)}) copy-start(s32[1,1,32]{2,1,0:T(1,128)} %lengths_ref.3) | copy-start | bytes 388
  58.3 44.7 %copy-start = (bf16[8,32,1152]{2,1,0:T(8,128)(2,1)S(1)}, bf16[8,32,1152]{2,1,0:T(8,128)(2,1)}, u32[]{:S(2)}) copy-start(bf16[8,32,1152]{2,1,0:T(8,128)(2,1)} %all_to_all.30.parts_ref.in_ref) | copy-start | bytes 1769476
  58.3 18.3 %all-to-all-start.3 = ((bf16[8,32,1024]{2,1,0:T(8,128)(2,1)}), bf16[8,32,1024]{2,1,0:T(8,128)(2,1)S(1)}, u32[]{:S(2)}, u32[]{:S(2)}) async-start(bf16[8,32,1024]{2,1,0:T(8,128)(2,1)} %get-tuple-element.17), calls=%async_computation.3 | async-start | bytes 1048576 | tf_op jit(solution)/shard_map/all_to_all | solution.py:239
  76.6 3.4 %copy-start.13 = (bf16[8,32,1024]{2,1,0:T(8,128)(2,1)}, bf16[8,32,1024]{2,1,0:T(8,128)(2,1)S(1)}, u32[]{:S(2)}) copy-start(bf16[8,32,1024]{2,1,0:T(8,128)(2,1)S(1)} %all-to-all-done.3.parts_ref) | copy-start | bytes 1572868
  76.6 10.1 %all-to-all-start.4 = ((f32[8,8,128]{2,1,0:T(8,128)}), f32[8,8,128]{2,1,0:T(8,128)S(1)}, u32[]{:S(2)}, u32[]{:S(2)}) async-start(f32[8,8,128]{2,1,0:T(8,128)} %row_sums.1), calls=%async_computation.4 | async-start | bytes 65536 | tf_op jit(solution)/shard_map/all_to_all | solution.py:239
  86.7 0.6 copy-start.15
  88.7 22.4 %all-to-all-start.5 = ((f32[8,8,128]{2,1,0:T(8,128)}), f32[8,8,128]{2,1,0:T(8,128)S(1)}, u32[]{:S(2)}, u32[]{:S(2)}) async-start(f32[8,8,128]{2,1,0:T(8,128)} %cycle_sums.1), calls=%async_computation.5 | async-start | bytes 65536 | tf_op jit(solution)/shard_map/all_to_all | solution.py:311
  103.0 1.2 %copy-start.4 = (bf16[1,512,1024]{2,1,0:T(8,128)(2,1)S(1)}, bf16[1,512,1024]{2,1,0:T(8,128)(2,1)}, u32[]{:S(2)}) copy-start(bf16[1,512,1024]{2,1,0:T(8,128)(2,1)} %tokens_ref.3) | copy-start | bytes 3145732
  104.2 1.2 %copy-start.6 = (bf16[512,1024]{1,0:T(8,128)(2,1)S(1)}, bf16[512,1024]{1,0:T(8,128)(2,1)}, u32[]{:S(2)}) copy-start(bf16[512,1024]{1,0:T(8,128)(2,1)} %copy-done.5) | copy-start | bytes 3145732
  111.2 0.6 copy-start.14

commit v2 on v0

v2 whole, which is shorter than its diff:
```python
import functools

import jax
import jax.numpy as jnp
from jax import lax
from jax.experimental import pallas as pl
from jax.experimental.pallas import tpu as pltpu
from jax.sharding import PartitionSpec as P

EPSILON = 1e-06
GELU_SCALE = 0.7978845608028654
GELU_CUBE = 0.044715
LANES = 128
VMEM_LIMIT = 32 * 1024 * 1024
F32 = jnp.float32
BF16 = jnp.bfloat16

VMEM = pl.BlockSpec(memory_space=pltpu.VMEM)
SMEM = pl.BlockSpec(memory_space=pltpu.SMEM)
HBM = pl.BlockSpec(memory_space=pltpu.HBM)


def params():
    return pltpu.CompilerParams(vmem_limit_bytes=VMEM_LIMIT)


def three_parts(values):
    high = values.astype(BF16).astype(F32)
    rest = values - high
    middle = rest.astype(BF16).astype(F32)
    return high, middle, rest - middle


def rows_to_column(row, count):
    here = lax.broadcasted_iota(jnp.int32, (count, count), 0)
    there = lax.broadcasted_iota(jnp.int32, (count, count), 1)
    return jnp.sum(jnp.where(here == there, row, 0.0), axis=1, keepdims=True)


def forward_kernel(
    tokens_hbm,
    gain_hbm,
    weight_hbm,
    lengths_hbm,
    positives_hbm,
    sample_hbm,
    send_hbm,
    slope_ref,
    pooled_ref,
    tokens_ref,
    gain_ref,
    weight_ref,
    lengths_ref,
    positives_ref,
    sample_ref,
    normed_ref,
    own_ref,
    small_sems,
    token_sems,
    weight_sems,
    send_sems,
):
    sketches = lengths_ref.shape[-1]
    tok_count, depth = tokens_ref.shape
    features = weight_ref.shape[1]
    token_parts, weight_parts = token_sems.shape[0], weight_sems.shape[0]
    block, width = tok_count // token_parts, features // weight_parts

    small = [
        pltpu.make_async_copy(source, target, small_sems.at[i])
        for i, (source, target) in enumerate(
            (
                (gain_hbm, gain_ref),
                (lengths_hbm, lengths_ref),
                (positives_hbm, positives_ref),
                (sample_hbm, sample_ref),
            )
        )
    ]
    token_copies = [
        pltpu.make_async_copy(
            tokens_hbm.at[0, pl.ds(i * block, block)], tokens_ref.at[pl.ds(i * block, block)], token_sems.at[i]
        )
        for i in range(token_parts)
    ]
    weight_copies = [
        pltpu.make_async_copy(
            weight_hbm.at[:, pl.ds(i * width, width)], weight_ref.at[:, pl.ds(i * width, width)], weight_sems.at[i]
        )
        for i in range(weight_parts)
    ]
    small[0].start()
    for copy in token_copies:
        copy.start()
    for copy in small[1:]:
        copy.start()
    for copy in weight_copies:
        copy.start()

    small[0].wait()
    gain = gain_ref[...]
    for i, copy in enumerate(token_copies):
        copy.wait()
        rows = pl.ds(i * block, block)
        inputs = tokens_ref[rows].astype(F32)
        inv_rms = lax.rsqrt(jnp.mean(inputs * inputs, axis=-1, keepdims=True) + EPSILON)
        normed_ref[rows] = (inputs * inv_rms * gain).astype(BF16)

    for copy in small[1:]:
        copy.wait()
    lens_row = lengths_ref[0].astype(F32)
    lens_col = rows_to_column(lens_row, sketches)
    here = lax.broadcasted_iota(jnp.int32, (sketches, sketches), 0)
    there = lax.broadcasted_iota(jnp.int32, (sketches, sketches), 1)
    ends = jnp.sum(jnp.where(there <= here, lens_row, 0.0), axis=1, keepdims=True)
    place = lax.broadcasted_iota(jnp.int32, (sketches, tok_count), 1).astype(F32)
    membership = jnp.where((place < ends) & (place >= ends - lens_col), 1.0, 0.0).astype(BF16)

    for i, copy in enumerate(weight_copies):
        copy.wait()
        columns = pl.ds(i * width, width)
        values = jnp.dot(normed_ref[...], weight_ref[:, columns], preferred_element_type=F32)
        square = values * values
        tanh_part = jnp.tanh(values * (GELU_SCALE + (GELU_SCALE * GELU_CUBE) * square))
        half = 0.5 + 0.5 * tanh_part
        activated = (values * half).astype(BF16)
        slope = half + values * (1.0 - tanh_part * tanh_part) * (
            0.5 * GELU_SCALE + (1.5 * GELU_SCALE * GELU_CUBE) * square
        )
        slope_ref[:, columns] = slope.astype(BF16)
        pooled_ref[:, columns] = jnp.dot(membership, activated, preferred_element_type=F32) / lens_col

    pooled = pooled_ref[...]
    rnorm = lax.rsqrt(jnp.sum(pooled * pooled, axis=-1, keepdims=True) + EPSILON)
    embed = (pooled * rnorm).astype(BF16)
    paired = rows_to_column(positives_ref[...].astype(F32), sketches)
    paired_high = jnp.floor(paired * (1.0 / 16.0))
    weight = three_parts(rows_to_column(sample_ref[...], sketches))
    lane = lax.broadcasted_iota(jnp.int32, (sketches, LANES), 1)
    extra = jnp.zeros((sketches, LANES), F32)
    for i, column in enumerate((paired_high, paired - 16.0 * paired_high) + weight):
        extra = jnp.where(lane == i, column, extra)
    own_ref[:, :features] = embed
    own_ref[:, features:] = extra.astype(BF16)
    send_copies = [
        pltpu.make_async_copy(own_ref, send_hbm.at[i], send_sems.at[i]) for i in range(send_hbm.shape[0])
    ]
    for copy in send_copies:
        copy.start()
    for copy in send_copies:
        copy.wait()


def score_kernel(
    inv_count,
    scalars_ref,
    place_ref,
    sketch_hbm,
    near_ref,
    other_ref,
    back_hbm,
    near_out_ref,
    other_out_hbm,
    sketch_ref,
    back_ref,
    other_out_ref,
    in_sem,
    out_sems,
):
    members, sketches = sketch_ref.shape[:2]
    far, _, features = near_ref.shape
    halves = 2
    rows, half = members * sketches, far * sketches
    texts = halves * half
    sketch_copy = pltpu.make_async_copy(sketch_hbm, sketch_ref, in_sem)
    sketch_copy.start()
    temper = jnp.exp(jnp.full((1, 1), scalars_ref[0], F32))
    column = lax.broadcasted_iota(jnp.int32, (1, texts), 1)
    first = jnp.zeros((1, texts), jnp.int32)
    for i in range(halves * far):
        first = jnp.where(column >= i * sketches, (place_ref[i] - i) * sketches, first)
    column = (column + first).astype(F32)
    text_in = jnp.concatenate(
        [ref[...].reshape(half, features) for ref in (near_ref, other_ref)], axis=0
    ).astype(F32)
    text_rnorm = lax.rsqrt(jnp.sum(text_in * text_in, axis=-1, keepdims=True) + EPSILON)
    text = (text_in * text_rnorm).astype(BF16)
    sketch_copy.wait()
    sketch = sketch_ref[:, :, :features].reshape(rows, features)
    extra = sketch_ref[:, :, features:].reshape(rows, LANES).astype(F32)
    paired = extra[:, 0:1] * 16.0 + extra[:, 1:2]
    weight = ((extra[:, 2:3] + extra[:, 3:4]) + extra[:, 4:5]) * inv_count
    dots = lax.dot_general(sketch, text, (((1,), (1,)), ((), ())), preferred_element_type=F32)
    logits = temper * dots + scalars_ref[1]
    is_pair = paired == column
    signs = jnp.where(is_pair, 1.0, -1.0)
    against = jnp.where(is_pair, -logits, logits)
    decay = jnp.exp(-jnp.abs(against))
    chance = jnp.where(against >= 0.0, 1.0, decay) / (1.0 + decay)
    coeffs = -weight * signs * chance
    scaled = (coeffs * (temper * scalars_ref[2])).astype(BF16)
    sketch_part = jnp.dot(scaled, text, preferred_element_type=F32).astype(BF16)
    back_ref[:, :, :features] = sketch_part.reshape(members, sketches, features)
    pair_loss = jnp.maximum(against, 0.0) + jnp.log1p(decay)

    def total(values):
        return jnp.sum(jnp.sum(values, axis=1, keepdims=True), axis=0, keepdims=True)

    lane = lax.broadcasted_iota(jnp.int32, (sketches, LANES), 1)
    sums = jnp.zeros((sketches, LANES), F32)
    for i, value in enumerate((total(weight * pair_loss), total(coeffs * temper * dots), total(coeffs))):
        for j, piece in enumerate(three_parts(value)):
            sums = jnp.where(lane == 3 * j + i, piece, sums)
    sums = sums.astype(BF16)
    for member in range(members):
        back_ref[member, :, features:] = sums
    back_copy = pltpu.make_async_copy(back_ref, back_hbm, out_sems.at[0])
    back_copy.start()
    text_part = lax.dot_general(scaled, sketch, (((0,), (0,)), ((), ())), preferred_element_type=F32)
    other_out_ref[...] = text_part[half:].astype(BF16).reshape(far, sketches, features)
    other_out_copy = pltpu.make_async_copy(other_out_ref, other_out_hbm, out_sems.at[1])
    other_out_copy.start()
    near_out_ref[...] = text_part[:half].reshape(far, sketches, features)
    back_copy.wait()
    other_out_copy.wait()


def backward_kernel(
    parts_ref,
    pooled_ref,
    slope_ref,
    lengths_hbm,
    tokens_hbm,
    gain_hbm,
    weight_hbm,
    out_hbm,
    lengths_ref,
    tokens_ref,
    gain_ref,
    weight_ref,
    act_ref,
    back_ref,
    out_ref,
    small_sems,
    token_sems,
    weight_sems,
    out_sems,
):
    sketches = lengths_ref.shape[-1]
    tok_count, depth = tokens_ref.shape
    features = slope_ref.shape[1]
    token_parts, weight_parts = token_sems.shape[0], weight_sems.shape[0]
    block, width = tok_count // token_parts, depth // weight_parts

    def rows(i):
        return pl.ds(i * block, block)

    def columns(i):
        return pl.ds(i * width, width)

    small = [
        pltpu.make_async_copy(lengths_hbm, lengths_ref, small_sems.at[0]),
        pltpu.make_async_copy(gain_hbm, gain_ref, small_sems.at[1]),
    ]
    weight_copies = [
        pltpu.make_async_copy(weight_hbm.at[columns(i)], weight_ref.at[columns(i)], weight_sems.at[i])
        for i in range(weight_parts)
    ]
    token_copies = [
        pltpu.make_async_copy(tokens_hbm.at[0, rows(i)], tokens_ref.at[rows(i)], token_sems.at[i])
        for i in range(token_parts)
    ]
    for copy in small + weight_copies + token_copies:
        copy.start()

    sketch_grad = jnp.sum(parts_ref[:, :, :features].astype(F32), axis=0)
    pooled = pooled_ref[...]
    rnorm = lax.rsqrt(jnp.sum(pooled * pooled, axis=-1, keepdims=True) + EPSILON)
    unit = pooled * rnorm
    along = jnp.sum(unit * sketch_grad, axis=-1, keepdims=True)
    for copy in small:
        copy.wait()
    lens_row = lengths_ref[0].astype(F32)
    lens_col = rows_to_column(lens_row, sketches)
    pool_grad = rnorm * (sketch_grad - unit * along) / lens_col
    high = pool_grad.astype(BF16)
    both = jnp.concatenate([high, (pool_grad - high.astype(F32)).astype(BF16)], axis=0)

    here = lax.broadcasted_iota(jnp.int32, (sketches, sketches), 0)
    there = lax.broadcasted_iota(jnp.int32, (sketches, sketches), 1)
    ends = jnp.sum(jnp.where(here <= there, lens_col, 0.0), axis=0, keepdims=True)
    place = lax.broadcasted_iota(jnp.int32, (tok_count, sketches), 0).astype(F32)
    membership = jnp.where((place < ends) & (place >= ends - lens_row), 1.0, 0.0).astype(BF16)
    membership = jnp.concatenate([membership, membership], axis=1)
    for i in range(token_parts):
        per_token = jnp.dot(membership[i * block : (i + 1) * block], both, preferred_element_type=F32)
        act_ref[rows(i)] = (per_token * slope_ref[rows(i)].astype(F32)).astype(BF16)

    for copy in token_copies:
        copy.wait()
    along_x = jnp.zeros((tok_count, 1), F32)
    power = jnp.zeros((tok_count, 1), F32)
    for i, copy in enumerate(weight_copies):
        copy.wait()
        grad = lax.dot_general(
            act_ref[...], weight_ref[columns(i)], (((1,), (1,)), ((), ())), preferred_element_type=F32
        )
        gain_part = grad * gain_ref[:, columns(i)]
        inputs = tokens_ref[:, columns(i)].astype(F32)
        back_ref[:, columns(i)] = gain_part
        along_x += jnp.sum(gain_part * inputs, axis=-1, keepdims=True)
        power += jnp.sum(inputs * inputs, axis=-1, keepdims=True)
    inv_rms = lax.rsqrt(power * (1.0 / depth) + EPSILON)
    shrink = inv_rms * inv_rms * inv_rms * (along_x * (1.0 / depth))
    out_copies = []
    for i in range(token_parts):
        span = slice(i * block, (i + 1) * block)
        inputs = tokens_ref[rows(i)].astype(F32)
        out_ref[rows(i)] = (inv_rms[span] * back_ref[rows(i)] - shrink[span] * inputs).astype(BF16)
        copy = pltpu.make_async_copy(out_ref.at[rows(i)], out_hbm.at[0, rows(i)], out_sems.at[i])
        copy.start()
        out_copies.append(copy)
    for copy in out_copies:
        copy.wait()


def on_device(cycle_size, cycles, tokens, norm_gain, proj_weight, text_feats, lengths, positives, sample_weight, log_temp, logit_bias, loss_scale):
    tok_count, depth = tokens.shape[1:]
    features = proj_weight.shape[1]
    sketches = text_feats.shape[1]
    far, near, members = lax.axis_size("far"), lax.axis_size("near"), lax.axis_size("col")
    inv_count = 1.0 / (cycles * cycle_size * sketches)
    wide = features + LANES

    def in_hbm(*values):
        return [pltpu.with_memory_space_constraint(value, pltpu.HBM) for value in values]

    def in_vmem(*values):
        return [pltpu.with_memory_space_constraint(value, pltpu.VMEM) for value in values]

    def partner(block):
        return lax.ppermute(block, "near", [(i, (i + 1) % near) for i in range(near)])

    text_send = jnp.broadcast_to(text_feats, (far, sketches, features))
    near_texts = lax.all_to_all(text_send, "far", 0, 0, tiled=True)

    gain, weights = norm_gain.reshape(1, depth), proj_weight
    token_parts, weight_parts = 4, 4
    sketch_send, slope, pooled = pl.pallas_call(
        forward_kernel,
        out_shape=(
            pltpu.HBM((members, sketches, wide), BF16),
            pltpu.VMEM((tok_count, features), BF16),
            pltpu.VMEM((sketches, features), F32),
        ),
        in_specs=[HBM] * 6,
        out_specs=(HBM, VMEM, VMEM),
        scratch_shapes=[
            pltpu.VMEM((tok_count, depth), BF16),
            pltpu.VMEM((1, depth), F32),
            pltpu.VMEM((depth, features), BF16),
            pltpu.VMEM((1, 1, sketches), jnp.int32),
            pltpu.VMEM((1, sketches), jnp.int32),
            pltpu.VMEM((1, sketches), F32),
            pltpu.VMEM((tok_count, depth), BF16),
            pltpu.VMEM((sketches, wide), BF16),
            pltpu.SemaphoreType.DMA((4,)),
            pltpu.SemaphoreType.DMA((token_parts,)),
            pltpu.SemaphoreType.DMA((weight_parts,)),
            pltpu.SemaphoreType.DMA((members,)),
        ],
        compiler_params=params(),
        cost_estimate=pl.CostEstimate(flops=2 * tok_count * depth * features, bytes_accessed=5 << 20, transcendentals=tok_count * features),
        name="forward",
    )(*in_hbm(tokens, gain, weights, lengths, positives, sample_weight))
    sketch_all = lax.all_to_all(sketch_send, "col", 0, 0, tiled=True)
    other_texts = partner(near_texts)

    far_place, near_place, col = lax.axis_index("far"), lax.axis_index("near"), lax.axis_index("col")
    place = jnp.stack(
        [(f * near + (near_place + h) % near) * members + col for h in range(near) for f in range(far)]
    ).astype(jnp.int32)
    scalars = jnp.stack([log_temp, logit_bias, loss_scale])
    sketch_parts, near_part, other_part = pl.pallas_call(
        functools.partial(score_kernel, inv_count),
        out_shape=(
            pltpu.HBM((members, sketches, wide), BF16),
            pltpu.VMEM((far, sketches, features), F32),
            pltpu.HBM((far, sketches, features), BF16),
        ),
        in_specs=[SMEM, SMEM, HBM, VMEM, VMEM],
        out_specs=(HBM, VMEM, HBM),
        scratch_shapes=[
            pltpu.VMEM((members, sketches, wide), BF16),
            pltpu.VMEM((members, sketches, wide), BF16),
            pltpu.VMEM((far, sketches, features), BF16),
            pltpu.SemaphoreType.DMA,
            pltpu.SemaphoreType.DMA((2,)),
        ],
        compiler_params=params(),
        name="score",
    )(scalars, place, *in_hbm(sketch_all), *in_vmem(near_texts, other_texts))
    sketch_back = lax.all_to_all(sketch_parts, "col", 0, 0, tiled=True)
    text_sum = (near_part + partner(other_part).astype(F32)).astype(BF16)

    def lane_sums(parts):
        found = jnp.sum(parts[:, 0, features : features + 9].astype(F32), axis=0)
        return found[0:3] + (found[3:6] + found[6:9])

    def rounded(values):
        return lax.reduce_precision(values, 8, 7)

    row_sums = lane_sums(sketch_back)
    high = rounded(row_sums)
    middle = rounded(row_sums - high)
    row_lanes = jnp.pad(jnp.concatenate([high, middle, row_sums - high - middle]), (0, LANES - 9)).astype(BF16)
    text_parts = jnp.concatenate([text_sum, jnp.broadcast_to(row_lanes, (far, sketches, LANES))], axis=2)
    text_back = lax.all_to_all(text_parts, "far", 0, 0, tiled=True)

    grad_tokens = pl.pallas_call(
        backward_kernel,
        out_shape=pltpu.HBM(tokens.shape, BF16),
        in_specs=[VMEM] * 3 + [HBM] * 4,
        out_specs=HBM,
        scratch_shapes=[
            pltpu.VMEM((1, 1, sketches), jnp.int32),
            pltpu.VMEM((tok_count, depth), BF16),
            pltpu.VMEM((1, depth), F32),
            pltpu.VMEM((depth, features), BF16),
            pltpu.VMEM((tok_count, features), BF16),
            pltpu.VMEM((tok_count, depth), F32),
            pltpu.VMEM((tok_count, depth), BF16),
            pltpu.SemaphoreType.DMA((2,)),
            pltpu.SemaphoreType.DMA((token_parts,)),
            pltpu.SemaphoreType.DMA((weight_parts,)),
            pltpu.SemaphoreType.DMA((token_parts,)),
        ],
        compiler_params=params(),
        cost_estimate=pl.CostEstimate(flops=2 * tok_count * depth * features, bytes_accessed=5 << 20, transcendentals=0),
        name="backward",
    )(sketch_back, *in_vmem(pooled, slope), *in_hbm(lengths, tokens, gain, weights))

    sums_send = jnp.broadcast_to(jnp.pad(lane_sums(text_back), (0, LANES - 3)), (near * cycles, 8, LANES))
    sums_all = lax.all_to_all(sums_send, ("near", "group"), 0, 0, tiled=True)
    sums = jnp.sum(sums_all[:, 0, :3], axis=0)

    text_grad = jnp.sum(text_back[:, :, :features].astype(F32), axis=0, keepdims=True)
    text_in = text_feats.astype(F32)
    rnorm = lax.rsqrt(jnp.sum(text_in * text_in, axis=-1, keepdims=True) + EPSILON)
    unit = text_in * rnorm
    along = jnp.sum(unit * text_grad, axis=-1, keepdims=True)
    grad_texts = rnorm * (text_grad - unit * along)
    return (grad_tokens, grad_texts, sums[0], sums[1], sums[2])


def solution(mesh):
    cycle_size, cycles = mesh.shape["blk"], mesh.shape["group"]
    far, near = 4, 2
    tiles = jax.sharding.Mesh(
        mesh.devices.reshape(far, near, cycle_size // (far * near), cycles), ("far", "near", "col", "group")
    )
    blk = ("far", "near", "col")
    placed = (
        P("group", blk, None),
        P(),
        P(),
        P("group", blk, None),
        P("group", blk, None),
        P("group", blk),
        P("group", blk),
        P(),
        P(),
        P(),
    )
    return jax.shard_map(
        functools.partial(on_device, cycle_size, cycles),
        mesh=tiles,
        in_specs=placed,
        out_specs=(P("group", blk, None), P("group", blk, None), P(), P(), P()),
        check_vma=False,
    )
```

time: 1080 us -> 89.7 us (0.08)
  waiting for transfers between devices: 400 us -> 20.1 us
  starting transfers between devices: 246 us -> 44 us
  blocking collectives: 165 us -> 0 us
  matrix products: 125 us -> 0 us
  loops' own time: 117 us -> 0 us
  Pallas kernels: 0 us -> 16.2 us
    ppermute x127 -> x2, waiting for transfers between devices: 400 us -> 7.87 us  [partner(): lax.ppermute(block, 'near', [(i, (i + 1) % near) for i in range(near)])]
    ppermute x127 -> x2, starting transfers between devices: 246 us -> 4.69 us  [partner(): lax.ppermute(block, 'near', [(i, (i + 1) % near) for i in range(near)])]
    psum x1 -> x0, blocking collectives: 165 us -> none  [on_device(): lax.psum((sums_now[0], sums_now[1], sums_now[2]), ('blk', 'group'))]
    dot_general x195 -> x0, matrix products: 125 us -> none  [the longest x64 93.6 us: score_tile(): lax.dot_general(sketch_embed, text_block, (((1,), (1,)), ((), ())), prefe...]
    another operation x1 -> x0, loops' own time: 117 us -> none  [on_device(): lax.fori_loop(0, cycle_size - 1, step_one, (text_embed, zero_rows, zero_r...]
    all_to_all x0 -> x5, starting transfers between devices: none -> 39.3 us  [the longest x1 15.2 us: on_device(): sums_all = lax.all_to_all(sums_send, ('near', 'group'), 0, 0, tiled=True)]
    pallas_call x0 -> x3, Pallas kernels: none -> 16.2 us  [the longest x1 6.87 us: on_device(): pl.pallas_call(forward_kernel, out_shape=(pltpu.HBM((members, sketches, w...]
    all_to_all x0 -> x5, waiting for transfers between devices: none -> 12.3 us  [the longest x1 7.25 us: on_device(): sums_all = lax.all_to_all(sums_send, ('near', 'group'), 0, 0, tiled=True)]
  transfers between devices with their start and end apart: 127 -> 7, of which waited for: 126 -> 7; matrix products, arithmetic and copies ran while one was open for 12% -> 1% of each run, Pallas kernels for 0% -> 14%
where the time goes in v2:
time: 89.7 us; the launch traced here: 89 us
  starting transfers between devices  44 us (49%)
  waiting for transfers between devices  20.1 us (22%)
  Pallas kernels  16.2 us (18%)
  local copies, waits for them, and re-layouts  3.69 us (4%)
  between operations  2.67 us (3%)
  other arithmetic  2.31 us (3%)
    all_to_all x1, starting transfers between devices, on_device(): sums_all = lax.all_to_all(sums_send, ('near', 'group'), 0, 0, tiled=True)  15.2 us
    ppermute x2, waiting for transfers between devices, partner(): lax.ppermute(block, 'near', [(i, (i + 1) % near) for i in range(near)])  7.87 us
    all_to_all x1, starting transfers between devices, on_device(): near_texts = lax.all_to_all(text_send, 'far', 0, 0, tiled=True)  7.64 us
    all_to_all x1, waiting for transfers between devices, on_device(): sums_all = lax.all_to_all(sums_send, ('near', 'group'), 0, 0, tiled=True)  7.25 us
    pallas_call x1, Pallas kernels, on_device(): pl.pallas_call(forward_kernel, out_shape=(pltpu.HBM((members, sketches, w...  6.87 us
    all_to_all x1, starting transfers between devices, on_device(): text_back = lax.all_to_all(text_parts, 'far', 0, 0, tiled=True)  6.64 us
    pallas_call x1, Pallas kernels, on_device(): pl.pallas_call(backward_kernel, out_shape=pltpu.HBM(tokens.shape, BF16),...  5.79 us
    all_to_all x1, starting transfers between devices, on_device(): sketch_all = lax.all_to_all(sketch_send, 'col', 0, 0, tiled=True)  5.23 us
  transfers between devices with their start and end apart: 7, of which 7 were waited for; matrix products, arithmetic and copies ran while one was open for 1% of the time, Pallas kernels for 14%

profile of v2, /device:TPU:1, one launch (start us, length us, event | category | flops | bytes accessed | tf_op | source)
XLA Modules:
  0.0 89.0 jit_solution(13294683459073578428)
XLA Ops:
  0.6 1.6 %broadcast_in_dim.19 = bf16[4,32,1024]{2,1,0:T(8,128)(2,1)} broadcast(bf16[32,1024]{1,0:T(8,128)(2,1)} %bitcast.22), dimensions={1,2} | broadcast | bytes 327680 | tf_op jit(solution)/shard_map/broadcast_in_dim | solution.py:344
  2.2 7.6 %all-to-all-start.1 = ((bf16[4,32,1024]{2,1,0:T(8,128)(2,1)}), bf16[4,32,1024]{2,1,0:T(8,128)(2,1)S(1)}, u32[]{:S(2)}, u32[]{:S(2)}) async-start(bf16[4,32,1024]{2,1,0:T(8,128)(2,1)} %broadcast_in_dim.19), calls=%async_computation.1 | async-start | bytes 524288 | tf_op jit(solution)/shard_map/all_to_all | solution.py:345
  9.8 6.9 %forward.1 = (bf16[8,32,1152]{2,1,0:T(8,128)(2,1)}, bf16[512,1024]{1,0:T(8,128)(2,1)S(1)}, f32[32,1024]{1,0:T(8,128)S(1)}) custom-call(bf16[1,512,1024]{2,1,0:T(8,128)(2,1)} %tokens_hbm.3, f32[1,1024]{1,0:T(1,128)} %bitcast.23, bf16[1024,1024]{1,0:T(8,128)(2,1)} %weight_hbm.3, s32[1,1,32]{2,1,0:T(1,128)} %lengths_hbm.3, s32[1,32]{1,0:T(1,128)} %positives_hbm.1, ...), custom_call_target="tpu_custom_call" | custom-call | flops 1073741824 | bytes 5242880 | tf_op jit(solution)/shard_map/forward/pallas_call | solution.py:349
  16.7 1.8 %all-to-all-done.1.near_ref = bf16[4,32,1024]{2,1,0:T(8,128)(2,1)S(1)} async-done(((bf16[4,32,1024]{2,1,0:T(8,128)(2,1)}), bf16[4,32,1024]{2,1,0:T(8,128)(2,1)S(1)}, u32[]{:S(2)}, u32[]{:S(2)}) %all-to-all-start.1) | async-done | bytes 262176 | tf_op jit(solution)/shard_map/all_to_all | solution.py:345
  18.6 5.2 %all-to-all-start = ((bf16[8,32,1152]{2,1,0:T(8,128)(2,1)}), bf16[8,32,1152]{2,1,0:T(8,128)(2,1)S(1)}, u32[]{:S(2)}, u32[]{:S(2)}) async-start(bf16[8,32,1152]{2,1,0:T(8,128)(2,1)} %get-tuple-element.11), calls=%async_computation | async-start | bytes 1179648 | tf_op jit(solution)/shard_map/all_to_all | solution.py:376
  23.8 2.3 %collective-permute-start = (bf16[4,32,1024]{2,1,0:T(8,128)(2,1)S(1)}, bf16[4,32,1024]{2,1,0:T(8,128)(2,1)S(1)}, u32[]{:S(2)}, u32[]{:S(2)}) collective-permute-start(bf16[4,32,1024]{2,1,0:T(8,128)(2,1)S(1)} %all-to-all-done.1.near_ref), channel_id=1, source_target_pairs={{0,64},{64,0},{1,65},{65,1},{2,66},{66,2},{3,67},{67,3},{4,68},{68... | collective-permute-start | bytes 786440 | tf_op jit(solution)/shard_map/ppermute | solution.py:342
  28.1 0.1 stack.51.place_ref
  28.2 0.1 pad_maximum_fusion.1.scalars_ref
  28.3 0.0 copy-start.1
  28.3 2.9 %collective-permute-done.other_ref = bf16[4,32,1024]{2,1,0:T(8,128)(2,1)S(1)} collective-permute-done((bf16[4,32,1024]{2,1,0:T(8,128)(2,1)S(1)}, bf16[4,32,1024]{2,1,0:T(8,128)(2,1)S(1)}, u32[]{:S(2)}, u32[]{:S(2)}) %collective-permute-start) | collective-permute-done | bytes 262176 | tf_op jit(solution)/shard_map/ppermute | solution.py:342
  31.2 0.5 all-to-all-done.sketch_hbm
  31.7 0.0 copy-start
  31.7 0.8 copy-done
  32.5 3.5 %score.1 = (bf16[8,32,1152]{2,1,0:T(8,128)(2,1)}, f32[4,32,1024]{2,1,0:T(8,128)S(1)}, bf16[4,32,1024]{2,1,0:T(8,128)(2,1)}) custom-call(f32[3]{0:T(128)S(1)} %pad_maximum_fusion.1.scalars_ref, s32[8]{0:T(128)S(1)} %stack.51.place_ref, bf16[8,32,1152]{2,1,0:T(8,128)(2,1)} %copy-done, bf16[4,32,1024]{2,1,0:T(8,128)(2,1)S(1)} %all-to-all-done.1.near_ref, ...), custom_call_target="tpu_custom_call" | custom-call | tf_op jit(solution)/shard_map/score/pallas_call | solution.py:384
  36.0 4.7 %all-to-all-start.2 = ((bf16[8,32,1152]{2,1,0:T(8,128)(2,1)}), bf16[8,32,1152]{2,1,0:T(8,128)(2,1)S(1)}, u32[]{:S(2)}, u32[]{:S(2)}) async-start(bf16[8,32,1152]{2,1,0:T(8,128)(2,1)} %get-tuple-element.12), calls=%async_computation.2 | async-start | bytes 1179648 | tf_op jit(solution)/shard_map/all_to_all | solution.py:403
  40.7 2.3 %collective-permute-start.1 = (bf16[4,32,1024]{2,1,0:T(8,128)(2,1)}, bf16[4,32,1024]{2,1,0:T(8,128)(2,1)S(1)}, u32[]{:S(2)}, u32[]{:S(2)}) collective-permute-start(bf16[4,32,1024]{2,1,0:T(8,128)(2,1)} %get-tuple-element.16), channel_id=1, source_target_pairs={{0,64},{64,0},{1,65},{65,1},{2,66},{66,2},{3,67},{67,3},{4,68},{68... | collective-permute-start | bytes 786440 | tf_op jit(solution)/shard_map/ppermute | solution.py:342
  43.0 5.0 %collective-permute-done.1 = bf16[4,32,1024]{2,1,0:T(8,128)(2,1)S(1)} collective-permute-done((bf16[4,32,1024]{2,1,0:T(8,128)(2,1)}, bf16[4,32,1024]{2,1,0:T(8,128)(2,1)S(1)}, u32[]{:S(2)}, u32[]{:S(2)}) %collective-permute-start.1) | collective-permute-done | bytes 262176 | tf_op jit(solution)/shard_map/ppermute | solution.py:342
  48.0 0.1 add_convert_fusion
  48.0 0.5 all-to-all-done.2.parts_ref
  48.6 0.1 reduce-precision_convert_fusion.1
  48.7 0.1 select_maximum_fusion
  48.7 0.8 pad_maximum_fusion
  49.5 6.6 %all-to-all-start.3 = ((bf16[4,32,1152]{2,1,0:T(8,128)(2,1)}), bf16[4,32,1152]{2,1,0:T(8,128)(2,1)S(1)}, u32[]{:S(2)}, u32[]{:S(2)}) async-start(bf16[4,32,1152]{2,1,0:T(8,128)(2,1)} %pad_maximum_fusion), calls=%async_computation.3 | async-start | bytes 589824 | tf_op jit(solution)/shard_map/all_to_all | solution.py:418
  56.1 0.0 copy-done.1
  56.1 0.1 fusion.5
  56.3 5.8 %backward.1 = bf16[1,512,1024]{2,1,0:T(8,128)(2,1)} custom-call(bf16[8,32,1152]{2,1,0:T(8,128)(2,1)S(1)} %all-to-all-done.2.parts_ref, f32[32,1024]{1,0:T(8,128)S(1)} %get-tuple-element.13.pooled_ref, bf16[512,1024]{1,0:T(8,128)(2,1)S(1)} %get-tuple-element.14.slope_ref, s32[1,1,32]{2,1,0:T(1,128)} %lengths_hbm.3, bf16[1,512,1024]{2,1,0:T(8,128)(2,1)} %tokens_hbm.3, ...), custom_call_target="tpu_custom_call" | custom-call | flops 1073741824 | bytes 5242880 | tf_op jit(solution)/shard_map/backward/pallas_call | solution.py:420
  62.1 2.2 %all-to-all-done.3 = bf16[4,32,1152]{2,1,0:T(8,128)(2,1)S(1)} async-done(((bf16[4,32,1152]{2,1,0:T(8,128)(2,1)}), bf16[4,32,1152]{2,1,0:T(8,128)(2,1)S(1)}, u32[]{:S(2)}, u32[]{:S(2)}) %all-to-all-start.3) | async-done | bytes 294944 | tf_op jit(solution)/shard_map/all_to_all | solution.py:418
  64.3 0.1 add_add_fusion
  64.4 0.6 broadcast_in_dim.22
  65.0 15.2 %all-to-all-start.4 = ((f32[16,8,128]{2,1,0:T(8,128)}), f32[16,8,128]{2,1,0:T(8,128)S(1)}, u32[]{:S(2)}, u32[]{:S(2)}) async-start(f32[16,8,128]{2,1,0:T(8,128)} %broadcast_in_dim.22), calls=%async_computation.4 | async-start | bytes 131072 | tf_op jit(solution)/shard_map/all_to_all | solution.py:444
  80.2 0.2 fusion.2
  80.4 0.7 fusion.4
  81.1 7.3 %all-to-all-done.4 = f32[16,8,128]{2,1,0:T(8,128)S(1)} async-done(((f32[16,8,128]{2,1,0:T(8,128)}), f32[16,8,128]{2,1,0:T(8,128)S(1)}, u32[]{:S(2)}, u32[]{:S(2)}) %all-to-all-start.4) | async-done | bytes 65568 | tf_op jit(solution)/shard_map/all_to_all | solution.py:444
  88.4 0.6 fusion.9
  (8 shorter events, 0.1 us)
Async XLA Ops:
  2.2 16.4 %all-to-all-start.1 = ((bf16[4,32,1024]{2,1,0:T(8,128)(2,1)}), bf16[4,32,1024]{2,1,0:T(8,128)(2,1)S(1)}, u32[]{:S(2)}, u32[]{:S(2)}) async-start(bf16[4,32,1024]{2,1,0:T(8,128)(2,1)} %broadcast_in_dim.19), calls=%async_computation.1 | async-start | bytes 524288 | tf_op jit(solution)/shard_map/all_to_all | solution.py:345
  18.6 13.1 %all-to-all-start = ((bf16[8,32,1152]{2,1,0:T(8,128)(2,1)}), bf16[8,32,1152]{2,1,0:T(8,128)(2,1)S(1)}, u32[]{:S(2)}, u32[]{:S(2)}) async-start(bf16[8,32,1152]{2,1,0:T(8,128)(2,1)} %get-tuple-element.11), calls=%async_computation | async-start | bytes 1179648 | tf_op jit(solution)/shard_map/all_to_all | solution.py:376
  23.8 7.4 %collective-permute-start = (bf16[4,32,1024]{2,1,0:T(8,128)(2,1)S(1)}, bf16[4,32,1024]{2,1,0:T(8,128)(2,1)S(1)}, u32[]{:S(2)}, u32[]{:S(2)}) collective-permute-start(bf16[4,32,1024]{2,1,0:T(8,128)(2,1)S(1)} %all-to-all-done.1.near_ref), channel_id=1, source_target_pairs={{0,64},{64,0},{1,65},{65,1},{2,66},{66,2},{3,67},{67,3},{4,68},{68... | collective-permute-start | bytes 786440 | tf_op jit(solution)/shard_map/ppermute | solution.py:342
  28.3 27.9 %copy-start.1 = (bf16[1,32,1024]{2,1,0:T(8,128)(2,1)S(1)}, bf16[1,32,1024]{2,1,0:T(8,128)(2,1)}, u32[]{:S(2)}) copy-start(bf16[1,32,1024]{2,1,0:T(8,128)(2,1)} %param.13) | copy-start | bytes 196612
  31.7 0.8 copy-start
  36.0 12.6 %all-to-all-start.2 = ((bf16[8,32,1152]{2,1,0:T(8,128)(2,1)}), bf16[8,32,1152]{2,1,0:T(8,128)(2,1)S(1)}, u32[]{:S(2)}, u32[]{:S(2)}) async-start(bf16[8,32,1152]{2,1,0:T(8,128)(2,1)} %get-tuple-element.12), calls=%async_computation.2 | async-start | bytes 1179648 | tf_op jit(solution)/shard_map/all_to_all | solution.py:403
  40.7 7.3 %collective-permute-start.1 = (bf16[4,32,1024]{2,1,0:T(8,128)(2,1)}, bf16[4,32,1024]{2,1,0:T(8,128)(2,1)S(1)}, u32[]{:S(2)}, u32[]{:S(2)}) collective-permute-start(bf16[4,32,1024]{2,1,0:T(8,128)(2,1)} %get-tuple-element.16), channel_id=1, source_target_pairs={{0,64},{64,0},{1,65},{65,1},{2,66},{66,2},{3,67},{67,3},{4,68},{68... | collective-permute-start | bytes 786440 | tf_op jit(solution)/shard_map/ppermute | solution.py:342
  49.5 14.7 %all-to-all-start.3 = ((bf16[4,32,1152]{2,1,0:T(8,128)(2,1)}), bf16[4,32,1152]{2,1,0:T(8,128)(2,1)S(1)}, u32[]{:S(2)}, u32[]{:S(2)}) async-start(bf16[4,32,1152]{2,1,0:T(8,128)(2,1)} %pad_maximum_fusion), calls=%async_computation.3 | async-start | bytes 589824 | tf_op jit(solution)/shard_map/all_to_all | solution.py:418
  65.0 23.4 %all-to-all-start.4 = ((f32[16,8,128]{2,1,0:T(8,128)}), f32[16,8,128]{2,1,0:T(8,128)S(1)}, u32[]{:S(2)}, u32[]{:S(2)}) async-start(f32[16,8,128]{2,1,0:T(8,128)} %broadcast_in_dim.22), calls=%async_computation.4 | async-start | bytes 131072 | tf_op jit(solution)/shard_map/all_to_all | solution.py:444

commit v3 on v2

--- a/solution.py
+++ b/solution.py
@@ -155,16 +155,14 @@
     inv_count,
     scalars_ref,
     place_ref,
-    sketch_hbm,
+    sketch_ref,
     near_ref,
     other_ref,
     back_hbm,
     near_out_ref,
     other_out_hbm,
-    sketch_ref,
     back_ref,
     other_out_ref,
-    in_sem,
     out_sems,
 ):
     members, sketches = sketch_ref.shape[:2]
@@ -172,8 +170,6 @@
     halves = 2
     rows, half = members * sketches, far * sketches
     texts = halves * half
-    sketch_copy = pltpu.make_async_copy(sketch_hbm, sketch_ref, in_sem)
-    sketch_copy.start()
     temper = jnp.exp(jnp.full((1, 1), scalars_ref[0], F32))
     column = lax.broadcasted_iota(jnp.int32, (1, texts), 1)
     first = jnp.zeros((1, texts), jnp.int32)
@@ -185,7 +181,6 @@
     ).astype(F32)
     text_rnorm = lax.rsqrt(jnp.sum(text_in * text_in, axis=-1, keepdims=True) + EPSILON)
     text = (text_in * text_rnorm).astype(BF16)
-    sketch_copy.wait()
     sketch = sketch_ref[:, :, :features].reshape(rows, features)
     extra = sketch_ref[:, :, features:].reshape(rows, LANES).astype(F32)
     paired = extra[:, 0:1] * 16.0 + extra[:, 1:2]
@@ -226,9 +221,9 @@
 
 
 def backward_kernel(
-    parts_ref,
     pooled_ref,
     slope_ref,
+    parts_ref,
     lengths_hbm,
     tokens_hbm,
     gain_hbm,
@@ -324,6 +319,18 @@
         copy.wait()
 
 
+def text_grad_kernel(parts_ref, text_hbm, out_ref, text_ref, text_sem):
+    copy = pltpu.make_async_copy(text_hbm.at[0], text_ref, text_sem)
+    copy.start()
+    text_grad = jnp.sum(parts_ref[:, :, : text_ref.shape[1]].astype(F32), axis=0)
+    copy.wait()
+    text_in = text_ref[...].astype(F32)
+    rnorm = lax.rsqrt(jnp.sum(text_in * text_in, axis=-1, keepdims=True) + EPSILON)
+    unit = text_in * rnorm
+    along = jnp.sum(unit * text_grad, axis=-1, keepdims=True)
+    out_ref[0] = rnorm * (text_grad - unit * along)
+
+
 def on_device(cycle_size, cycles, tokens, norm_gain, proj_weight, text_feats, lengths, positives, sample_weight, log_temp, logit_bias, loss_scale):
     tok_count, depth = tokens.shape[1:]
     features = proj_weight.shape[1]
@@ -345,7 +352,7 @@
     near_texts = lax.all_to_all(text_send, "far", 0, 0, tiled=True)
 
     gain, weights = norm_gain.reshape(1, depth), proj_weight
-    token_parts, weight_parts = 4, 4
+    token_parts, weight_parts = 4, 1
     sketch_send, slope, pooled = pl.pallas_call(
         forward_kernel,
         out_shape=(
@@ -388,18 +395,16 @@
             pltpu.VMEM((far, sketches, features), F32),
             pltpu.HBM((far, sketches, features), BF16),
         ),
-        in_specs=[SMEM, SMEM, HBM, VMEM, VMEM],
+        in_specs=[SMEM, SMEM, VMEM, VMEM, VMEM],
         out_specs=(HBM, VMEM, HBM),
         scratch_shapes=[
             pltpu.VMEM((members, sketches, wide), BF16),
-            pltpu.VMEM((members, sketches, wide), BF16),
             pltpu.VMEM((far, sketches, features), BF16),
-            pltpu.SemaphoreType.DMA,
             pltpu.SemaphoreType.DMA((2,)),
         ],
         compiler_params=params(),
         name="score",
-    )(scalars, place, *in_hbm(sketch_all), *in_vmem(near_texts, other_texts))
+    )(scalars, place, *in_vmem(sketch_all, near_texts, other_texts))
     sketch_back = lax.all_to_all(sketch_parts, "col", 0, 0, tiled=True)
     text_sum = (near_part + partner(other_part).astype(F32)).astype(BF16)
 
@@ -438,18 +443,20 @@
         compiler_params=params(),
         cost_estimate=pl.CostEstimate(flops=2 * tok_count * depth * features, bytes_accessed=5 << 20, transcendentals=0),
         name="backward",
-    )(sketch_back, *in_vmem(pooled, slope), *in_hbm(lengths, tokens, gain, weights))
-
+    )(*in_vmem(pooled, slope, sketch_back), *in_hbm(lengths, tokens, gain, weights))
     sums_send = jnp.broadcast_to(jnp.pad(lane_sums(text_back), (0, LANES - 3)), (near * cycles, 8, LANES))
+    sums_send, grad_tokens = lax.optimization_barrier((sums_send, grad_tokens))
     sums_all = lax.all_to_all(sums_send, ("near", "group"), 0, 0, tiled=True)
     sums = jnp.sum(sums_all[:, 0, :3], axis=0)
 
-    text_grad = jnp.sum(text_back[:, :, :features].astype(F32), axis=0, keepdims=True)
-    text_in = text_feats.astype(F32)
-    rnorm = lax.rsqrt(jnp.sum(text_in * text_in, axis=-1, keepdims=True) + EPSILON)
-    unit = text_in * rnorm
-    along = jnp.sum(unit * text_grad, axis=-1, keepdims=True)
-    grad_texts = rnorm * (text_grad - unit * along)
+    grad_texts = pl.pallas_call(
+        text_grad_kernel,
+        out_shape=pltpu.HBM(text_feats.shape, F32),
+        in_specs=[VMEM, HBM],
+        out_specs=VMEM,
+        scratch_shapes=[pltpu.VMEM((sketches, features), BF16), pltpu.SemaphoreType.DMA],
+        name="text_grad",
+    )(text_back, *in_hbm(text_feats))
     return (grad_tokens, grad_texts, sums[0], sums[1], sums[2])
 
 

time: 89.7 us -> 87.8 us (0.979)
  waiting for transfers between devices: 20.1 us -> 21.7 us
  Pallas kernels: 16.2 us -> 14.7 us
  other arithmetic: 2.31 us -> 1.23 us
    pallas_call x0 -> x1, Pallas kernels: none -> 2.66 us  [on_device(): pl.pallas_call(text_grad_kernel, out_shape=pltpu.HBM(text_feats.shape, F3...]
    all_to_all x1, waiting for transfers between devices: 7.25 us -> 5.56 us  [on_device(): sums_all = lax.all_to_all(sums_send, ('near', 'group'), 0, 0, tiled=True)]
    all_to_all x1, waiting for transfers between devices: 1.85 us -> 3.51 us  [on_device(): near_texts = lax.all_to_all(text_send, 'far', 0, 0, tiled=True)]
    pallas_call x1, Pallas kernels: 6.87 us -> 5.21 us  [on_device(): pl.pallas_call(forward_kernel, out_shape=(pltpu.HBM((members, sketches, w...]
    all_to_all x1, waiting for transfers between devices: 2.17 us -> 3.72 us  [on_device(): text_back = lax.all_to_all(text_parts, 'far', 0, 0, tiled=True)]
    pallas_call x1, Pallas kernels: 5.79 us -> 4.4 us  [on_device(): pl.pallas_call(backward_kernel, out_shape=pltpu.HBM(tokens.shape, BF16),...]
    pallas_call x1, Pallas kernels: 3.49 us -> 2.48 us  [on_device(): pl.pallas_call(functools.partial(score_kernel, inv_count), out_shape=(plt...]
  transfers between devices with their start and end apart: 7 -> 7, of which waited for: 7 -> 7; matrix products, arithmetic and copies ran while one was open for 1% -> 0% of each run, Pallas kernels for 14% -> 14%
where the time goes in v3:
time: 87.8 us; the launch traced here: 87.1 us
  starting transfers between devices  43.9 us (50%)
  waiting for transfers between devices  21.7 us (25%)
  Pallas kernels  14.7 us (17%)
  local copies, waits for them, and re-layouts  2.89 us (3%)
  between operations  2.68 us (3%)
  other arithmetic  1.23 us (1%)
    all_to_all x1, starting transfers between devices, on_device(): sums_all = lax.all_to_all(sums_send, ('near', 'group'), 0, 0, tiled=True)  15 us
    ppermute x2, waiting for transfers between devices, partner(): lax.ppermute(block, 'near', [(i, (i + 1) % near) for i in range(near)])  7.87 us
    all_to_all x1, starting transfers between devices, on_device(): near_texts = lax.all_to_all(text_send, 'far', 0, 0, tiled=True)  7.64 us
    all_to_all x1, starting transfers between devices, on_device(): text_back = lax.all_to_all(text_parts, 'far', 0, 0, tiled=True)  6.65 us
    all_to_all x1, waiting for transfers between devices, on_device(): sums_all = lax.all_to_all(sums_send, ('near', 'group'), 0, 0, tiled=True)  5.56 us
    all_to_all x1, starting transfers between devices, on_device(): sketch_all = lax.all_to_all(sketch_send, 'col', 0, 0, tiled=True)  5.23 us
    pallas_call x1, Pallas kernels, on_device(): pl.pallas_call(forward_kernel, out_shape=(pltpu.HBM((members, sketches, w...  5.21 us
    ppermute x2, starting transfers between devices, partner(): lax.ppermute(block, 'near', [(i, (i + 1) % near) for i in range(near)])  4.69 us
  transfers between devices with their start and end apart: 7, of which 7 were waited for; matrix products, arithmetic and copies ran while one was open for 0% of the time, Pallas kernels for 14%

profile of v3, /device:TPU:1, one launch (start us, length us, event | category | flops | bytes accessed | tf_op | source)
XLA Modules:
  0.0 87.1 jit_solution(14710166565088720883)
XLA Ops:
  0.6 1.6 %broadcast_in_dim.14 = bf16[4,32,1024]{2,1,0:T(8,128)(2,1)} broadcast(bf16[32,1024]{1,0:T(8,128)(2,1)} %bitcast.19), dimensions={1,2} | broadcast | bytes 327680 | tf_op jit(solution)/shard_map/broadcast_in_dim | solution.py:351
  2.2 7.6 %all-to-all-start.1 = ((bf16[4,32,1024]{2,1,0:T(8,128)(2,1)}), bf16[4,32,1024]{2,1,0:T(8,128)(2,1)S(1)}, u32[]{:S(2)}, u32[]{:S(2)}) async-start(bf16[4,32,1024]{2,1,0:T(8,128)(2,1)} %broadcast_in_dim.14), calls=%async_computation.1 | async-start | bytes 524288 | tf_op jit(solution)/shard_map/all_to_all | solution.py:352
  9.8 5.2 %forward.1 = (bf16[8,32,1152]{2,1,0:T(8,128)(2,1)}, bf16[512,1024]{1,0:T(8,128)(2,1)S(1)}, f32[32,1024]{1,0:T(8,128)S(1)}) custom-call(bf16[1,512,1024]{2,1,0:T(8,128)(2,1)} %tokens_hbm.3, f32[1,1024]{1,0:T(1,128)} %bitcast.20, bf16[1024,1024]{1,0:T(8,128)(2,1)} %weight_hbm.3, s32[1,1,32]{2,1,0:T(1,128)} %lengths_hbm.3, s32[1,32]{1,0:T(1,128)} %positives_hbm.1, ...), custom_call_target="tpu_custom_call" | custom-call | flops 1073741824 | bytes 5242880 | tf_op jit(solution)/shard_map/forward/pallas_call | solution.py:356
  15.1 3.5 %all-to-all-done.1.near_ref = bf16[4,32,1024]{2,1,0:T(8,128)(2,1)S(1)} async-done(((bf16[4,32,1024]{2,1,0:T(8,128)(2,1)}), bf16[4,32,1024]{2,1,0:T(8,128)(2,1)S(1)}, u32[]{:S(2)}, u32[]{:S(2)}) %all-to-all-start.1) | async-done | bytes 262176 | tf_op jit(solution)/shard_map/all_to_all | solution.py:352
  18.6 5.2 %all-to-all-start = ((bf16[8,32,1152]{2,1,0:T(8,128)(2,1)}), bf16[8,32,1152]{2,1,0:T(8,128)(2,1)S(1)}, u32[]{:S(2)}, u32[]{:S(2)}) async-start(bf16[8,32,1152]{2,1,0:T(8,128)(2,1)} %get-tuple-element.13), calls=%async_computation | async-start | bytes 1179648 | tf_op jit(solution)/shard_map/all_to_all | solution.py:383
  23.8 2.3 %collective-permute-start = (bf16[4,32,1024]{2,1,0:T(8,128)(2,1)S(1)}, bf16[4,32,1024]{2,1,0:T(8,128)(2,1)S(1)}, u32[]{:S(2)}, u32[]{:S(2)}) collective-permute-start(bf16[4,32,1024]{2,1,0:T(8,128)(2,1)S(1)} %all-to-all-done.1.near_ref), channel_id=1, source_target_pairs={{0,64},{64,0},{1,65},{65,1},{2,66},{66,2},{3,67},{67,3},{4,68},{68... | collective-permute-start | bytes 786440 | tf_op jit(solution)/shard_map/ppermute | solution.py:349
  28.1 0.1 stack.51.place_ref
  28.2 0.1 pad_maximum_fusion.1.scalars_ref
  28.3 2.9 %collective-permute-done.other_ref = bf16[4,32,1024]{2,1,0:T(8,128)(2,1)S(1)} collective-permute-done((bf16[4,32,1024]{2,1,0:T(8,128)(2,1)S(1)}, bf16[4,32,1024]{2,1,0:T(8,128)(2,1)S(1)}, u32[]{:S(2)}, u32[]{:S(2)}) %collective-permute-start) | collective-permute-done | bytes 262176 | tf_op jit(solution)/shard_map/ppermute | solution.py:349
  31.2 0.5 all-to-all-done.sketch_ref
  31.7 2.5 %score.1 = (bf16[8,32,1152]{2,1,0:T(8,128)(2,1)}, f32[4,32,1024]{2,1,0:T(8,128)S(1)}, bf16[4,32,1024]{2,1,0:T(8,128)(2,1)}) custom-call(f32[3]{0:T(128)S(1)} %pad_maximum_fusion.1.scalars_ref, s32[8]{0:T(128)S(1)} %stack.51.place_ref, bf16[8,32,1152]{2,1,0:T(8,128)(2,1)S(1)} %all-to-all-done.sketch_ref, bf16[4,32,1024]{2,1,0:T(8,128)(2,1)S(1)} %all-to-all-done.1.near_ref, ...), custom_call_target="tpu_custom_call" | custom-call | tf_op jit(solution)/shard_map/score/pallas_call | solution.py:391
  34.2 4.7 %all-to-all-start.2 = ((bf16[8,32,1152]{2,1,0:T(8,128)(2,1)}), bf16[8,32,1152]{2,1,0:T(8,128)(2,1)S(1)}, u32[]{:S(2)}, u32[]{:S(2)}) async-start(bf16[8,32,1152]{2,1,0:T(8,128)(2,1)} %get-tuple-element.16), calls=%async_computation.2 | async-start | bytes 1179648 | tf_op jit(solution)/shard_map/all_to_all | solution.py:408
  38.8 2.3 %collective-permute-start.1 = (bf16[4,32,1024]{2,1,0:T(8,128)(2,1)}, bf16[4,32,1024]{2,1,0:T(8,128)(2,1)S(1)}, u32[]{:S(2)}, u32[]{:S(2)}) collective-permute-start(bf16[4,32,1024]{2,1,0:T(8,128)(2,1)} %get-tuple-element.15), channel_id=1, source_target_pairs={{0,64},{64,0},{1,65},{65,1},{2,66},{66,2},{3,67},{67,3},{4,68},{68... | collective-permute-start | bytes 786440 | tf_op jit(solution)/shard_map/ppermute | solution.py:349
  41.2 5.0 %collective-permute-done.1 = bf16[4,32,1024]{2,1,0:T(8,128)(2,1)S(1)} collective-permute-done((bf16[4,32,1024]{2,1,0:T(8,128)(2,1)}, bf16[4,32,1024]{2,1,0:T(8,128)(2,1)S(1)}, u32[]{:S(2)}, u32[]{:S(2)}) %collective-permute-start.1) | collective-permute-done | bytes 262176 | tf_op jit(solution)/shard_map/ppermute | solution.py:349
  46.2 0.1 add_convert_fusion
  46.2 0.5 all-to-all-done.2.parts_ref
  46.8 0.1 reduce-precision_convert_fusion.1
  46.8 0.1 select_maximum_fusion
  46.9 0.8 pad_maximum_fusion
  47.7 6.7 %all-to-all-start.3 = ((bf16[4,32,1152]{2,1,0:T(8,128)(2,1)}), bf16[4,32,1152]{2,1,0:T(8,128)(2,1)S(1)}, u32[]{:S(2)}, u32[]{:S(2)}) async-start(bf16[4,32,1152]{2,1,0:T(8,128)(2,1)} %pad_maximum_fusion), calls=%async_computation.3 | async-start | bytes 589824 | tf_op jit(solution)/shard_map/all_to_all | solution.py:423
  54.4 4.4 %backward.1 = bf16[1,512,1024]{2,1,0:T(8,128)(2,1)} custom-call(f32[32,1024]{1,0:T(8,128)S(1)} %get-tuple-element.17.pooled_ref, bf16[512,1024]{1,0:T(8,128)(2,1)S(1)} %get-tuple-element.18.slope_ref, bf16[8,32,1152]{2,1,0:T(8,128)(2,1)S(1)} %all-to-all-done.2.parts_ref, s32[1,1,32]{2,1,0:T(1,128)} %lengths_hbm.3, bf16[1,512,1024]{2,1,0:T(8,128)(2,1)} %tokens_hbm.3, ...), custom_call_target="tpu_custom_call" | custom-call | flops 1073741824 | bytes 5242880 | tf_op jit(solution)/shard_map/backward/pallas_call | solution.py:425
  58.8 3.7 %all-to-all-done.3.parts_ref = bf16[4,32,1152]{2,1,0:T(8,128)(2,1)S(1)} async-done(((bf16[4,32,1152]{2,1,0:T(8,128)(2,1)}), bf16[4,32,1152]{2,1,0:T(8,128)(2,1)S(1)}, u32[]{:S(2)}, u32[]{:S(2)}) %all-to-all-start.3) | async-done | bytes 294944 | tf_op jit(solution)/shard_map/all_to_all | solution.py:423
  62.5 0.0 copy-start
  62.5 0.1 add_add_fusion
  62.6 0.6 broadcast_in_dim.16
  63.2 15.0 %all-to-all-start.4 = ((f32[16,8,128]{2,1,0:T(8,128)}), f32[16,8,128]{2,1,0:T(8,128)S(1)}, u32[]{:S(2)}, u32[]{:S(2)}) async-start(f32[16,8,128]{2,1,0:T(8,128)} %broadcast_in_dim.16), calls=%async_computation.4 | async-start | bytes 131072 | tf_op jit(solution)/shard_map/all_to_all | solution.py:449
  78.3 0.0 copy-done
  78.3 2.7 %text_grad.1 = f32[1,32,1024]{2,1,0:T(8,128)} custom-call(bf16[4,32,1152]{2,1,0:T(8,128)(2,1)} %copy-done, bf16[1,32,1024]{2,1,0:T(8,128)(2,1)} %text_hbm.1), custom_call_target="tpu_custom_call" | custom-call | tf_op jit(solution)/shard_map/text_grad/pallas_call | solution.py:452
  80.9 5.6 %all-to-all-done.4 = f32[16,8,128]{2,1,0:T(8,128)S(1)} async-done(((f32[16,8,128]{2,1,0:T(8,128)}), f32[16,8,128]{2,1,0:T(8,128)S(1)}, u32[]{:S(2)}, u32[]{:S(2)}) %all-to-all-start.4) | async-done | bytes 65568 | tf_op jit(solution)/shard_map/all_to_all | solution.py:449
  86.5 0.6 fusion.3
  (6 shorter events, 0.1 us)
Async XLA Ops:
  2.2 16.4 %all-to-all-start.1 = ((bf16[4,32,1024]{2,1,0:T(8,128)(2,1)}), bf16[4,32,1024]{2,1,0:T(8,128)(2,1)S(1)}, u32[]{:S(2)}, u32[]{:S(2)}) async-start(bf16[4,32,1024]{2,1,0:T(8,128)(2,1)} %broadcast_in_dim.14), calls=%async_computation.1 | async-start | bytes 524288 | tf_op jit(solution)/shard_map/all_to_all | solution.py:352
  18.6 13.1 %all-to-all-start = ((bf16[8,32,1152]{2,1,0:T(8,128)(2,1)}), bf16[8,32,1152]{2,1,0:T(8,128)(2,1)S(1)}, u32[]{:S(2)}, u32[]{:S(2)}) async-start(bf16[8,32,1152]{2,1,0:T(8,128)(2,1)} %get-tuple-element.13), calls=%async_computation | async-start | bytes 1179648 | tf_op jit(solution)/shard_map/all_to_all | solution.py:383
  23.8 7.4 %collective-permute-start = (bf16[4,32,1024]{2,1,0:T(8,128)(2,1)S(1)}, bf16[4,32,1024]{2,1,0:T(8,128)(2,1)S(1)}, u32[]{:S(2)}, u32[]{:S(2)}) collective-permute-start(bf16[4,32,1024]{2,1,0:T(8,128)(2,1)S(1)} %all-to-all-done.1.near_ref), channel_id=1, source_target_pairs={{0,64},{64,0},{1,65},{65,1},{2,66},{66,2},{3,67},{67,3},{4,68},{68... | collective-permute-start | bytes 786440 | tf_op jit(solution)/shard_map/ppermute | solution.py:349
  34.2 12.6 %all-to-all-start.2 = ((bf16[8,32,1152]{2,1,0:T(8,128)(2,1)}), bf16[8,32,1152]{2,1,0:T(8,128)(2,1)S(1)}, u32[]{:S(2)}, u32[]{:S(2)}) async-start(bf16[8,32,1152]{2,1,0:T(8,128)(2,1)} %get-tuple-element.16), calls=%async_computation.2 | async-start | bytes 1179648 | tf_op jit(solution)/shard_map/all_to_all | solution.py:408
  38.8 7.3 %collective-permute-start.1 = (bf16[4,32,1024]{2,1,0:T(8,128)(2,1)}, bf16[4,32,1024]{2,1,0:T(8,128)(2,1)S(1)}, u32[]{:S(2)}, u32[]{:S(2)}) collective-permute-start(bf16[4,32,1024]{2,1,0:T(8,128)(2,1)} %get-tuple-element.15), channel_id=1, source_target_pairs={{0,64},{64,0},{1,65},{65,1},{2,66},{66,2},{3,67},{67,3},{4,68},{68... | collective-permute-start | bytes 786440 | tf_op jit(solution)/shard_map/ppermute | solution.py:349
  47.7 14.8 %all-to-all-start.3 = ((bf16[4,32,1152]{2,1,0:T(8,128)(2,1)}), bf16[4,32,1152]{2,1,0:T(8,128)(2,1)S(1)}, u32[]{:S(2)}, u32[]{:S(2)}) async-start(bf16[4,32,1152]{2,1,0:T(8,128)(2,1)} %pad_maximum_fusion), calls=%async_computation.3 | async-start | bytes 589824 | tf_op jit(solution)/shard_map/all_to_all | solution.py:423
  62.5 15.8 %copy-start = (bf16[4,32,1152]{2,1,0:T(8,128)(2,1)}, bf16[4,32,1152]{2,1,0:T(8,128)(2,1)S(1)}, u32[]{:S(2)}) copy-start(bf16[4,32,1152]{2,1,0:T(8,128)(2,1)S(1)} %all-to-all-done.3.parts_ref) | copy-start | bytes 884740
  63.2 23.3 %all-to-all-start.4 = ((f32[16,8,128]{2,1,0:T(8,128)}), f32[16,8,128]{2,1,0:T(8,128)S(1)}, u32[]{:S(2)}, u32[]{:S(2)}) async-start(f32[16,8,128]{2,1,0:T(8,128)} %broadcast_in_dim.16), calls=%async_computation.4 | async-start | bytes 131072 | tf_op jit(solution)/shard_map/all_to_all | solution.py:449

commit v4 on v3

--- a/solution.py
+++ b/solution.py
@@ -45,7 +45,7 @@
     positives_hbm,
     sample_hbm,
     send_hbm,
-    slope_ref,
+    preact_ref,
     pooled_ref,
     tokens_ref,
     gain_ref,
@@ -122,12 +122,8 @@
         values = jnp.dot(normed_ref[...], weight_ref[:, columns], preferred_element_type=F32)
         square = values * values
         tanh_part = jnp.tanh(values * (GELU_SCALE + (GELU_SCALE * GELU_CUBE) * square))
-        half = 0.5 + 0.5 * tanh_part
-        activated = (values * half).astype(BF16)
-        slope = half + values * (1.0 - tanh_part * tanh_part) * (
-            0.5 * GELU_SCALE + (1.5 * GELU_SCALE * GELU_CUBE) * square
-        )
-        slope_ref[:, columns] = slope.astype(BF16)
+        activated = (values * (0.5 + 0.5 * tanh_part)).astype(BF16)
+        preact_ref[:, columns] = values.astype(BF16)
         pooled_ref[:, columns] = jnp.dot(membership, activated, preferred_element_type=F32) / lens_col
 
     pooled = pooled_ref[...]
@@ -222,7 +218,7 @@
 
 def backward_kernel(
     pooled_ref,
-    slope_ref,
+    preact_ref,
     parts_ref,
     lengths_hbm,
     tokens_hbm,
@@ -243,7 +239,7 @@
 ):
     sketches = lengths_ref.shape[-1]
     tok_count, depth = tokens_ref.shape
-    features = slope_ref.shape[1]
+    features = preact_ref.shape[1]
     token_parts, weight_parts = token_sems.shape[0], weight_sems.shape[0]
     block, width = tok_count // token_parts, depth // weight_parts
 
@@ -289,7 +285,13 @@
     membership = jnp.concatenate([membership, membership], axis=1)
     for i in range(token_parts):
         per_token = jnp.dot(membership[i * block : (i + 1) * block], both, preferred_element_type=F32)
-        act_ref[rows(i)] = (per_token * slope_ref[rows(i)].astype(F32)).astype(BF16)
+        values = preact_ref[rows(i)].astype(F32)
+        square = values * values
+        tanh_part = jnp.tanh(values * (GELU_SCALE + (GELU_SCALE * GELU_CUBE) * square))
+        slope = (0.5 + 0.5 * tanh_part) + values * (1.0 - tanh_part * tanh_part) * (
+            0.5 * GELU_SCALE + (1.5 * GELU_SCALE * GELU_CUBE) * square
+        )
+        act_ref[rows(i)] = (per_token * slope).astype(BF16)
 
     for copy in token_copies:
         copy.wait()
@@ -353,7 +355,7 @@
 
     gain, weights = norm_gain.reshape(1, depth), proj_weight
     token_parts, weight_parts = 4, 1
-    sketch_send, slope, pooled = pl.pallas_call(
+    sketch_send, preact, pooled = pl.pallas_call(
         forward_kernel,
         out_shape=(
             pltpu.HBM((members, sketches, wide), BF16),
@@ -385,7 +387,7 @@
 
     far_place, near_place, col = lax.axis_index("far"), lax.axis_index("near"), lax.axis_index("col")
     place = jnp.stack(
-        [(f * near + (near_place + h) % near) * members + col for h in range(near) for f in range(far)]
+        [(f * members + col) * near + (near_place + h) % near for h in range(near) for f in range(far)]
     ).astype(jnp.int32)
     scalars = jnp.stack([log_temp, logit_bias, loss_scale])
     sketch_parts, near_part, other_part = pl.pallas_call(
@@ -443,7 +445,7 @@
         compiler_params=params(),
         cost_estimate=pl.CostEstimate(flops=2 * tok_count * depth * features, bytes_accessed=5 << 20, transcendentals=0),
         name="backward",
-    )(*in_vmem(pooled, slope, sketch_back), *in_hbm(lengths, tokens, gain, weights))
+    )(*in_vmem(pooled, preact, sketch_back), *in_hbm(lengths, tokens, gain, weights))
     sums_send = jnp.broadcast_to(jnp.pad(lane_sums(text_back), (0, LANES - 3)), (near * cycles, 8, LANES))
     sums_send, grad_tokens = lax.optimization_barrier((sums_send, grad_tokens))
     sums_all = lax.all_to_all(sums_send, ("near", "group"), 0, 0, tiled=True)
@@ -464,9 +466,9 @@
     cycle_size, cycles = mesh.shape["blk"], mesh.shape["group"]
     far, near = 4, 2
     tiles = jax.sharding.Mesh(
-        mesh.devices.reshape(far, near, cycle_size // (far * near), cycles), ("far", "near", "col", "group")
+        mesh.devices.reshape(far, cycle_size // (far * near), near, cycles), ("far", "col", "near", "group")
     )
-    blk = ("far", "near", "col")
+    blk = ("far", "col", "near")
     placed = (
         P("group", blk, None),
         P(),

time: 87.8 us -> 86.9 us (0.990)
  waiting for transfers between devices: 21.7 us -> 19.3 us
  starting transfers between devices: 43.9 us -> 45.6 us
    ppermute x2, starting transfers between devices: 4.69 us -> 7.34 us  [partner(): lax.ppermute(block, 'near', [(i, (i + 1) % near) for i in range(near)])]
    ppermute x2, waiting for transfers between devices: 7.87 us -> 5.87 us  [partner(): lax.ppermute(block, 'near', [(i, (i + 1) % near) for i in range(near)])]
    all_to_all x1, starting transfers between devices: 5.23 us -> 3.59 us  [on_device(): sketch_all = lax.all_to_all(sketch_send, 'col', 0, 0, tiled=True)]
  transfers between devices with their start and end apart: 7 -> 7, of which waited for: 7 -> 5; matrix products, arithmetic and copies ran while one was open for 0% -> 0% of each run, Pallas kernels for 14% -> 14%
where the time goes in v4:
time: 86.9 us; the launch traced here: 86.1 us
  starting transfers between devices  45.6 us (52%)
  waiting for transfers between devices  19.3 us (22%)
  Pallas kernels  14.5 us (17%)
  local copies, waits for them, and re-layouts  2.89 us (3%)
  between operations  2.68 us (3%)
  other arithmetic  1.24 us (1%)
    all_to_all x1, starting transfers between devices, on_device(): sums_all = lax.all_to_all(sums_send, ('near', 'group'), 0, 0, tiled=True)  14.9 us
    all_to_all x1, starting transfers between devices, on_device(): near_texts = lax.all_to_all(text_send, 'far', 0, 0, tiled=True)  7.64 us
    ppermute x2, starting transfers between devices, partner(): lax.ppermute(block, 'near', [(i, (i + 1) % near) for i in range(near)])  7.34 us
    all_to_all x1, starting transfers between devices, on_device(): text_back = lax.all_to_all(text_parts, 'far', 0, 0, tiled=True)  6.97 us
    ppermute x2, waiting for transfers between devices, partner(): lax.ppermute(block, 'near', [(i, (i + 1) % near) for i in range(near)])  5.87 us
    all_to_all x1, starting transfers between devices, on_device(): sketch_back = lax.all_to_all(sketch_parts, 'col', 0, 0, tiled=True)  5.16 us
    all_to_all x1, waiting for transfers between devices, on_device(): sums_all = lax.all_to_all(sums_send, ('near', 'group'), 0, 0, tiled=True)  5.14 us
    pallas_call x1, Pallas kernels, on_device(): pl.pallas_call(forward_kernel, out_shape=(pltpu.HBM((members, sketches, w...  4.75 us
  transfers between devices with their start and end apart: 7, of which 5 were waited for; matrix products, arithmetic and copies ran while one was open for 0% of the time, Pallas kernels for 14%

profile of v4, /device:TPU:1, one launch (start us, length us, event | category | flops | bytes accessed | tf_op | source)
XLA Modules:
  0.0 86.1 jit_solution(2390053198129872578)
XLA Ops:
  0.6 1.6 %broadcast_in_dim.14 = bf16[4,32,1024]{2,1,0:T(8,128)(2,1)} broadcast(bf16[32,1024]{1,0:T(8,128)(2,1)} %bitcast.19), dimensions={1,2} | broadcast | bytes 327680 | tf_op jit(solution)/shard_map/broadcast_in_dim | solution.py:353
  2.2 7.6 %all-to-all-start.1 = ((bf16[4,32,1024]{2,1,0:T(8,128)(2,1)}), bf16[4,32,1024]{2,1,0:T(8,128)(2,1)S(1)}, u32[]{:S(2)}, u32[]{:S(2)}) async-start(bf16[4,32,1024]{2,1,0:T(8,128)(2,1)} %broadcast_in_dim.14), calls=%async_computation.1 | async-start | bytes 524288 | tf_op jit(solution)/shard_map/all_to_all | solution.py:354
  9.8 4.8 %forward.1 = (bf16[8,32,1152]{2,1,0:T(8,128)(2,1)}, bf16[512,1024]{1,0:T(8,128)(2,1)S(1)}, f32[32,1024]{1,0:T(8,128)S(1)}) custom-call(bf16[1,512,1024]{2,1,0:T(8,128)(2,1)} %tokens_hbm.3, f32[1,1024]{1,0:T(1,128)} %bitcast.20, bf16[1024,1024]{1,0:T(8,128)(2,1)} %weight_hbm.3, s32[1,1,32]{2,1,0:T(1,128)} %lengths_hbm.3, s32[1,32]{1,0:T(1,128)} %positives_hbm.1, ...), custom_call_target="tpu_custom_call" | custom-call | flops 1073741824 | bytes 5242880 | tf_op jit(solution)/shard_map/forward/pallas_call | solution.py:358
  14.6 4.0 %all-to-all-done.1.near_ref = bf16[4,32,1024]{2,1,0:T(8,128)(2,1)S(1)} async-done(((bf16[4,32,1024]{2,1,0:T(8,128)(2,1)}), bf16[4,32,1024]{2,1,0:T(8,128)(2,1)S(1)}, u32[]{:S(2)}, u32[]{:S(2)}) %all-to-all-start.1) | async-done | bytes 262176 | tf_op jit(solution)/shard_map/all_to_all | solution.py:354
  18.6 3.6 %all-to-all-start = ((bf16[8,32,1152]{2,1,0:T(8,128)(2,1)}), bf16[8,32,1152]{2,1,0:T(8,128)(2,1)S(1)}, u32[]{:S(2)}, u32[]{:S(2)}) async-start(bf16[8,32,1152]{2,1,0:T(8,128)(2,1)} %get-tuple-element.13), calls=%async_computation | async-start | bytes 1179648 | tf_op jit(solution)/shard_map/all_to_all | solution.py:385
  22.2 4.0 %collective-permute-start = (bf16[4,32,1024]{2,1,0:T(8,128)(2,1)S(1)}, bf16[4,32,1024]{2,1,0:T(8,128)(2,1)S(1)}, u32[]{:S(2)}, u32[]{:S(2)}) collective-permute-start(bf16[4,32,1024]{2,1,0:T(8,128)(2,1)S(1)} %all-to-all-done.1.near_ref), channel_id=1, source_target_pairs={{0,8},{8,0},{1,9},{9,1},{2,10},{10,2},{3,11},{11,3},{4,12},{12,4},... | collective-permute-start | bytes 786440 | tf_op jit(solution)/shard_map/ppermute | solution.py:351
  28.1 0.1 stack.51.place_ref
  28.2 0.1 pad_maximum_fusion.1.scalars_ref
  28.3 1.9 %collective-permute-done.other_ref = bf16[4,32,1024]{2,1,0:T(8,128)(2,1)S(1)} collective-permute-done((bf16[4,32,1024]{2,1,0:T(8,128)(2,1)S(1)}, bf16[4,32,1024]{2,1,0:T(8,128)(2,1)S(1)}, u32[]{:S(2)}, u32[]{:S(2)}) %collective-permute-start) | collective-permute-done | bytes 262176 | tf_op jit(solution)/shard_map/ppermute | solution.py:351
  30.2 0.0 all-to-all-done.sketch_ref
  30.2 2.5 %score.1 = (bf16[8,32,1152]{2,1,0:T(8,128)(2,1)}, f32[4,32,1024]{2,1,0:T(8,128)S(1)}, bf16[4,32,1024]{2,1,0:T(8,128)(2,1)}) custom-call(f32[3]{0:T(128)S(1)} %pad_maximum_fusion.1.scalars_ref, s32[8]{0:T(128)S(1)} %stack.51.place_ref, bf16[8,32,1152]{2,1,0:T(8,128)(2,1)S(1)} %all-to-all-done.sketch_ref, bf16[4,32,1024]{2,1,0:T(8,128)(2,1)S(1)} %all-to-all-done.1.near_ref, ...), custom_call_target="tpu_custom_call" | custom-call | tf_op jit(solution)/shard_map/score/pallas_call | solution.py:393
  32.7 5.2 %all-to-all-start.2 = ((bf16[8,32,1152]{2,1,0:T(8,128)(2,1)}), bf16[8,32,1152]{2,1,0:T(8,128)(2,1)S(1)}, u32[]{:S(2)}, u32[]{:S(2)}) async-start(bf16[8,32,1152]{2,1,0:T(8,128)(2,1)} %get-tuple-element.16), calls=%async_computation.2 | async-start | bytes 1179648 | tf_op jit(solution)/shard_map/all_to_all | solution.py:410
  37.8 3.3 %collective-permute-start.1 = (bf16[4,32,1024]{2,1,0:T(8,128)(2,1)}, bf16[4,32,1024]{2,1,0:T(8,128)(2,1)S(1)}, u32[]{:S(2)}, u32[]{:S(2)}) collective-permute-start(bf16[4,32,1024]{2,1,0:T(8,128)(2,1)} %get-tuple-element.15), channel_id=1, source_target_pairs={{0,8},{8,0},{1,9},{9,1},{2,10},{10,2},{3,11},{11,3},{4,12},{12,4},... | collective-permute-start | bytes 786440 | tf_op jit(solution)/shard_map/ppermute | solution.py:351
  41.2 4.0 %collective-permute-done.1 = bf16[4,32,1024]{2,1,0:T(8,128)(2,1)S(1)} collective-permute-done((bf16[4,32,1024]{2,1,0:T(8,128)(2,1)}, bf16[4,32,1024]{2,1,0:T(8,128)(2,1)S(1)}, u32[]{:S(2)}, u32[]{:S(2)}) %collective-permute-start.1) | collective-permute-done | bytes 262176 | tf_op jit(solution)/shard_map/ppermute | solution.py:351
  45.2 0.1 add_convert_fusion
  45.2 0.0 all-to-all-done.2.parts_ref
  45.3 0.1 reduce-precision_convert_fusion.1
  45.4 0.1 select_maximum_fusion
  45.4 0.8 pad_maximum_fusion
  46.2 7.0 %all-to-all-start.3 = ((bf16[4,32,1152]{2,1,0:T(8,128)(2,1)}), bf16[4,32,1152]{2,1,0:T(8,128)(2,1)S(1)}, u32[]{:S(2)}, u32[]{:S(2)}) async-start(bf16[4,32,1152]{2,1,0:T(8,128)(2,1)} %pad_maximum_fusion), calls=%async_computation.3 | async-start | bytes 589824 | tf_op jit(solution)/shard_map/all_to_all | solution.py:425
  53.2 4.6 %backward.1 = bf16[1,512,1024]{2,1,0:T(8,128)(2,1)} custom-call(f32[32,1024]{1,0:T(8,128)S(1)} %get-tuple-element.17.pooled_ref, bf16[512,1024]{1,0:T(8,128)(2,1)S(1)} %get-tuple-element.18.preact_ref, bf16[8,32,1152]{2,1,0:T(8,128)(2,1)S(1)} %all-to-all-done.2.parts_ref, s32[1,1,32]{2,1,0:T(1,128)} %lengths_hbm.3, bf16[1,512,1024]{2,1,0:T(8,128)(2,1)} %tokens_hbm.3, ...), custom_call_target="tpu_custom_call" | custom-call | flops 1073741824 | bytes 5242880 | tf_op jit(solution)/shard_map/backward/pallas_call | solution.py:427
  57.8 4.3 %all-to-all-done.3.parts_ref = bf16[4,32,1152]{2,1,0:T(8,128)(2,1)S(1)} async-done(((bf16[4,32,1152]{2,1,0:T(8,128)(2,1)}), bf16[4,32,1152]{2,1,0:T(8,128)(2,1)S(1)}, u32[]{:S(2)}, u32[]{:S(2)}) %all-to-all-start.3) | async-done | bytes 294944 | tf_op jit(solution)/shard_map/all_to_all | solution.py:425
  62.1 0.0 copy-start
  62.1 0.1 add_add_fusion
  62.2 0.6 broadcast_in_dim.16
  62.8 14.9 %all-to-all-start.4 = ((f32[16,8,128]{2,1,0:T(8,128)}), f32[16,8,128]{2,1,0:T(8,128)S(1)}, u32[]{:S(2)}, u32[]{:S(2)}) async-start(f32[16,8,128]{2,1,0:T(8,128)} %broadcast_in_dim.16), calls=%async_computation.4 | async-start | bytes 131072 | tf_op jit(solution)/shard_map/all_to_all | solution.py:451
  77.7 0.0 copy-done
  77.7 2.7 %text_grad.1 = f32[1,32,1024]{2,1,0:T(8,128)} custom-call(bf16[4,32,1152]{2,1,0:T(8,128)(2,1)} %copy-done, bf16[1,32,1024]{2,1,0:T(8,128)(2,1)} %text_hbm.1), custom_call_target="tpu_custom_call" | custom-call | tf_op jit(solution)/shard_map/text_grad/pallas_call | solution.py:454
  80.4 5.1 %all-to-all-done.4 = f32[16,8,128]{2,1,0:T(8,128)S(1)} async-done(((f32[16,8,128]{2,1,0:T(8,128)}), f32[16,8,128]{2,1,0:T(8,128)S(1)}, u32[]{:S(2)}, u32[]{:S(2)}) %all-to-all-start.4) | async-done | bytes 65568 | tf_op jit(solution)/shard_map/all_to_all | solution.py:451
  85.5 0.6 fusion.3
  (6 shorter events, 0.1 us)
Async XLA Ops:
  2.2 16.4 %all-to-all-start.1 = ((bf16[4,32,1024]{2,1,0:T(8,128)(2,1)}), bf16[4,32,1024]{2,1,0:T(8,128)(2,1)S(1)}, u32[]{:S(2)}, u32[]{:S(2)}) async-start(bf16[4,32,1024]{2,1,0:T(8,128)(2,1)} %broadcast_in_dim.14), calls=%async_computation.1 | async-start | bytes 524288 | tf_op jit(solution)/shard_map/all_to_all | solution.py:354
  18.6 11.6 %all-to-all-start = ((bf16[8,32,1152]{2,1,0:T(8,128)(2,1)}), bf16[8,32,1152]{2,1,0:T(8,128)(2,1)S(1)}, u32[]{:S(2)}, u32[]{:S(2)}) async-start(bf16[8,32,1152]{2,1,0:T(8,128)(2,1)} %get-tuple-element.13), calls=%async_computation | async-start | bytes 1179648 | tf_op jit(solution)/shard_map/all_to_all | solution.py:385
  22.2 8.0 %collective-permute-start = (bf16[4,32,1024]{2,1,0:T(8,128)(2,1)S(1)}, bf16[4,32,1024]{2,1,0:T(8,128)(2,1)S(1)}, u32[]{:S(2)}, u32[]{:S(2)}) collective-permute-start(bf16[4,32,1024]{2,1,0:T(8,128)(2,1)S(1)} %all-to-all-done.1.near_ref), channel_id=1, source_target_pairs={{0,8},{8,0},{1,9},{9,1},{2,10},{10,2},{3,11},{11,3},{4,12},{12,4},... | collective-permute-start | bytes 786440 | tf_op jit(solution)/shard_map/ppermute | solution.py:351
  32.7 12.5 %all-to-all-start.2 = ((bf16[8,32,1152]{2,1,0:T(8,128)(2,1)}), bf16[8,32,1152]{2,1,0:T(8,128)(2,1)S(1)}, u32[]{:S(2)}, u32[]{:S(2)}) async-start(bf16[8,32,1152]{2,1,0:T(8,128)(2,1)} %get-tuple-element.16), calls=%async_computation.2 | async-start | bytes 1179648 | tf_op jit(solution)/shard_map/all_to_all | solution.py:410
  37.8 7.3 %collective-permute-start.1 = (bf16[4,32,1024]{2,1,0:T(8,128)(2,1)}, bf16[4,32,1024]{2,1,0:T(8,128)(2,1)S(1)}, u32[]{:S(2)}, u32[]{:S(2)}) collective-permute-start(bf16[4,32,1024]{2,1,0:T(8,128)(2,1)} %get-tuple-element.15), channel_id=1, source_target_pairs={{0,8},{8,0},{1,9},{9,1},{2,10},{10,2},{3,11},{11,3},{4,12},{12,4},... | collective-permute-start | bytes 786440 | tf_op jit(solution)/shard_map/ppermute | solution.py:351
  46.2 15.9 %all-to-all-start.3 = ((bf16[4,32,1152]{2,1,0:T(8,128)(2,1)}), bf16[4,32,1152]{2,1,0:T(8,128)(2,1)S(1)}, u32[]{:S(2)}, u32[]{:S(2)}) async-start(bf16[4,32,1152]{2,1,0:T(8,128)(2,1)} %pad_maximum_fusion), calls=%async_computation.3 | async-start | bytes 589824 | tf_op jit(solution)/shard_map/all_to_all | solution.py:425
  62.1 15.6 %copy-start = (bf16[4,32,1152]{2,1,0:T(8,128)(2,1)}, bf16[4,32,1152]{2,1,0:T(8,128)(2,1)S(1)}, u32[]{:S(2)}) copy-start(bf16[4,32,1152]{2,1,0:T(8,128)(2,1)S(1)} %all-to-all-done.3.parts_ref) | copy-start | bytes 884740
  62.8 22.7 %all-to-all-start.4 = ((f32[16,8,128]{2,1,0:T(8,128)}), f32[16,8,128]{2,1,0:T(8,128)S(1)}, u32[]{:S(2)}, u32[]{:S(2)}) async-start(f32[16,8,128]{2,1,0:T(8,128)} %broadcast_in_dim.16), calls=%async_computation.4 | async-start | bytes 131072 | tf_op jit(solution)/shard_map/all_to_all | solution.py:451

commit v5 on v4

--- a/solution.py
+++ b/solution.py
@@ -156,9 +156,8 @@
     other_ref,
     back_hbm,
     near_out_ref,
-    other_out_hbm,
+    other_out_ref,
     back_ref,
-    other_out_ref,
     out_sems,
 ):
     members, sketches = sketch_ref.shape[:2]
@@ -192,6 +191,10 @@
     scaled = (coeffs * (temper * scalars_ref[2])).astype(BF16)
     sketch_part = jnp.dot(scaled, text, preferred_element_type=F32).astype(BF16)
     back_ref[:, :, :features] = sketch_part.reshape(members, sketches, features)
+    main = (slice(None), slice(None), pl.ds(0, features))
+    lanes = (slice(None), slice(None), pl.ds(features, LANES))
+    main_copy = pltpu.make_async_copy(back_ref.at[main], back_hbm.at[main], out_sems.at[0])
+    main_copy.start()
     pair_loss = jnp.maximum(against, 0.0) + jnp.log1p(decay)
 
     def total(values):
@@ -205,15 +208,13 @@
     sums = sums.astype(BF16)
     for member in range(members):
         back_ref[member, :, features:] = sums
-    back_copy = pltpu.make_async_copy(back_ref, back_hbm, out_sems.at[0])
-    back_copy.start()
+    lanes_copy = pltpu.make_async_copy(back_ref.at[lanes], back_hbm.at[lanes], out_sems.at[1])
+    lanes_copy.start()
     text_part = lax.dot_general(scaled, sketch, (((0,), (0,)), ((), ())), preferred_element_type=F32)
+    near_out_ref[...] = text_part[:half].reshape(far, sketches, features)
     other_out_ref[...] = text_part[half:].astype(BF16).reshape(far, sketches, features)
-    other_out_copy = pltpu.make_async_copy(other_out_ref, other_out_hbm, out_sems.at[1])
-    other_out_copy.start()
-    near_out_ref[...] = text_part[:half].reshape(far, sketches, features)
-    back_copy.wait()
-    other_out_copy.wait()
+    main_copy.wait()
+    lanes_copy.wait()
 
 
 def backward_kernel(
@@ -395,13 +396,12 @@
         out_shape=(
             pltpu.HBM((members, sketches, wide), BF16),
             pltpu.VMEM((far, sketches, features), F32),
-            pltpu.HBM((far, sketches, features), BF16),
+            pltpu.VMEM((far, sketches, features), BF16),
         ),
         in_specs=[SMEM, SMEM, VMEM, VMEM, VMEM],
-        out_specs=(HBM, VMEM, HBM),
+        out_specs=(HBM, VMEM, VMEM),
         scratch_shapes=[
             pltpu.VMEM((members, sketches, wide), BF16),
-            pltpu.VMEM((far, sketches, features), BF16),
             pltpu.SemaphoreType.DMA((2,)),
         ],
         compiler_params=params(),

time: 86.9 us -> 86.7 us (level)
  transfers between devices with their start and end apart: 7 -> 7, of which waited for: 5 -> 6; matrix products, arithmetic and copies ran while one was open for 0% -> 0% of each run, Pallas kernels for 14% -> 14%
where the time goes in v5:
time: 86.7 us; the launch traced here: 86 us
  starting transfers between devices  45.5 us (52%)
  waiting for transfers between devices  19.3 us (22%)
  Pallas kernels  14.4 us (17%)
  local copies, waits for them, and re-layouts  2.89 us (3%)
  between operations  2.67 us (3%)
  other arithmetic  1.24 us (1%)
    all_to_all x1, starting transfers between devices, on_device(): sums_all = lax.all_to_all(sums_send, ('near', 'group'), 0, 0, tiled=True)  15 us
    all_to_all x1, starting transfers between devices, on_device(): near_texts = lax.all_to_all(text_send, 'far', 0, 0, tiled=True)  7.64 us
    ppermute x2, starting transfers between devices, partner(): lax.ppermute(block, 'near', [(i, (i + 1) % near) for i in range(near)])  7.34 us
    all_to_all x1, starting transfers between devices, on_device(): text_back = lax.all_to_all(text_parts, 'far', 0, 0, tiled=True)  6.77 us
    ppermute x2, waiting for transfers between devices, partner(): lax.ppermute(block, 'near', [(i, (i + 1) % near) for i in range(near)])  5.66 us
    all_to_all x1, starting transfers between devices, on_device(): sketch_back = lax.all_to_all(sketch_parts, 'col', 0, 0, tiled=True)  5.16 us
    all_to_all x1, waiting for transfers between devices, on_device(): sums_all = lax.all_to_all(sums_send, ('near', 'group'), 0, 0, tiled=True)  5.14 us
    pallas_call x1, Pallas kernels, on_device(): pl.pallas_call(forward_kernel, out_shape=(pltpu.HBM((members, sketches, w...  4.75 us
  transfers between devices with their start and end apart: 7, of which 6 were waited for; matrix products, arithmetic and copies ran while one was open for 0% of the time, Pallas kernels for 14%

profile of v5, /device:TPU:1, one launch (start us, length us, event | category | flops | bytes accessed | tf_op | source)
XLA Modules:
  0.0 86.0 jit_solution(5985974974122062664)
XLA Ops:
  0.6 1.6 %broadcast_in_dim.14 = bf16[4,32,1024]{2,1,0:T(8,128)(2,1)} broadcast(bf16[32,1024]{1,0:T(8,128)(2,1)} %bitcast.19), dimensions={1,2} | broadcast | bytes 327680 | tf_op jit(solution)/shard_map/broadcast_in_dim | solution.py:354
  2.2 7.6 %all-to-all-start.1 = ((bf16[4,32,1024]{2,1,0:T(8,128)(2,1)}), bf16[4,32,1024]{2,1,0:T(8,128)(2,1)S(1)}, u32[]{:S(2)}, u32[]{:S(2)}) async-start(bf16[4,32,1024]{2,1,0:T(8,128)(2,1)} %broadcast_in_dim.14), calls=%async_computation.1 | async-start | bytes 524288 | tf_op jit(solution)/shard_map/all_to_all | solution.py:355
  9.8 4.8 %forward.1 = (bf16[8,32,1152]{2,1,0:T(8,128)(2,1)}, bf16[512,1024]{1,0:T(8,128)(2,1)S(1)}, f32[32,1024]{1,0:T(8,128)S(1)}) custom-call(bf16[1,512,1024]{2,1,0:T(8,128)(2,1)} %tokens_hbm.3, f32[1,1024]{1,0:T(1,128)} %bitcast.20, bf16[1024,1024]{1,0:T(8,128)(2,1)} %weight_hbm.3, s32[1,1,32]{2,1,0:T(1,128)} %lengths_hbm.3, s32[1,32]{1,0:T(1,128)} %positives_hbm.1, ...), custom_call_target="tpu_custom_call" | custom-call | flops 1073741824 | bytes 5242880 | tf_op jit(solution)/shard_map/forward/pallas_call | solution.py:359
  14.6 4.0 %all-to-all-done.1.near_ref = bf16[4,32,1024]{2,1,0:T(8,128)(2,1)S(1)} async-done(((bf16[4,32,1024]{2,1,0:T(8,128)(2,1)}), bf16[4,32,1024]{2,1,0:T(8,128)(2,1)S(1)}, u32[]{:S(2)}, u32[]{:S(2)}) %all-to-all-start.1) | async-done | bytes 262176 | tf_op jit(solution)/shard_map/all_to_all | solution.py:355
  18.6 3.6 %all-to-all-start = ((bf16[8,32,1152]{2,1,0:T(8,128)(2,1)}), bf16[8,32,1152]{2,1,0:T(8,128)(2,1)S(1)}, u32[]{:S(2)}, u32[]{:S(2)}) async-start(bf16[8,32,1152]{2,1,0:T(8,128)(2,1)} %get-tuple-element.13), calls=%async_computation | async-start | bytes 1179648 | tf_op jit(solution)/shard_map/all_to_all | solution.py:386
  22.2 4.0 %collective-permute-start = (bf16[4,32,1024]{2,1,0:T(8,128)(2,1)S(1)}, bf16[4,32,1024]{2,1,0:T(8,128)(2,1)S(1)}, u32[]{:S(2)}, u32[]{:S(2)}) collective-permute-start(bf16[4,32,1024]{2,1,0:T(8,128)(2,1)S(1)} %all-to-all-done.1.near_ref), channel_id=1, source_target_pairs={{0,8},{8,0},{1,9},{9,1},{2,10},{10,2},{3,11},{11,3},{4,12},{12,4},... | collective-permute-start | bytes 786440 | tf_op jit(solution)/shard_map/ppermute | solution.py:352
  28.1 0.1 stack.51.place_ref
  28.2 0.1 pad_maximum_fusion.1.scalars_ref
  28.3 1.9 %collective-permute-done.other_ref = bf16[4,32,1024]{2,1,0:T(8,128)(2,1)S(1)} collective-permute-done((bf16[4,32,1024]{2,1,0:T(8,128)(2,1)S(1)}, bf16[4,32,1024]{2,1,0:T(8,128)(2,1)S(1)}, u32[]{:S(2)}, u32[]{:S(2)}) %collective-permute-start) | collective-permute-done | bytes 262176 | tf_op jit(solution)/shard_map/ppermute | solution.py:352
  30.2 0.0 all-to-all-done.sketch_ref
  30.2 2.4 %score.1 = (bf16[8,32,1152]{2,1,0:T(8,128)(2,1)}, f32[4,32,1024]{2,1,0:T(8,128)S(1)}, bf16[4,32,1024]{2,1,0:T(8,128)(2,1)S(1)}) custom-call(f32[3]{0:T(128)S(1)} %pad_maximum_fusion.1.scalars_ref, s32[8]{0:T(128)S(1)} %stack.51.place_ref, bf16[8,32,1152]{2,1,0:T(8,128)(2,1)S(1)} %all-to-all-done.sketch_ref, ...), custom_call_target="tpu_custom_call" | custom-call | tf_op jit(solution)/shard_map/score/pallas_call | solution.py:394
  32.6 5.2 %all-to-all-start.2 = ((bf16[8,32,1152]{2,1,0:T(8,128)(2,1)}), bf16[8,32,1152]{2,1,0:T(8,128)(2,1)S(1)}, u32[]{:S(2)}, u32[]{:S(2)}) async-start(bf16[8,32,1152]{2,1,0:T(8,128)(2,1)} %get-tuple-element.16), calls=%async_computation.2 | async-start | bytes 1179648 | tf_op jit(solution)/shard_map/all_to_all | solution.py:410
  37.8 3.3 %collective-permute-start.1 = (bf16[4,32,1024]{2,1,0:T(8,128)(2,1)S(1)}, bf16[4,32,1024]{2,1,0:T(8,128)(2,1)S(1)}, u32[]{:S(2)}, u32[]{:S(2)}) collective-permute-start(bf16[4,32,1024]{2,1,0:T(8,128)(2,1)S(1)} %get-tuple-element.15), channel_id=1, source_target_pairs={{0,8},{8,0},{1,9},{9,1},{2,10},{10,2},{3,11},{11,3},{4,12},{12,4},... | collective-permute-start | bytes 786440 | tf_op jit(solution)/shard_map/ppermute | solution.py:352
  41.1 3.7 %collective-permute-done.1 = bf16[4,32,1024]{2,1,0:T(8,128)(2,1)S(1)} collective-permute-done((bf16[4,32,1024]{2,1,0:T(8,128)(2,1)S(1)}, bf16[4,32,1024]{2,1,0:T(8,128)(2,1)S(1)}, u32[]{:S(2)}, u32[]{:S(2)}) %collective-permute-start.1) | collective-permute-done | bytes 262176 | tf_op jit(solution)/shard_map/ppermute | solution.py:352
  44.9 0.1 add_convert_fusion
  44.9 0.2 all-to-all-done.2.parts_ref
  45.2 0.1 reduce-precision_convert_fusion.1
  45.3 0.1 select_maximum_fusion
  45.3 0.8 pad_maximum_fusion
  46.1 6.8 %all-to-all-start.3 = ((bf16[4,32,1152]{2,1,0:T(8,128)(2,1)}), bf16[4,32,1152]{2,1,0:T(8,128)(2,1)S(1)}, u32[]{:S(2)}, u32[]{:S(2)}) async-start(bf16[4,32,1152]{2,1,0:T(8,128)(2,1)} %pad_maximum_fusion), calls=%async_computation.3 | async-start | bytes 589824 | tf_op jit(solution)/shard_map/all_to_all | solution.py:425
  52.9 4.6 %backward.1 = bf16[1,512,1024]{2,1,0:T(8,128)(2,1)} custom-call(f32[32,1024]{1,0:T(8,128)S(1)} %get-tuple-element.17.pooled_ref, bf16[512,1024]{1,0:T(8,128)(2,1)S(1)} %get-tuple-element.18.preact_ref, bf16[8,32,1152]{2,1,0:T(8,128)(2,1)S(1)} %all-to-all-done.2.parts_ref, s32[1,1,32]{2,1,0:T(1,128)} %lengths_hbm.3, bf16[1,512,1024]{2,1,0:T(8,128)(2,1)} %tokens_hbm.3, ...), custom_call_target="tpu_custom_call" | custom-call | flops 1073741824 | bytes 5242880 | tf_op jit(solution)/shard_map/backward/pallas_call | solution.py:427
  57.5 4.3 %all-to-all-done.3.parts_ref = bf16[4,32,1152]{2,1,0:T(8,128)(2,1)S(1)} async-done(((bf16[4,32,1152]{2,1,0:T(8,128)(2,1)}), bf16[4,32,1152]{2,1,0:T(8,128)(2,1)S(1)}, u32[]{:S(2)}, u32[]{:S(2)}) %all-to-all-start.3) | async-done | bytes 294944 | tf_op jit(solution)/shard_map/all_to_all | solution.py:425
  61.8 0.0 copy-start
  61.8 0.1 add_add_fusion
  61.9 0.6 broadcast_in_dim.16
  62.5 15.0 %all-to-all-start.4 = ((f32[16,8,128]{2,1,0:T(8,128)}), f32[16,8,128]{2,1,0:T(8,128)S(1)}, u32[]{:S(2)}, u32[]{:S(2)}) async-start(f32[16,8,128]{2,1,0:T(8,128)} %broadcast_in_dim.16), calls=%async_computation.4 | async-start | bytes 131072 | tf_op jit(solution)/shard_map/all_to_all | solution.py:451
  77.5 0.0 copy-done
  77.5 2.7 %text_grad.1 = f32[1,32,1024]{2,1,0:T(8,128)} custom-call(bf16[4,32,1152]{2,1,0:T(8,128)(2,1)} %copy-done, bf16[1,32,1024]{2,1,0:T(8,128)(2,1)} %text_hbm.1), custom_call_target="tpu_custom_call" | custom-call | tf_op jit(solution)/shard_map/text_grad/pallas_call | solution.py:454
  80.2 5.1 %all-to-all-done.4 = f32[16,8,128]{2,1,0:T(8,128)S(1)} async-done(((f32[16,8,128]{2,1,0:T(8,128)}), f32[16,8,128]{2,1,0:T(8,128)S(1)}, u32[]{:S(2)}, u32[]{:S(2)}) %all-to-all-start.4) | async-done | bytes 65568 | tf_op jit(solution)/shard_map/all_to_all | solution.py:451
  85.4 0.6 fusion.3
  (6 shorter events, 0.1 us)
Async XLA Ops:
  2.2 16.4 %all-to-all-start.1 = ((bf16[4,32,1024]{2,1,0:T(8,128)(2,1)}), bf16[4,32,1024]{2,1,0:T(8,128)(2,1)S(1)}, u32[]{:S(2)}, u32[]{:S(2)}) async-start(bf16[4,32,1024]{2,1,0:T(8,128)(2,1)} %broadcast_in_dim.14), calls=%async_computation.1 | async-start | bytes 524288 | tf_op jit(solution)/shard_map/all_to_all | solution.py:355
  18.6 11.6 %all-to-all-start = ((bf16[8,32,1152]{2,1,0:T(8,128)(2,1)}), bf16[8,32,1152]{2,1,0:T(8,128)(2,1)S(1)}, u32[]{:S(2)}, u32[]{:S(2)}) async-start(bf16[8,32,1152]{2,1,0:T(8,128)(2,1)} %get-tuple-element.13), calls=%async_computation | async-start | bytes 1179648 | tf_op jit(solution)/shard_map/all_to_all | solution.py:386
  22.2 8.0 %collective-permute-start = (bf16[4,32,1024]{2,1,0:T(8,128)(2,1)S(1)}, bf16[4,32,1024]{2,1,0:T(8,128)(2,1)S(1)}, u32[]{:S(2)}, u32[]{:S(2)}) collective-permute-start(bf16[4,32,1024]{2,1,0:T(8,128)(2,1)S(1)} %all-to-all-done.1.near_ref), channel_id=1, source_target_pairs={{0,8},{8,0},{1,9},{9,1},{2,10},{10,2},{3,11},{11,3},{4,12},{12,4},... | collective-permute-start | bytes 786440 | tf_op jit(solution)/shard_map/ppermute | solution.py:352
  32.6 12.5 %all-to-all-start.2 = ((bf16[8,32,1152]{2,1,0:T(8,128)(2,1)}), bf16[8,32,1152]{2,1,0:T(8,128)(2,1)S(1)}, u32[]{:S(2)}, u32[]{:S(2)}) async-start(bf16[8,32,1152]{2,1,0:T(8,128)(2,1)} %get-tuple-element.16), calls=%async_computation.2 | async-start | bytes 1179648 | tf_op jit(solution)/shard_map/all_to_all | solution.py:410
  37.8 7.1 %collective-permute-start.1 = (bf16[4,32,1024]{2,1,0:T(8,128)(2,1)S(1)}, bf16[4,32,1024]{2,1,0:T(8,128)(2,1)S(1)}, u32[]{:S(2)}, u32[]{:S(2)}) collective-permute-start(bf16[4,32,1024]{2,1,0:T(8,128)(2,1)S(1)} %get-tuple-element.15), channel_id=1, source_target_pairs={{0,8},{8,0},{1,9},{9,1},{2,10},{10,2},{3,11},{11,3},{4,12},{12,4},... | collective-permute-start | bytes 786440 | tf_op jit(solution)/shard_map/ppermute | solution.py:352
  46.1 15.7 %all-to-all-start.3 = ((bf16[4,32,1152]{2,1,0:T(8,128)(2,1)}), bf16[4,32,1152]{2,1,0:T(8,128)(2,1)S(1)}, u32[]{:S(2)}, u32[]{:S(2)}) async-start(bf16[4,32,1152]{2,1,0:T(8,128)(2,1)} %pad_maximum_fusion), calls=%async_computation.3 | async-start | bytes 589824 | tf_op jit(solution)/shard_map/all_to_all | solution.py:425
  61.8 15.7 %copy-start = (bf16[4,32,1152]{2,1,0:T(8,128)(2,1)}, bf16[4,32,1152]{2,1,0:T(8,128)(2,1)S(1)}, u32[]{:S(2)}) copy-start(bf16[4,32,1152]{2,1,0:T(8,128)(2,1)S(1)} %all-to-all-done.3.parts_ref) | copy-start | bytes 884740
  62.5 22.8 %all-to-all-start.4 = ((f32[16,8,128]{2,1,0:T(8,128)}), f32[16,8,128]{2,1,0:T(8,128)S(1)}, u32[]{:S(2)}, u32[]{:S(2)}) async-start(f32[16,8,128]{2,1,0:T(8,128)} %broadcast_in_dim.16), calls=%async_computation.4 | async-start | bytes 131072 | tf_op jit(solution)/shard_map/all_to_all | solution.py:451

commit v6 on v5

--- a/solution.py
+++ b/solution.py
@@ -446,7 +446,7 @@
         cost_estimate=pl.CostEstimate(flops=2 * tok_count * depth * features, bytes_accessed=5 << 20, transcendentals=0),
         name="backward",
     )(*in_vmem(pooled, preact, sketch_back), *in_hbm(lengths, tokens, gain, weights))
-    sums_send = jnp.broadcast_to(jnp.pad(lane_sums(text_back), (0, LANES - 3)), (near * cycles, 8, LANES))
+    sums_send = jnp.broadcast_to(jnp.pad(lane_sums(text_back), (0, LANES - 3)), (near * cycles, 1, LANES))
     sums_send, grad_tokens = lax.optimization_barrier((sums_send, grad_tokens))
     sums_all = lax.all_to_all(sums_send, ("near", "group"), 0, 0, tiled=True)
     sums = jnp.sum(sums_all[:, 0, :3], axis=0)

time: 86.7 us -> 85.8 us (0.990)
  no operation moved by 1% of the time
where the time goes in v6:
time: 85.8 us; the launch traced here: 85.1 us
  starting transfers between devices  45.5 us (53%)
  waiting for transfers between devices  18.5 us (22%)
  Pallas kernels  14.4 us (17%)
  local copies, waits for them, and re-layouts  2.86 us (3%)
  between operations  2.67 us (3%)
  other arithmetic  1.24 us (1%)
    all_to_all x1, starting transfers between devices, on_device(): sums_all = lax.all_to_all(sums_send, ('near', 'group'), 0, 0, tiled=True)  15 us
    all_to_all x1, starting transfers between devices, on_device(): near_texts = lax.all_to_all(text_send, 'far', 0, 0, tiled=True)  7.64 us
    ppermute x2, starting transfers between devices, partner(): lax.ppermute(block, 'near', [(i, (i + 1) % near) for i in range(near)])  7.34 us
    all_to_all x1, starting transfers between devices, on_device(): text_back = lax.all_to_all(text_parts, 'far', 0, 0, tiled=True)  6.77 us
    ppermute x2, waiting for transfers between devices, partner(): lax.ppermute(block, 'near', [(i, (i + 1) % near) for i in range(near)])  5.66 us
    all_to_all x1, starting transfers between devices, on_device(): sketch_back = lax.all_to_all(sketch_parts, 'col', 0, 0, tiled=True)  5.16 us
    pallas_call x1, Pallas kernels, on_device(): pl.pallas_call(forward_kernel, out_shape=(pltpu.HBM((members, sketches, w...  4.75 us
    pallas_call x1, Pallas kernels, on_device(): pl.pallas_call(backward_kernel, out_shape=pltpu.HBM(tokens.shape, BF16),...  4.58 us
  transfers between devices with their start and end apart: 7, of which 6 were waited for; matrix products, arithmetic and copies ran while one was open for 0% of the time, Pallas kernels for 14%

profile of v6, /device:TPU:1, one launch (start us, length us, event | category | flops | bytes accessed | tf_op | source)
XLA Modules:
  0.0 85.1 jit_solution(4026111975013022284)
XLA Ops:
  0.6 1.6 %broadcast_in_dim.14 = bf16[4,32,1024]{2,1,0:T(8,128)(2,1)} broadcast(bf16[32,1024]{1,0:T(8,128)(2,1)} %bitcast.19), dimensions={1,2} | broadcast | bytes 327680 | tf_op jit(solution)/shard_map/broadcast_in_dim | solution.py:354
  2.2 7.6 %all-to-all-start.1 = ((bf16[4,32,1024]{2,1,0:T(8,128)(2,1)}), bf16[4,32,1024]{2,1,0:T(8,128)(2,1)S(1)}, u32[]{:S(2)}, u32[]{:S(2)}) async-start(bf16[4,32,1024]{2,1,0:T(8,128)(2,1)} %broadcast_in_dim.14), calls=%async_computation.1 | async-start | bytes 524288 | tf_op jit(solution)/shard_map/all_to_all | solution.py:355
  9.8 4.8 %forward.1 = (bf16[8,32,1152]{2,1,0:T(8,128)(2,1)}, bf16[512,1024]{1,0:T(8,128)(2,1)S(1)}, f32[32,1024]{1,0:T(8,128)S(1)}) custom-call(bf16[1,512,1024]{2,1,0:T(8,128)(2,1)} %tokens_hbm.3, f32[1,1024]{1,0:T(1,128)} %bitcast.20, bf16[1024,1024]{1,0:T(8,128)(2,1)} %weight_hbm.3, s32[1,1,32]{2,1,0:T(1,128)} %lengths_hbm.3, s32[1,32]{1,0:T(1,128)} %positives_hbm.1, ...), custom_call_target="tpu_custom_call" | custom-call | flops 1073741824 | bytes 5242880 | tf_op jit(solution)/shard_map/forward/pallas_call | solution.py:359
  14.6 4.0 %all-to-all-done.1.near_ref = bf16[4,32,1024]{2,1,0:T(8,128)(2,1)S(1)} async-done(((bf16[4,32,1024]{2,1,0:T(8,128)(2,1)}), bf16[4,32,1024]{2,1,0:T(8,128)(2,1)S(1)}, u32[]{:S(2)}, u32[]{:S(2)}) %all-to-all-start.1) | async-done | bytes 262176 | tf_op jit(solution)/shard_map/all_to_all | solution.py:355
  18.6 3.6 %all-to-all-start = ((bf16[8,32,1152]{2,1,0:T(8,128)(2,1)}), bf16[8,32,1152]{2,1,0:T(8,128)(2,1)S(1)}, u32[]{:S(2)}, u32[]{:S(2)}) async-start(bf16[8,32,1152]{2,1,0:T(8,128)(2,1)} %get-tuple-element.13), calls=%async_computation | async-start | bytes 1179648 | tf_op jit(solution)/shard_map/all_to_all | solution.py:386
  22.2 4.0 %collective-permute-start = (bf16[4,32,1024]{2,1,0:T(8,128)(2,1)S(1)}, bf16[4,32,1024]{2,1,0:T(8,128)(2,1)S(1)}, u32[]{:S(2)}, u32[]{:S(2)}) collective-permute-start(bf16[4,32,1024]{2,1,0:T(8,128)(2,1)S(1)} %all-to-all-done.1.near_ref), channel_id=1, source_target_pairs={{0,8},{8,0},{1,9},{9,1},{2,10},{10,2},{3,11},{11,3},{4,12},{12,4},... | collective-permute-start | bytes 786440 | tf_op jit(solution)/shard_map/ppermute | solution.py:352
  28.1 0.1 stack.51.place_ref
  28.2 0.1 pad_maximum_fusion.1.scalars_ref
  28.3 1.9 %collective-permute-done.other_ref = bf16[4,32,1024]{2,1,0:T(8,128)(2,1)S(1)} collective-permute-done((bf16[4,32,1024]{2,1,0:T(8,128)(2,1)S(1)}, bf16[4,32,1024]{2,1,0:T(8,128)(2,1)S(1)}, u32[]{:S(2)}, u32[]{:S(2)}) %collective-permute-start) | collective-permute-done | bytes 262176 | tf_op jit(solution)/shard_map/ppermute | solution.py:352
  30.2 0.0 all-to-all-done.sketch_ref
  30.2 2.4 %score.1 = (bf16[8,32,1152]{2,1,0:T(8,128)(2,1)}, f32[4,32,1024]{2,1,0:T(8,128)S(1)}, bf16[4,32,1024]{2,1,0:T(8,128)(2,1)S(1)}) custom-call(f32[3]{0:T(128)S(1)} %pad_maximum_fusion.1.scalars_ref, s32[8]{0:T(128)S(1)} %stack.51.place_ref, bf16[8,32,1152]{2,1,0:T(8,128)(2,1)S(1)} %all-to-all-done.sketch_ref, ...), custom_call_target="tpu_custom_call" | custom-call | tf_op jit(solution)/shard_map/score/pallas_call | solution.py:394
  32.6 5.2 %all-to-all-start.2 = ((bf16[8,32,1152]{2,1,0:T(8,128)(2,1)}), bf16[8,32,1152]{2,1,0:T(8,128)(2,1)S(1)}, u32[]{:S(2)}, u32[]{:S(2)}) async-start(bf16[8,32,1152]{2,1,0:T(8,128)(2,1)} %get-tuple-element.16), calls=%async_computation.2 | async-start | bytes 1179648 | tf_op jit(solution)/shard_map/all_to_all | solution.py:410
  37.8 3.3 %collective-permute-start.1 = (bf16[4,32,1024]{2,1,0:T(8,128)(2,1)S(1)}, bf16[4,32,1024]{2,1,0:T(8,128)(2,1)S(1)}, u32[]{:S(2)}, u32[]{:S(2)}) collective-permute-start(bf16[4,32,1024]{2,1,0:T(8,128)(2,1)S(1)} %get-tuple-element.15), channel_id=1, source_target_pairs={{0,8},{8,0},{1,9},{9,1},{2,10},{10,2},{3,11},{11,3},{4,12},{12,4},... | collective-permute-start | bytes 786440 | tf_op jit(solution)/shard_map/ppermute | solution.py:352
  41.1 3.7 %collective-permute-done.1 = bf16[4,32,1024]{2,1,0:T(8,128)(2,1)S(1)} collective-permute-done((bf16[4,32,1024]{2,1,0:T(8,128)(2,1)S(1)}, bf16[4,32,1024]{2,1,0:T(8,128)(2,1)S(1)}, u32[]{:S(2)}, u32[]{:S(2)}) %collective-permute-start.1) | collective-permute-done | bytes 262176 | tf_op jit(solution)/shard_map/ppermute | solution.py:352
  44.9 0.1 add_convert_fusion
  44.9 0.2 all-to-all-done.2.parts_ref
  45.2 0.1 reduce-precision_convert_fusion.1
  45.3 0.1 select_maximum_fusion
  45.3 0.8 pad_maximum_fusion
  46.1 6.8 %all-to-all-start.3 = ((bf16[4,32,1152]{2,1,0:T(8,128)(2,1)}), bf16[4,32,1152]{2,1,0:T(8,128)(2,1)S(1)}, u32[]{:S(2)}, u32[]{:S(2)}) async-start(bf16[4,32,1152]{2,1,0:T(8,128)(2,1)} %pad_maximum_fusion), calls=%async_computation.3 | async-start | bytes 589824 | tf_op jit(solution)/shard_map/all_to_all | solution.py:425
  52.9 4.6 %backward.1 = bf16[1,512,1024]{2,1,0:T(8,128)(2,1)} custom-call(f32[32,1024]{1,0:T(8,128)S(1)} %get-tuple-element.17.pooled_ref, bf16[512,1024]{1,0:T(8,128)(2,1)S(1)} %get-tuple-element.18.preact_ref, bf16[8,32,1152]{2,1,0:T(8,128)(2,1)S(1)} %all-to-all-done.2.parts_ref, s32[1,1,32]{2,1,0:T(1,128)} %lengths_hbm.3, bf16[1,512,1024]{2,1,0:T(8,128)(2,1)} %tokens_hbm.3, ...), custom_call_target="tpu_custom_call" | custom-call | flops 1073741824 | bytes 5242880 | tf_op jit(solution)/shard_map/backward/pallas_call | solution.py:427
  57.5 4.3 %all-to-all-done.3.parts_ref = bf16[4,32,1152]{2,1,0:T(8,128)(2,1)S(1)} async-done(((bf16[4,32,1152]{2,1,0:T(8,128)(2,1)}), bf16[4,32,1152]{2,1,0:T(8,128)(2,1)S(1)}, u32[]{:S(2)}, u32[]{:S(2)}) %all-to-all-start.3) | async-done | bytes 294944 | tf_op jit(solution)/shard_map/all_to_all | solution.py:425
  61.8 0.0 copy-start
  61.8 0.1 add_add_fusion
  61.9 0.6 broadcast_in_dim.16
  62.5 15.0 %all-to-all-start.4 = ((f32[16,1,128]{2,1,0:T(1,128)}), f32[16,1,128]{2,1,0:T(1,128)S(1)}, u32[]{:S(2)}, u32[]{:S(2)}) async-start(f32[16,1,128]{2,1,0:T(1,128)} %broadcast_in_dim.16), calls=%async_computation.4 | async-start | bytes 16384 | tf_op jit(solution)/shard_map/all_to_all | solution.py:451
  77.5 0.0 copy-done
  77.5 2.7 %text_grad.1 = f32[1,32,1024]{2,1,0:T(8,128)} custom-call(bf16[4,32,1152]{2,1,0:T(8,128)(2,1)} %copy-done, bf16[1,32,1024]{2,1,0:T(8,128)(2,1)} %text_hbm.1), custom_call_target="tpu_custom_call" | custom-call | tf_op jit(solution)/shard_map/text_grad/pallas_call | solution.py:454
  80.2 4.3 %all-to-all-done.4 = f32[16,1,128]{2,1,0:T(1,128)S(1)} async-done(((f32[16,1,128]{2,1,0:T(1,128)}), f32[16,1,128]{2,1,0:T(1,128)S(1)}, u32[]{:S(2)}, u32[]{:S(2)}) %all-to-all-start.4) | async-done | bytes 8224 | tf_op jit(solution)/shard_map/all_to_all | solution.py:451
  84.6 0.6 fusion.3
  (6 shorter events, 0.1 us)
Async XLA Ops:
  2.2 16.4 %all-to-all-start.1 = ((bf16[4,32,1024]{2,1,0:T(8,128)(2,1)}), bf16[4,32,1024]{2,1,0:T(8,128)(2,1)S(1)}, u32[]{:S(2)}, u32[]{:S(2)}) async-start(bf16[4,32,1024]{2,1,0:T(8,128)(2,1)} %broadcast_in_dim.14), calls=%async_computation.1 | async-start | bytes 524288 | tf_op jit(solution)/shard_map/all_to_all | solution.py:355
  18.6 11.6 %all-to-all-start = ((bf16[8,32,1152]{2,1,0:T(8,128)(2,1)}), bf16[8,32,1152]{2,1,0:T(8,128)(2,1)S(1)}, u32[]{:S(2)}, u32[]{:S(2)}) async-start(bf16[8,32,1152]{2,1,0:T(8,128)(2,1)} %get-tuple-element.13), calls=%async_computation | async-start | bytes 1179648 | tf_op jit(solution)/shard_map/all_to_all | solution.py:386
  22.2 8.0 %collective-permute-start = (bf16[4,32,1024]{2,1,0:T(8,128)(2,1)S(1)}, bf16[4,32,1024]{2,1,0:T(8,128)(2,1)S(1)}, u32[]{:S(2)}, u32[]{:S(2)}) collective-permute-start(bf16[4,32,1024]{2,1,0:T(8,128)(2,1)S(1)} %all-to-all-done.1.near_ref), channel_id=1, source_target_pairs={{0,8},{8,0},{1,9},{9,1},{2,10},{10,2},{3,11},{11,3},{4,12},{12,4},... | collective-permute-start | bytes 786440 | tf_op jit(solution)/shard_map/ppermute | solution.py:352
  32.6 12.5 %all-to-all-start.2 = ((bf16[8,32,1152]{2,1,0:T(8,128)(2,1)}), bf16[8,32,1152]{2,1,0:T(8,128)(2,1)S(1)}, u32[]{:S(2)}, u32[]{:S(2)}) async-start(bf16[8,32,1152]{2,1,0:T(8,128)(2,1)} %get-tuple-element.16), calls=%async_computation.2 | async-start | bytes 1179648 | tf_op jit(solution)/shard_map/all_to_all | solution.py:410
  37.8 7.1 %collective-permute-start.1 = (bf16[4,32,1024]{2,1,0:T(8,128)(2,1)S(1)}, bf16[4,32,1024]{2,1,0:T(8,128)(2,1)S(1)}, u32[]{:S(2)}, u32[]{:S(2)}) collective-permute-start(bf16[4,32,1024]{2,1,0:T(8,128)(2,1)S(1)} %get-tuple-element.15), channel_id=1, source_target_pairs={{0,8},{8,0},{1,9},{9,1},{2,10},{10,2},{3,11},{11,3},{4,12},{12,4},... | collective-permute-start | bytes 786440 | tf_op jit(solution)/shard_map/ppermute | solution.py:352
  46.1 15.7 %all-to-all-start.3 = ((bf16[4,32,1152]{2,1,0:T(8,128)(2,1)}), bf16[4,32,1152]{2,1,0:T(8,128)(2,1)S(1)}, u32[]{:S(2)}, u32[]{:S(2)}) async-start(bf16[4,32,1152]{2,1,0:T(8,128)(2,1)} %pad_maximum_fusion), calls=%async_computation.3 | async-start | bytes 589824 | tf_op jit(solution)/shard_map/all_to_all | solution.py:425
  61.8 15.7 %copy-start = (bf16[4,32,1152]{2,1,0:T(8,128)(2,1)}, bf16[4,32,1152]{2,1,0:T(8,128)(2,1)S(1)}, u32[]{:S(2)}) copy-start(bf16[4,32,1152]{2,1,0:T(8,128)(2,1)S(1)} %all-to-all-done.3.parts_ref) | copy-start | bytes 884740
  62.5 22.0 %all-to-all-start.4 = ((f32[16,1,128]{2,1,0:T(1,128)}), f32[16,1,128]{2,1,0:T(1,128)S(1)}, u32[]{:S(2)}, u32[]{:S(2)}) async-start(f32[16,1,128]{2,1,0:T(1,128)} %broadcast_in_dim.16), calls=%async_computation.4 | async-start | bytes 16384 | tf_op jit(solution)/shard_map/all_to_all | solution.py:451

commit v7 on v6

--- a/solution.py
+++ b/solution.py
@@ -171,11 +171,9 @@
     for i in range(halves * far):
         first = jnp.where(column >= i * sketches, (place_ref[i] - i) * sketches, first)
     column = (column + first).astype(F32)
-    text_in = jnp.concatenate(
-        [ref[...].reshape(half, features) for ref in (near_ref, other_ref)], axis=0
-    ).astype(F32)
+    text_in = other_ref[...].reshape(half, features).astype(F32)
     text_rnorm = lax.rsqrt(jnp.sum(text_in * text_in, axis=-1, keepdims=True) + EPSILON)
-    text = (text_in * text_rnorm).astype(BF16)
+    text = jnp.concatenate([near_ref[...].reshape(half, features), (text_in * text_rnorm).astype(BF16)], axis=0)
     sketch = sketch_ref[:, :, :features].reshape(rows, features)
     extra = sketch_ref[:, :, features:].reshape(rows, LANES).astype(F32)
     paired = extra[:, 0:1] * 16.0 + extra[:, 1:2]
@@ -385,6 +383,8 @@
     )(*in_hbm(tokens, gain, weights, lengths, positives, sample_weight))
     sketch_all = lax.all_to_all(sketch_send, "col", 0, 0, tiled=True)
     other_texts = partner(near_texts)
+    near_in = near_texts.astype(F32)
+    near_embed = (near_in * lax.rsqrt(jnp.sum(near_in * near_in, axis=-1, keepdims=True) + EPSILON)).astype(BF16)
 
     far_place, near_place, col = lax.axis_index("far"), lax.axis_index("near"), lax.axis_index("col")
     place = jnp.stack(
@@ -406,7 +406,7 @@
         ],
         compiler_params=params(),
         name="score",
-    )(scalars, place, *in_vmem(sketch_all, near_texts, other_texts))
+    )(scalars, place, *in_vmem(sketch_all, near_embed, other_texts))
     sketch_back = lax.all_to_all(sketch_parts, "col", 0, 0, tiled=True)
     text_sum = (near_part + partner(other_part).astype(F32)).astype(BF16)
 

time: 85.8 us -> 87.7 us (1.022)
  waiting for transfers between devices: 18.5 us -> 20.3 us
    ppermute x2, waiting for transfers between devices: 5.66 us -> 7.52 us  [partner(): lax.ppermute(block, 'near', [(i, (i + 1) % near) for i in range(near)])]
  transfers between devices with their start and end apart: 7 -> 7, of which waited for: 6 -> 6; matrix products, arithmetic and copies ran while one was open for 0% -> 1% of each run, Pallas kernels for 14% -> 14%
where the time goes in v7:
time: 87.7 us; the launch traced here: 87 us
  starting transfers between devices  45.3 us (52%)
  waiting for transfers between devices  20.3 us (23%)
  Pallas kernels  14.3 us (16%)
  local copies, waits for them, and re-layouts  2.87 us (3%)
  between operations  2.67 us (3%)
  other arithmetic  1.47 us (2%)
    all_to_all x1, starting transfers between devices, on_device(): sums_all = lax.all_to_all(sums_send, ('near', 'group'), 0, 0, tiled=True)  14.8 us
    all_to_all x1, starting transfers between devices, on_device(): near_texts = lax.all_to_all(text_send, 'far', 0, 0, tiled=True)  7.64 us
    ppermute x2, waiting for transfers between devices, partner(): lax.ppermute(block, 'near', [(i, (i + 1) % near) for i in range(near)])  7.52 us
    ppermute x2, starting transfers between devices, partner(): lax.ppermute(block, 'near', [(i, (i + 1) % near) for i in range(near)])  7.34 us
    all_to_all x1, starting transfers between devices, on_device(): text_back = lax.all_to_all(text_parts, 'far', 0, 0, tiled=True)  7.05 us
    all_to_all x1, starting transfers between devices, on_device(): sketch_back = lax.all_to_all(sketch_parts, 'col', 0, 0, tiled=True)  4.86 us
    pallas_call x1, Pallas kernels, on_device(): pl.pallas_call(forward_kernel, out_shape=(pltpu.HBM((members, sketches, w...  4.76 us
    pallas_call x1, Pallas kernels, on_device(): pl.pallas_call(backward_kernel, out_shape=pltpu.HBM(tokens.shape, BF16),...  4.59 us
  transfers between devices with their start and end apart: 7, of which 6 were waited for; matrix products, arithmetic and copies ran while one was open for 1% of the time, Pallas kernels for 14%

profile of v7, /device:TPU:1, one launch (start us, length us, event | category | flops | bytes accessed | tf_op | source)
XLA Modules:
  0.0 87.0 jit_solution(13548191538111469689)
XLA Ops:
  0.6 1.6 %broadcast_in_dim.15 = bf16[4,32,1024]{2,1,0:T(8,128)(2,1)} broadcast(bf16[32,1024]{1,0:T(8,128)(2,1)} %bitcast.19), dimensions={1,2} | broadcast | bytes 327680 | tf_op jit(solution)/shard_map/broadcast_in_dim | solution.py:352
  2.2 7.6 %all-to-all-start.1 = ((bf16[4,32,1024]{2,1,0:T(8,128)(2,1)}), bf16[4,32,1024]{2,1,0:T(8,128)(2,1)S(1)}, u32[]{:S(2)}, u32[]{:S(2)}) async-start(bf16[4,32,1024]{2,1,0:T(8,128)(2,1)} %broadcast_in_dim.15), calls=%async_computation.1 | async-start | bytes 524288 | tf_op jit(solution)/shard_map/all_to_all | solution.py:353
  9.8 4.8 %forward.1 = (bf16[8,32,1152]{2,1,0:T(8,128)(2,1)}, bf16[512,1024]{1,0:T(8,128)(2,1)S(1)}, f32[32,1024]{1,0:T(8,128)S(1)}) custom-call(bf16[1,512,1024]{2,1,0:T(8,128)(2,1)} %tokens_hbm.3, f32[1,1024]{1,0:T(1,128)} %bitcast.20, bf16[1024,1024]{1,0:T(8,128)(2,1)} %weight_hbm.3, s32[1,1,32]{2,1,0:T(1,128)} %lengths_hbm.3, s32[1,32]{1,0:T(1,128)} %positives_hbm.1, ...), custom_call_target="tpu_custom_call" | custom-call | flops 1073741824 | bytes 5242880 | tf_op jit(solution)/shard_map/forward/pallas_call | solution.py:357
  14.6 4.0 %all-to-all-done.1 = bf16[4,32,1024]{2,1,0:T(8,128)(2,1)S(1)} async-done(((bf16[4,32,1024]{2,1,0:T(8,128)(2,1)}), bf16[4,32,1024]{2,1,0:T(8,128)(2,1)S(1)}, u32[]{:S(2)}, u32[]{:S(2)}) %all-to-all-start.1) | async-done | bytes 262176 | tf_op jit(solution)/shard_map/all_to_all | solution.py:353
  18.6 3.6 %all-to-all-start = ((bf16[8,32,1152]{2,1,0:T(8,128)(2,1)}), bf16[8,32,1152]{2,1,0:T(8,128)(2,1)S(1)}, u32[]{:S(2)}, u32[]{:S(2)}) async-start(bf16[8,32,1152]{2,1,0:T(8,128)(2,1)} %get-tuple-element.13), calls=%async_computation | async-start | bytes 1179648 | tf_op jit(solution)/shard_map/all_to_all | solution.py:384
  24.1 0.1 stack.51.place_ref
  24.2 0.1 pad_maximum_fusion.1.scalars_ref
  24.3 4.0 %collective-permute-start = (bf16[4,32,1024]{2,1,0:T(8,128)(2,1)S(1)}, bf16[4,32,1024]{2,1,0:T(8,128)(2,1)S(1)}, u32[]{:S(2)}, u32[]{:S(2)}) collective-permute-start(bf16[4,32,1024]{2,1,0:T(8,128)(2,1)S(1)} %all-to-all-done.1), channel_id=1, source_target_pairs={{0,8},{8,0},{1,9},{9,1},{2,10},{10,2},{3,11},{11,3},{4,12},{12,4},... | collective-permute-start | bytes 786440 | tf_op jit(solution)/shard_map/ppermute | solution.py:350
  28.3 0.1 fusion
  28.4 0.1 fusion.1.near_ref
  28.5 3.8 %collective-permute-done.other_ref = bf16[4,32,1024]{2,1,0:T(8,128)(2,1)S(1)} collective-permute-done((bf16[4,32,1024]{2,1,0:T(8,128)(2,1)S(1)}, bf16[4,32,1024]{2,1,0:T(8,128)(2,1)S(1)}, u32[]{:S(2)}, u32[]{:S(2)}) %collective-permute-start) | collective-permute-done | bytes 262176 | tf_op jit(solution)/shard_map/ppermute | solution.py:350
  32.3 0.0 all-to-all-done.sketch_ref
  32.3 2.3 %score.1 = (bf16[8,32,1152]{2,1,0:T(8,128)(2,1)}, f32[4,32,1024]{2,1,0:T(8,128)S(1)}, bf16[4,32,1024]{2,1,0:T(8,128)(2,1)S(1)}) custom-call(f32[3]{0:T(128)S(1)} %pad_maximum_fusion.1.scalars_ref, s32[8]{0:T(128)S(1)} %stack.51.place_ref, bf16[8,32,1152]{2,1,0:T(8,128)(2,1)S(1)} %all-to-all-done.sketch_ref, bf16[4,32,1024]{2,1,0:T(8,128)(2,1)S(1)} %fusion.1.near_ref, ...), custom_call_target="tpu_custom_call" | custom-call | tf_op jit(solution)/shard_map/score/pallas_call | solution.py:394
  34.6 4.9 %all-to-all-start.2 = ((bf16[8,32,1152]{2,1,0:T(8,128)(2,1)}), bf16[8,32,1152]{2,1,0:T(8,128)(2,1)S(1)}, u32[]{:S(2)}, u32[]{:S(2)}) async-start(bf16[8,32,1152]{2,1,0:T(8,128)(2,1)} %get-tuple-element.16), calls=%async_computation.2 | async-start | bytes 1179648 | tf_op jit(solution)/shard_map/all_to_all | solution.py:410
  39.5 3.4 %collective-permute-start.1 = (bf16[4,32,1024]{2,1,0:T(8,128)(2,1)S(1)}, bf16[4,32,1024]{2,1,0:T(8,128)(2,1)S(1)}, u32[]{:S(2)}, u32[]{:S(2)}) collective-permute-start(bf16[4,32,1024]{2,1,0:T(8,128)(2,1)S(1)} %get-tuple-element.15), channel_id=1, source_target_pairs={{0,8},{8,0},{1,9},{9,1},{2,10},{10,2},{3,11},{11,3},{4,12},{12,4},... | collective-permute-start | bytes 786440 | tf_op jit(solution)/shard_map/ppermute | solution.py:350
  42.9 3.7 %collective-permute-done.1 = bf16[4,32,1024]{2,1,0:T(8,128)(2,1)S(1)} collective-permute-done((bf16[4,32,1024]{2,1,0:T(8,128)(2,1)S(1)}, bf16[4,32,1024]{2,1,0:T(8,128)(2,1)S(1)}, u32[]{:S(2)}, u32[]{:S(2)}) %collective-permute-start.1) | collective-permute-done | bytes 262176 | tf_op jit(solution)/shard_map/ppermute | solution.py:350
  46.6 0.1 add_convert_fusion
  46.7 0.2 all-to-all-done.2.parts_ref
  46.9 0.1 reduce-precision_convert_fusion.1
  47.0 0.1 select_maximum_fusion
  47.1 0.8 pad_maximum_fusion
  47.9 7.0 %all-to-all-start.3 = ((bf16[4,32,1152]{2,1,0:T(8,128)(2,1)}), bf16[4,32,1152]{2,1,0:T(8,128)(2,1)S(1)}, u32[]{:S(2)}, u32[]{:S(2)}) async-start(bf16[4,32,1152]{2,1,0:T(8,128)(2,1)} %pad_maximum_fusion), calls=%async_computation.3 | async-start | bytes 589824 | tf_op jit(solution)/shard_map/all_to_all | solution.py:425
  54.9 4.6 %backward.1 = bf16[1,512,1024]{2,1,0:T(8,128)(2,1)} custom-call(f32[32,1024]{1,0:T(8,128)S(1)} %get-tuple-element.17.pooled_ref, bf16[512,1024]{1,0:T(8,128)(2,1)S(1)} %get-tuple-element.18.preact_ref, bf16[8,32,1152]{2,1,0:T(8,128)(2,1)S(1)} %all-to-all-done.2.parts_ref, s32[1,1,32]{2,1,0:T(1,128)} %lengths_hbm.3, bf16[1,512,1024]{2,1,0:T(8,128)(2,1)} %tokens_hbm.3, ...), custom_call_target="tpu_custom_call" | custom-call | flops 1073741824 | bytes 5242880 | tf_op jit(solution)/shard_map/backward/pallas_call | solution.py:427
  59.5 4.3 %all-to-all-done.3.parts_ref = bf16[4,32,1152]{2,1,0:T(8,128)(2,1)S(1)} async-done(((bf16[4,32,1152]{2,1,0:T(8,128)(2,1)}), bf16[4,32,1152]{2,1,0:T(8,128)(2,1)S(1)}, u32[]{:S(2)}, u32[]{:S(2)}) %all-to-all-start.3) | async-done | bytes 294944 | tf_op jit(solution)/shard_map/all_to_all | solution.py:425
  63.8 0.0 copy-start
  63.8 0.1 add_add_fusion
  63.9 0.6 broadcast_in_dim.17
  64.5 14.8 %all-to-all-start.4 = ((f32[16,1,128]{2,1,0:T(1,128)}), f32[16,1,128]{2,1,0:T(1,128)S(1)}, u32[]{:S(2)}, u32[]{:S(2)}) async-start(f32[16,1,128]{2,1,0:T(1,128)} %broadcast_in_dim.17), calls=%async_computation.4 | async-start | bytes 16384 | tf_op jit(solution)/shard_map/all_to_all | solution.py:451
  79.4 0.0 copy-done
  79.4 2.7 %text_grad.1 = f32[1,32,1024]{2,1,0:T(8,128)} custom-call(bf16[4,32,1152]{2,1,0:T(8,128)(2,1)} %copy-done, bf16[1,32,1024]{2,1,0:T(8,128)(2,1)} %text_hbm.1), custom_call_target="tpu_custom_call" | custom-call | tf_op jit(solution)/shard_map/text_grad/pallas_call | solution.py:454
  82.0 4.3 %all-to-all-done.4 = f32[16,1,128]{2,1,0:T(1,128)S(1)} async-done(((f32[16,1,128]{2,1,0:T(1,128)}), f32[16,1,128]{2,1,0:T(1,128)S(1)}, u32[]{:S(2)}, u32[]{:S(2)}) %all-to-all-start.4) | async-done | bytes 8224 | tf_op jit(solution)/shard_map/all_to_all | solution.py:451
  86.4 0.6 fusion.5
  (7 shorter events, 0.1 us)
Async XLA Ops:
  2.2 16.4 %all-to-all-start.1 = ((bf16[4,32,1024]{2,1,0:T(8,128)(2,1)}), bf16[4,32,1024]{2,1,0:T(8,128)(2,1)S(1)}, u32[]{:S(2)}, u32[]{:S(2)}) async-start(bf16[4,32,1024]{2,1,0:T(8,128)(2,1)} %broadcast_in_dim.15), calls=%async_computation.1 | async-start | bytes 524288 | tf_op jit(solution)/shard_map/all_to_all | solution.py:353
  18.6 13.7 %all-to-all-start = ((bf16[8,32,1152]{2,1,0:T(8,128)(2,1)}), bf16[8,32,1152]{2,1,0:T(8,128)(2,1)S(1)}, u32[]{:S(2)}, u32[]{:S(2)}) async-start(bf16[8,32,1152]{2,1,0:T(8,128)(2,1)} %get-tuple-element.13), calls=%async_computation | async-start | bytes 1179648 | tf_op jit(solution)/shard_map/all_to_all | solution.py:384
  24.3 8.0 %collective-permute-start = (bf16[4,32,1024]{2,1,0:T(8,128)(2,1)S(1)}, bf16[4,32,1024]{2,1,0:T(8,128)(2,1)S(1)}, u32[]{:S(2)}, u32[]{:S(2)}) collective-permute-start(bf16[4,32,1024]{2,1,0:T(8,128)(2,1)S(1)} %all-to-all-done.1), channel_id=1, source_target_pairs={{0,8},{8,0},{1,9},{9,1},{2,10},{10,2},{3,11},{11,3},{4,12},{12,4},... | collective-permute-start | bytes 786440 | tf_op jit(solution)/shard_map/ppermute | solution.py:350
  34.6 12.3 %all-to-all-start.2 = ((bf16[8,32,1152]{2,1,0:T(8,128)(2,1)}), bf16[8,32,1152]{2,1,0:T(8,128)(2,1)S(1)}, u32[]{:S(2)}, u32[]{:S(2)}) async-start(bf16[8,32,1152]{2,1,0:T(8,128)(2,1)} %get-tuple-element.16), calls=%async_computation.2 | async-start | bytes 1179648 | tf_op jit(solution)/shard_map/all_to_all | solution.py:410
  39.5 7.1 %collective-permute-start.1 = (bf16[4,32,1024]{2,1,0:T(8,128)(2,1)S(1)}, bf16[4,32,1024]{2,1,0:T(8,128)(2,1)S(1)}, u32[]{:S(2)}, u32[]{:S(2)}) collective-permute-start(bf16[4,32,1024]{2,1,0:T(8,128)(2,1)S(1)} %get-tuple-element.15), channel_id=1, source_target_pairs={{0,8},{8,0},{1,9},{9,1},{2,10},{10,2},{3,11},{11,3},{4,12},{12,4},... | collective-permute-start | bytes 786440 | tf_op jit(solution)/shard_map/ppermute | solution.py:350
  47.9 15.9 %all-to-all-start.3 = ((bf16[4,32,1152]{2,1,0:T(8,128)(2,1)}), bf16[4,32,1152]{2,1,0:T(8,128)(2,1)S(1)}, u32[]{:S(2)}, u32[]{:S(2)}) async-start(bf16[4,32,1152]{2,1,0:T(8,128)(2,1)} %pad_maximum_fusion), calls=%async_computation.3 | async-start | bytes 589824 | tf_op jit(solution)/shard_map/all_to_all | solution.py:425
  63.8 15.6 %copy-start = (bf16[4,32,1152]{2,1,0:T(8,128)(2,1)}, bf16[4,32,1152]{2,1,0:T(8,128)(2,1)S(1)}, u32[]{:S(2)}) copy-start(bf16[4,32,1152]{2,1,0:T(8,128)(2,1)S(1)} %all-to-all-done.3.parts_ref) | copy-start | bytes 884740
  64.5 21.9 %all-to-all-start.4 = ((f32[16,1,128]{2,1,0:T(1,128)}), f32[16,1,128]{2,1,0:T(1,128)S(1)}, u32[]{:S(2)}, u32[]{:S(2)}) async-start(f32[16,1,128]{2,1,0:T(1,128)} %broadcast_in_dim.17), calls=%async_computation.4 | async-start | bytes 16384 | tf_op jit(solution)/shard_map/all_to_all | solution.py:451
